TPU v7x, 256 devices: a whole 4x4x8 slice. The times are simulated.
256 devices in a mesh: tm: 4 (over y), tile: 64 (over z, x, core).
Axes of the slice: x: 4, y: 4, z: 8, core: 2. Of those that a mesh axis runs over, the one named last changes fastest.
Arguments:
- latent: bfloat16 [8, 128, 128, 512], P('tm', 'tile'), may hold values from -90 to 90
- kernel: bfloat16 [512, 3, 3, 3, 512], P(('tm', 'tile')), may hold values from -0.0546875 to 0.0546875
- norm_gain: float32 [512], replicated, may hold values from 0.5 to 2
- norm_shift: float32 [512], replicated, may hold values from -3 to 3
- conv_bias: float32 [512], replicated, may hold values from -3 to 3
Outputs:
- decoded: bfloat16 [8, 128, 128, 512], P('tm', 'tile')
All inputs are finite; a program needn't handle non-finite values.
Results may differ from a plain program's by a relative error of at most 0.0044.
The roundings to bfloat16 on the way count: a program that leaves them out, or rounds other values in their place, can miss the bound.
Values may be sent and summed in bfloat16 or wider, within the bound.
No kernel may reach another device: no remote copies, remote signals or barrier semaphores. Data moves between devices by JAX's collectives and lax.ppermute only.
A program may use at most 128 MiB of HBM per device.

v0:
```python
import jax
import jax.numpy as jnp
from jax import lax
from jax.sharding import PartitionSpec as P

GROUPS = 32


epsilon = 1e-06


def shifted(array, axis, by):
    devices = lax.axis_size(axis)
    pairs = [(i, i + by) for i in range(devices) if 0 <= i + by < devices]
    return lax.ppermute(array, axis, pairs)


def with_halo(array, sides, width):
    for axis, dim in sides:
        devices, length = (lax.axis_size(axis), array.shape[dim])
        up = [(i, (i + 1) % devices) for i in range(devices - 1)]
        down = [(j, i) for i, j in up]
        last = lax.slice_in_dim(array, length - width, length, axis=dim)
        leading = lax.slice_in_dim(array, 0, width, axis=dim)
        before = lax.ppermute(last, axis, up)
        after = lax.ppermute(leading, axis, down)
        array = jnp.concatenate([before, array, after], axis=dim)
    return array


def activate(span, group_mean, inv_spread, norm_gain, norm_shift):
    channels = span.shape[-1]
    grouped = span.reshape(span.shape[:-1] + (GROUPS, channels // GROUPS)).astype(jnp.float32)
    scaled = ((grouped - group_mean[:, None]) * inv_spread[:, None]).reshape(span.shape)
    return jax.nn.silu(scaled * norm_gain + norm_shift).astype(jnp.bfloat16)


def convolve(bordered, piece):
    frame_count = bordered.shape[0] - 2
    row_count = bordered.shape[1] - 2
    col_count = bordered.shape[2] - 2
    channels = bordered.shape[3]
    summed = jnp.zeros((frame_count * row_count * col_count, piece.shape[0]), jnp.float32)
    for time_tap in range(3):
        for row_tap in range(3):
            for col_tap in range(3):
                sliced = bordered[
                    time_tap : time_tap + frame_count,
                    row_tap : row_tap + row_count,
                    col_tap : col_tap + col_count,
                    :,
                ]
                sliced = sliced.reshape(-1, channels)
                summed = summed + lax.dot_general(
                    sliced,
                    piece[:, time_tap, row_tap, col_tap, :],
                    (((1,), (1,)), ((), ())),
                    preferred_element_type=jnp.float32,
                )
    return summed.reshape(frame_count, row_count, col_count, piece.shape[0])


def per_device(latent, kernel, norm_gain, norm_shift, conv_bias):
    frame_count, row_count, col_count, channels = latent.shape
    group_width = channels // GROUPS
    cell_count = frame_count * row_count * col_count * group_width * lax.axis_size("tile")
    time_index = lax.axis_index("tm")
    grouped = latent.reshape(-1, GROUPS, group_width)
    summed = lax.psum(jnp.sum(grouped.astype(jnp.float32), axis=(0, 2)), "tile")
    group_mean = summed / cell_count
    centered = grouped.astype(jnp.float32) - group_mean[None, :, None]
    spread = lax.psum(jnp.sum(centered * centered, axis=(0, 2)), "tile")
    inv_spread = lax.rsqrt(spread / cell_count + epsilon)
    active = activate(latent, group_mean, inv_spread, norm_gain, norm_shift)
    earlier = shifted(active, "tm", 1)
    opening = jnp.concatenate([active[:1], active[:1]], axis=0)
    earlier = jnp.where(time_index == 0, opening, earlier)
    extended = jnp.concatenate([earlier, active], axis=0)
    bordered = with_halo(extended, (("tile", 1),), 1)
    bordered = jnp.pad(bordered, ((0, 0), (0, 0), (1, 1), (0, 0)))
    kernel_block = lax.all_gather(kernel, "tile", axis=0, tiled=True)
    mixed = convolve(bordered, lax.all_gather(kernel_block, "tm", axis=0, tiled=True))
    return (mixed + conv_bias).astype(jnp.bfloat16)


def solution(mesh):
    return jax.shard_map(
        per_device,
        mesh=mesh,
        in_specs=(
            P("tm", "tile", None, None),
            P(("tm", "tile"), None, None, None, None),
            P(),
            P(),
            P(),
        ),
        out_specs=P("tm", "tile", None, None),
        check_vma=False,
    )
```

profile of v0, /device:TPU:1, one launch (start us, length us, event | category | flops | bytes accessed | tf_op | source)
XLA Modules:
  0.0 435.9 jit_solution(9644086465827529965)
XLA Ops:
  8.1 85.5 %all-gather.3.cloned.1.call-done = bf16[128,3,3,3,512]{4,3,2,1,0:T(4,128)(2,1)} async-done(((bf16[2,3,3,3,512]{4,3,2,1,0:T(4,128)(2,1)}), bf16[128,3,3,3,512]{4,3,2,1,0:T(4,128)(2,1)}) %all-gather.3.cloned.1.call-update) | async-done | bytes 3538960 | tf_op jit(solution)/shard_map/all_gather | solution.py:81
  93.6 5.1 %copy.8 = bf16[128,3,3,3,512]{4,0,3,2,1:T(8,128)(2,1)} copy(bf16[128,3,3,3,512]{4,3,2,1,0:T(4,128)(2,1)} %all-gather.3.cloned.1.call-done) | data formatting | bytes 7077888 | tf_op jit(solution)/shard_map/all_gather | solution.py:81
  100.1 123.7 %psum.14 = f32[32]{0:T(128)S(1)} all-reduce(f32[32]{0:T(128)S(1)} %reduce_sum.25), channel_id=1, replica_groups=mesh['tm'=4,'tile'=64] {'tile'}, use_global_device_ids=true, to_apply=%region_2.0 | all-reduce | flops 32 | bytes 256 | tf_op jit(solution)/shard_map/psum | solution.py:69
  225.3 126.5 %psum.15 = f32[32]{0:T(128)S(1)} all-reduce(f32[32]{0:T(128)S(1)} %reduce_sum.37), channel_id=1, replica_groups=mesh['tm'=4,'tile'=64] {'tile'}, use_global_device_ids=true, to_apply=%region_5.6 | all-reduce | flops 32 | bytes 256 | tf_op jit(solution)/shard_map/psum | solution.py:72
  353.5 3.1 collective-permute-start
  356.6 10.5 %collective-permute-done = bf16[2,2,128,512]{3,2,1,0:T(8,128)(2,1)S(1)} collective-permute-done((bf16[2,2,128,512]{3,2,1,0:T(8,128)(2,1)S(1)}, bf16[2,2,128,512]{3,2,1,0:T(8,128)(2,1)S(1)}, u32[]{:S(2)}, u32[]{:S(2)}) %collective-permute-start) | collective-permute-done | bytes 524320 | tf_op jit(solution)/shard_map/ppermute | solution.py:15
  367.4 1.9 collective-permute-start.1
  369.3 3.0 collective-permute-start.2
  373.1 2.2 collective-permute-done.1
  375.4 4.4 %collective-permute-done.2 = bf16[4,1,128,512]{3,2,1,0:T(8,128)(2,1)S(1)} collective-permute-done((bf16[4,1,128,512]{3,2,1,0:T(8,128)(2,1)S(1)}, bf16[4,1,128,512]{3,2,1,0:T(8,128)(2,1)S(1)}, u32[]{:S(2)}, u32[]{:S(2)}) %collective-permute-start.2) | collective-permute-done | bytes 524320 | tf_op jit(solution)/shard_map/ppermute | solution.py:26
  382.6 3.4 fusion.53
  386.1 1.8 fusion.34
  388.0 2.4 fusion.37
  390.4 2.5 fusion.42
  392.9 1.6 fusion.45
  394.5 1.6 fusion.51
  396.0 1.7 fusion.32
  397.8 1.7 fusion.33
  399.5 1.5 fusion.35
  405.4 1.5 fusion.47
  412.7 1.5 fusion.48
  415.7 1.5 fusion.29
  420.1 5.4 %fusion.14 = f32[512,512]{1,0:T(8,128)S(1)} fusion(f32[512,512]{1,0:T(8,128)} %fusion.31, f32[512,512]{1,0:T(8,128)S(1)} %fusion.32, f32[512,512]{1,0:T(8,128)S(1)} %fusion.33, f32[512,512]{1,0:T(8,128)S(1)} %fusion.34, f32[512,512]{1,0:T(8,128)S(1)} %fusion.35, f32[512,512]{1,0:T(8,128)S(1)} %fusion.36, f32[512,512]{1,0:T(8,128)S(1)} %fusion.37, ...), kind=kOutput, calls=%fused_computation.24 | convolution fusion | flops 274202624 | bytes 25165824 | tf_op jit(solution)/shard_map/dot_general | solution.py:54
  425.5 2.6 fusion.6
  (71 shorter events, 25.4 us)
Async XLA Ops:
  6.5 87.1 %all-gather.3.cloned.1.call-start = ((), (), s32[]{:S(2)}) async-start(), calls=%async_computation | async-start | bytes 4792320 | tf_op jit(solution)/shard_map/all_gather | solution.py:81
  8.0 378.0 %all-gather.5.cloned.1.call-start = ((), (), s32[]{:S(2)}) async-start(), calls=%async_computation.1 | async-start | bytes 17694720 | tf_op jit(solution)/shard_map/all_gather | solution.py:82
  353.5 13.7 %collective-permute-start = (bf16[2,2,128,512]{3,2,1,0:T(8,128)(2,1)S(1)}, bf16[2,2,128,512]{3,2,1,0:T(8,128)(2,1)S(1)}, u32[]{:S(2)}, u32[]{:S(2)}) collective-permute-start(bf16[2,2,128,512]{3,2,1,0:T(8,128)(2,1)S(1)} %fusion.25), channel_id=1, source_target_pairs={{0,64},{64,128},{128,192},{1,65},{65,129},{129,193},{2,66},{66,130... | collective-permute-start | bytes 1572872 | tf_op jit(solution)/shard_map/ppermute | solution.py:15
  367.4 8.0 %collective-permute-start.1 = (bf16[4,1,128,512]{3,2,1,0:T(8,128)(2,1)S(1)}, bf16[4,1,128,512]{3,2,1,0:T(8,128)(2,1)S(1)}, u32[]{:S(2)}, u32[]{:S(2)}) collective-permute-start(bf16[4,1,128,512]{3,2,1,0:T(8,128)(2,1)S(1)} %get-tuple-element.31), channel_id=1, source_target_pairs={{0,1},{1,2},{2,3},{3,4},{4,5},{5,6},{6,7},{7,8},{8,9},{9,10},{10,1... | collective-permute-start | bytes 1572872 | tf_op jit(solution)/shard_map/ppermute | solution.py:25
  369.3 10.5 %collective-permute-start.2 = (bf16[4,1,128,512]{3,2,1,0:T(8,128)(2,1)S(1)}, bf16[4,1,128,512]{3,2,1,0:T(8,128)(2,1)S(1)}, u32[]{:S(2)}, u32[]{:S(2)}) collective-permute-start(bf16[4,1,128,512]{3,2,1,0:T(8,128)(2,1)S(1)} %get-tuple-element.32), channel_id=1, source_target_pairs={{1,0},{2,1},{3,2},{4,3},{5,4},{6,5},{7,6},{8,7},{9,8},{10,9},{11,1... | collective-permute-start | bytes 1572872 | tf_op jit(solution)/shard_map/ppermute | solution.py:26
  386.1 13.4 %copy-start = (bf16[512,3,3,3,512]{4,0,3,2,1:T(8,128)(2,1)S(1)}, bf16[512,3,3,3,512]{4,0,3,2,1:T(8,128)(2,1)}, u32[]{:S(2)}) copy-start(bf16[512,3,3,3,512]{4,0,3,2,1:T(8,128)(2,1)} %all-gather.5.cloned.1.call-done) | copy-start | bytes 42467332
  386.1 14.9 %copy-start.13 = (bf16[2,2,128,512]{3,2,1,0:T(8,128)(2,1)S(1)}, bf16[2,2,128,512]{3,2,1,0:T(8,128)(2,1)}, u32[]{:S(2)}) copy-start(bf16[2,2,128,512]{3,2,1,0:T(8,128)(2,1)} %get-tuple-element.10) | copy-start | bytes 1572868
  386.1 15.4 %copy-start.12 = (bf16[2,2,128,512]{3,2,1,0:T(8,128)(2,1)S(1)}, bf16[2,2,128,512]{3,2,1,0:T(8,128)(2,1)}, u32[]{:S(2)}) copy-start(bf16[2,2,128,512]{3,2,1,0:T(8,128)(2,1)} %get-tuple-element.11) | copy-start | bytes 1572868
  386.1 15.9 %copy-start.11 = (bf16[2,2,128,512]{3,2,1,0:T(8,128)(2,1)S(1)}, bf16[2,2,128,512]{3,2,1,0:T(8,128)(2,1)}, u32[]{:S(2)}) copy-start(bf16[2,2,128,512]{3,2,1,0:T(8,128)(2,1)} %get-tuple-element.13) | copy-start | bytes 1572868
  386.1 17.3 %copy-start.10 = (bf16[2,2,128,512]{3,2,1,0:T(8,128)(2,1)S(1)}, bf16[2,2,128,512]{3,2,1,0:T(8,128)(2,1)}, u32[]{:S(2)}) copy-start(bf16[2,2,128,512]{3,2,1,0:T(8,128)(2,1)} %get-tuple-element.16) | copy-start | bytes 1572868
  387.9 16.0 %copy-start.9 = (bf16[2,2,128,512]{3,2,1,0:T(8,128)(2,1)S(1)}, bf16[2,2,128,512]{3,2,1,0:T(8,128)(2,1)}, u32[]{:S(2)}) copy-start(bf16[2,2,128,512]{3,2,1,0:T(8,128)(2,1)} %get-tuple-element.17) | copy-start | bytes 1572868
  390.4 15.0 %copy-start.8 = (bf16[2,2,128,512]{3,2,1,0:T(8,128)(2,1)S(1)}, bf16[2,2,128,512]{3,2,1,0:T(8,128)(2,1)}, u32[]{:S(2)}) copy-start(bf16[2,2,128,512]{3,2,1,0:T(8,128)(2,1)} %get-tuple-element.18) | copy-start | bytes 1572868
  392.9 14.0 %copy-start.7 = (bf16[2,2,128,512]{3,2,1,0:T(8,128)(2,1)S(1)}, bf16[2,2,128,512]{3,2,1,0:T(8,128)(2,1)}, u32[]{:S(2)}) copy-start(bf16[2,2,128,512]{3,2,1,0:T(8,128)(2,1)} %get-tuple-element.19) | copy-start | bytes 1572868
  394.5 13.9 %copy-start.6 = (bf16[2,2,128,512]{3,2,1,0:T(8,128)(2,1)S(1)}, bf16[2,2,128,512]{3,2,1,0:T(8,128)(2,1)}, u32[]{:S(2)}) copy-start(bf16[2,2,128,512]{3,2,1,0:T(8,128)(2,1)} %get-tuple-element.20) | copy-start | bytes 1572868
  396.0 13.8 %copy-start.5 = (bf16[2,2,128,512]{3,2,1,0:T(8,128)(2,1)S(1)}, bf16[2,2,128,512]{3,2,1,0:T(8,128)(2,1)}, u32[]{:S(2)}) copy-start(bf16[2,2,128,512]{3,2,1,0:T(8,128)(2,1)} %get-tuple-element.21) | copy-start | bytes 1572868
  397.8 13.5 %copy-start.1 = (bf16[2,2,128,512]{3,2,1,0:T(8,128)(2,1)S(1)}, bf16[2,2,128,512]{3,2,1,0:T(8,128)(2,1)}, u32[]{:S(2)}) copy-start(bf16[2,2,128,512]{3,2,1,0:T(8,128)(2,1)} %pad_maximum_fusion.1) | copy-start | bytes 1572868
  401.5 14.2 %copy-start.2 = (bf16[2,2,128,512]{3,2,1,0:T(8,128)(2,1)S(1)}, bf16[2,2,128,512]{3,2,1,0:T(8,128)(2,1)}, u32[]{:S(2)}) copy-start(bf16[2,2,128,512]{3,2,1,0:T(8,128)(2,1)} %get-tuple-element.34) | copy-start | bytes 1572868
  402.0 15.2 %copy-start.4 = (bf16[2,2,128,512]{3,2,1,0:T(8,128)(2,1)S(1)}, bf16[2,2,128,512]{3,2,1,0:T(8,128)(2,1)}, u32[]{:S(2)}) copy-start(bf16[2,2,128,512]{3,2,1,0:T(8,128)(2,1)} %get-tuple-element.22) | copy-start | bytes 1572868
  402.5 16.2 %copy-start.3 = (bf16[2,2,128,512]{3,2,1,0:T(8,128)(2,1)S(1)}, bf16[2,2,128,512]{3,2,1,0:T(8,128)(2,1)}, u32[]{:S(2)}) copy-start(bf16[2,2,128,512]{3,2,1,0:T(8,128)(2,1)} %get-tuple-element.6) | copy-start | bytes 1572868
  420.1 8.0 %copy-start.14 = (f32[512]{0:T(512)S(1)}, f32[512]{0:T(512)}, u32[]{:S(2)}) copy-start(f32[512]{0:T(512)} %param.9) | copy-start | bytes 6148
Sparse Core Ops, SparseCore 0:
  10.1 83.4 all-gather.2
  98.8 131.3 all-gather.4
where the time goes:
time: 441 us; the launch traced here: 436 us
  blocking collectives  250 us (57%)
  waiting for transfers between devices  103 us (23%)
  matrix products  41.7 us (9%)
  between operations  13.7 us (3%)
  local copies, waits for them, and re-layouts  12 us (3%)
  starting transfers between devices  8.11 us (2%)
  other arithmetic  7.38 us (2%)
    psum x1, blocking collectives, per_device(): spread = lax.psum(jnp.sum(centered * centered, axis=(0, 2)), 'tile')  127 us
    psum x1, blocking collectives, per_device(): summed = lax.psum(jnp.sum(grouped.astype(jnp.float32), axis=(0, 2)), 'tile')  124 us
    all_gather x1, waiting for transfers between devices, per_device(): kernel_block = lax.all_gather(kernel, 'tile', axis=0, tiled=True)  85.5 us
    dot_general x27, matrix products, convolve(): lax.dot_general(sliced, piece[:, time_tap, row_tap, col_tap, :], (((1,),...  41.7 us
    ppermute x1, waiting for transfers between devices, shifted(): return lax.ppermute(array, axis, pairs)  10.5 us
  transfers between devices with their start and end apart: 5, of which 4 were waited for; matrix products, arithmetic and copies ran while one was open for 3% of the time, Pallas kernels for 0%

commit v1 on v0

v1 whole, which is shorter than its diff:
```python
import jax
import jax.numpy as jnp
from jax import lax
from jax.experimental import pallas as pl
from jax.experimental.pallas import tpu as pltpu
from jax.sharding import PartitionSpec as P

GROUPS = 32
EPSILON = 1e-06
NY, NZ, NX, NC = 4, 8, 4, 2
DEVICES = NY * NZ * NX * NC
AXES = ("tm", "tile")
FRAMES, ROWS, WIDTH, HALF, OUTS = 8, 4, 128, 256, 128
VMEM = 56 * 2**20


def send(array, move):
    pairs = []
    for y in range(NY):
        for z in range(NZ):
            for x in range(NX):
                for c in range(NC):
                    to = move(y, z, x, c)
                    if to is not None:
                        ty, tz, tx, tc = to
                        source = ((y * NZ + z) * NX + x) * NC + c
                        target = ((ty % NY * NZ + tz % NZ) * NX + tx % NX) * NC + tc % NC
                        pairs.append((source, target))
    return lax.ppermute(array, AXES, pairs)


def along_y(by):
    return lambda y, z, x, c: (y + by, z, x, c)


def along_z(by):
    return lambda y, z, x, c: (y, z + by, x, c)


def along_x(by):
    return lambda y, z, x, c: (y, z, x + by, c)


def sibling(y, z, x, c):
    return (y, z, x, 1 - c)


def strip(by):
    def move(y, z, x, c):
        chip = z * NX + x + by
        return (y, chip // NX, chip % NX, c) if 0 <= chip < NZ * NX else None
    return move


def conv_kernel(info, stat, own, after, across_a, across_b, before, *rest):
    weights, (keep, give, act, taps) = rest[:NZ], rest[NZ:]
    time_index, plane, top, bottom, core = (info[i] for i in range(5))
    column = lax.broadcasted_iota(jnp.int32, (WIDTH, HALF), 0)
    for j in range(NZ):
        taps[:, lax.rem(plane + j, NZ)] = weights[j][...]
    pieces = ((own, 0, 0, 2), (after, 1, 0, 2), (across_a, 2, 0, 1), (across_b, 2, 1, 1), (before, 3, 0, 2))
    for piece, ahead, first, count in pieces:
        span = lax.rem(time_index + ahead, NY)
        mean, gain, shift = (stat[span, i : i + 1] for i in range(3))

        def row(i, _):
            frame, r = i // 6, lax.rem(i, 6)
            v = (piece[frame, r].astype(jnp.float32) - mean) * gain + shift
            s = v / (1.0 + jnp.exp(-v))
            inside = jnp.logical_and(
                jnp.logical_or(r != 0, top == 0), jnp.logical_or(r != 5, bottom == 0)
            )
            s = jnp.where(inside, s, 0.0)
            at = 2 * span + first + frame
            act[1, at, r] = s.astype(jnp.bfloat16)
            act[0, at, r] = jnp.where(column == 0, 0.0, pltpu.roll(s, 1, 0)).astype(jnp.bfloat16)
            act[2, at, r] = jnp.where(column == WIDTH - 1, 0.0, pltpu.roll(s, WIDTH - 1, 0)).astype(jnp.bfloat16)
            return 0

        lax.fori_loop(0, 6 * count, row, 0, unroll=2)

    def products(frame):
        total = None
        for b in range(3):
            for c in range(3):
                lhs = act[c, frame, b : b + ROWS].reshape(ROWS * WIDTH, HALF)
                rhs = jnp.concatenate([taps[(a * 3 + b) * 3 + c].reshape(OUTS, HALF) for a in range(3)], 0)
                term = lax.dot_general(lhs, rhs, (((1,), (1,)), ((), ())), preferred_element_type=jnp.float32)
                total = term if total is None else total + term
        return total[:, :OUTS], total[:, OUTS : 2 * OUTS], total[:, 2 * OUTS :]

    def emit(frame, value):
        value = value.reshape(ROWS, WIDTH, OUTS)

        @pl.when(core == 0)
        def _():
            keep[frame] = value[:2]
            give[frame] = value[2:]

        @pl.when(core == 1)
        def _():
            keep[frame] = value[2:]
            give[frame] = value[:2]

    first, second, third = products(0)
    emit(0, first + second + third)

    def step(frame, carry):
        ready, started = carry
        first, second, third = products(frame)
        emit(frame, ready + third)
        return started + second, first

    lax.fori_loop(1, FRAMES, step, (first + second, first))


def convolve(info, stat, pieces, weights):
    vmem = pl.BlockSpec(memory_space=pltpu.VMEM)
    shape = jax.ShapeDtypeStruct((FRAMES, 2, WIDTH, OUTS), jnp.float32)
    return pl.pallas_call(
        conv_kernel,
        out_shape=[shape, shape],
        in_specs=[pl.BlockSpec(memory_space=pltpu.SMEM)] + [vmem] * (1 + len(pieces) + len(weights)),
        out_specs=[vmem, vmem],
        scratch_shapes=[
            pltpu.VMEM((3, FRAMES, ROWS + 2, WIDTH, HALF), jnp.bfloat16),
            pltpu.VMEM((27, NZ, 16, HALF), jnp.bfloat16),
        ],
        compiler_params=pltpu.CompilerParams(vmem_limit_bytes=VMEM),
        cost_estimate=pl.CostEstimate(flops=2 * 4096 * 256 * 27 * 128, bytes_accessed=8 * 2**20, transcendentals=0),
    )(info, stat, *pieces, *weights)


def per_device(latent, kernel, norm_gain, norm_shift, conv_bias):
    time_index = lax.axis_index("tm")
    tile = lax.axis_index("tile")
    plane, core, chip = tile // (NX * NC), tile % NC, tile // NC
    channels = latent.shape[3]
    group_width = channels // GROUPS

    half = lambda a, which: lax.dynamic_slice_in_dim(a, which * HALF, HALF, axis=a.ndim - 1)
    theirs = send(half(latent, 1 - core), sibling)
    mine = half(latent, core)
    rows = jnp.zeros((2, ROWS, WIDTH, HALF), jnp.bfloat16)
    rows = lax.dynamic_update_slice(rows, mine, (0, 2 * core, 0, 0))
    rows = lax.dynamic_update_slice(rows, theirs, (0, 2 - 2 * core, 0, 0))
    above = send(rows[:, ROWS - 1 :], strip(1))
    below = send(rows[:, :1], strip(-1))
    own = jnp.concatenate([above, rows, below], axis=1)
    after = send(own, along_y(-1))
    before = send(own, along_y(1))
    across_a = send(after[:1], along_y(-1))
    across_b = send(before[1:], along_y(1))

    shard = kernel.reshape(2, 27, channels)
    other = send(half(shard, 1 - core), sibling)
    near = half(shard, core)
    pair = jnp.where(core == 0, jnp.stack([near, other]), jnp.stack([other, near]))
    pair = pair.reshape(4, 27, HALF)
    x_index = (tile // NC) % NX
    block = jnp.zeros((NX, 4, 27, HALF), jnp.bfloat16)
    for by in range(NX):
        got = pair if by == 0 else send(pair, along_x(-by))
        block = lax.dynamic_update_slice(block, got[None], ((x_index + by) % NX, 0, 0, 0))
    block = block.reshape(16, 27, HALF).transpose(1, 0, 2)
    ring = [block] + [None] * (NZ - 1)
    for by in range(1, 4):
        ring[by] = send(ring[by - 1], along_z(-1))
        ring[-by] = send(ring[(1 - by) % NZ], along_z(1))
    ring[4] = jnp.concatenate(
        [send(ring[3][:14], along_z(-1)), send(ring[5][14:], along_z(1))], axis=0
    )

    grouped = latent.astype(jnp.float32)
    cells = 2 * 2 * WIDTH * group_width
    local_sum = jnp.sum(jnp.sum(grouped, axis=(0, 1, 2)).reshape(GROUPS, group_width), axis=1)
    local_mean = local_sum / cells
    centered = grouped - jnp.repeat(local_mean, group_width)
    local_squares = jnp.sum(jnp.sum(centered * centered, axis=(0, 1, 2)).reshape(GROUPS, group_width), axis=1)
    local = jnp.concatenate([local_mean, local_squares, jnp.zeros((64,), jnp.float32)])[None]
    everyone = jnp.broadcast_to(local[None], (DEVICES, 1, 128))
    everyone = lax.all_to_all(everyone, AXES, 0, 0).reshape(NY, DEVICES // NY, 128)
    means, squares = everyone[..., :GROUPS], everyone[..., GROUPS : 2 * GROUPS]
    group_mean = jnp.mean(means, axis=1)
    deviation = means - group_mean[:, None]
    variance = (jnp.sum(squares, axis=1) / cells + jnp.sum(deviation * deviation, axis=1)) / (DEVICES // NY)
    inv_spread = lax.rsqrt(variance + EPSILON)
    stat = jnp.stack(
        [
            jnp.repeat(group_mean, group_width, axis=1),
            jnp.repeat(inv_spread, group_width, axis=1) * norm_gain,
            jnp.broadcast_to(norm_shift, (NY, channels)),
        ],
        axis=1,
    )
    stat = half(stat, core)
    info = jnp.stack([time_index, plane, chip == 0, chip == NZ * NX - 1, core]).astype(jnp.int32)

    keep, give = convolve(info, stat, [own, after, across_a, across_b, before], ring)
    bias = lax.dynamic_slice_in_dim(conv_bias, time_index * OUTS, OUTS)
    mixed = (keep + send(give, sibling) + bias).astype(jnp.bfloat16)
    mixed = lax.all_to_all(mixed.reshape(NY, 2, 2, WIDTH, OUTS), "tm", 0, 0)
    return mixed.transpose(1, 2, 3, 0, 4).reshape(2, 2, WIDTH, channels)


def solution(mesh):
    return jax.shard_map(
        per_device,
        mesh=mesh,
        in_specs=(
            P("tm", "tile", None, None),
            P(("tm", "tile"), None, None, None, None),
            P(),
            P(),
            P(),
        ),
        out_specs=P("tm", "tile", None, None),
        check_vma=False,
    )
```

time: 441 us -> 117 us (0.27)
  the two profiles are of different devices: /device:TPU:1 before, /device:TPU:6 now
where the time goes in v1:
time: 117 us
  starting transfers between devices  44.8 us (38%)
  waiting for transfers between devices  26.8 us (23%)
  Pallas kernels  19.9 us (17%)
  blocking collectives  12.9 us (11%)
  local copies, waits for them, and re-layouts  7.4 us (6%)
  other arithmetic  4.76 us (4%)
    ppermute x20, starting transfers between devices, send(): return lax.ppermute(array, AXES, pairs)  30.1 us
    ppermute x20, waiting for transfers between devices, send(): return lax.ppermute(array, AXES, pairs)  26.8 us
    pallas_call x1, Pallas kernels, convolve(): pl.pallas_call(conv_kernel, out_shape=[shape, shape], in_specs=[pl.BlockS...  19.9 us
    all_to_all x1, starting transfers between devices, per_device(): lax.all_to_all(everyone, AXES, 0, 0).reshape(NY, DEVICES // NY, 128)  14.7 us
    all_to_all x1, blocking collectives, per_device(): mixed = lax.all_to_all(mixed.reshape(NY, 2, 2, WIDTH, OUTS), 'tm', 0, 0)  12.9 us
  transfers between devices with their start and end apart: 21, of which 7 were waited for; matrix products, arithmetic and copies ran while one was open for 7% of the time, Pallas kernels for 0%

profile of v1, /device:TPU:6, one launch (start us, length us, event | category | flops | bytes accessed | tf_op | source)
XLA Modules:
  0.0 116.9 jit_solution(7620267355916379982)
XLA Ops:
  1.0 1.2 convert_reduce_fusion
  3.7 14.7 %all-to-all-start = ((f32[256,1,128]{2,1,0:T(1,128)}), f32[256,1,128]{2,1,0:T(1,128)S(1)}, u32[]{:S(2)}, u32[]{:S(2)}) async-start(f32[256,1,128]{2,1,0:T(1,128)} %broadcast_in_dim.37), calls=%async_computation | async-start | bytes 262144 | tf_op jit(solution)/shard_map/all_to_all | solution.py:182
  19.0 2.2 %collective-permute-start.10 = (bf16[4,27,256]{2,0,1:T(4,128)(2,1)S(1)}, bf16[4,27,256]{2,0,1:T(4,128)(2,1)S(1)}, u32[]{:S(2)}, u32[]{:S(2)}) collective-permute-start(bf16[4,27,256]{2,0,1:T(4,128)(2,1)S(1)} %select_n.100), channel_id=1, source_target_pairs={{0,2},{1,3},{2,4},{3,5},{4,6},{5,7},{6,0},{7,1},{8,10},{9,11},{10,... | collective-permute-start | bytes 165896 | tf_op jit(solution)/shard_map/ppermute | solution.py:29
  22.3 5.7 %collective-permute-done.8 = bf16[4,27,256]{2,0,1:T(4,128)(2,1)S(1)} collective-permute-done((bf16[4,27,256]{2,0,1:T(4,128)(2,1)S(1)}, bf16[4,27,256]{2,0,1:T(4,128)(2,1)S(1)}, u32[]{:S(2)}, u32[]{:S(2)}) %collective-permute-start.8) | collective-permute-done | bytes 55328 | tf_op jit(solution)/shard_map/ppermute | solution.py:29
  28.2 3.0 %collective-permute-start.1 = (bf16[2,1,128,256]{3,2,1,0:T(8,128)(2,1)S(1)}, bf16[2,1,128,256]{3,2,1,0:T(8,128)(2,1)S(1)}, u32[]{:S(2)}, u32[]{:S(2)}) collective-permute-start(bf16[2,1,128,256]{3,2,1,0:T(8,128)(2,1)S(1)} %get-tuple-element.11), channel_id=1, source_target_pairs={{0,2},{1,3},{2,4},{3,5},{4,6},{5,7},{6,8},{7,9},{8,10},{9,11},{10,... | collective-permute-start | bytes 393224 | tf_op jit(solution)/shard_map/ppermute | solution.py:29
  31.1 2.9 %collective-permute-start.2 = (bf16[2,1,128,256]{3,2,1,0:T(8,128)(2,1)S(1)}, bf16[2,1,128,256]{3,2,1,0:T(8,128)(2,1)S(1)}, u32[]{:S(2)}, u32[]{:S(2)}) collective-permute-start(bf16[2,1,128,256]{3,2,1,0:T(8,128)(2,1)S(1)} %get-tuple-element.12), channel_id=1, source_target_pairs={{2,0},{3,1},{4,2},{5,3},{6,4},{7,5},{8,6},{9,7},{10,8},{11,9},{12,... | collective-permute-start | bytes 393224 | tf_op jit(solution)/shard_map/ppermute | solution.py:29
  34.2 3.9 %collective-permute-start.11 = (bf16[27,16,256]{2,1,0:T(8,128)(2,1)S(1)}, bf16[27,16,256]{2,1,0:T(8,128)(2,1)S(1)}, u32[]{:S(2)}, u32[]{:S(2)}) collective-permute-start(bf16[27,16,256]{2,1,0:T(8,128)(2,1)S(1)} %bitcast.37), channel_id=1, source_target_pairs={{0,56},{1,57},{2,58},{3,59},{4,60},{5,61},{6,62},{7,63},{8,0},{9,1... | collective-permute-start | bytes 663560 | tf_op jit(solution)/shard_map/ppermute | solution.py:29
  38.0 3.5 %collective-permute-done.2 = bf16[2,1,128,256]{3,2,1,0:T(8,128)(2,1)S(1)} collective-permute-done((bf16[2,1,128,256]{3,2,1,0:T(8,128)(2,1)S(1)}, bf16[2,1,128,256]{3,2,1,0:T(8,128)(2,1)S(1)}, u32[]{:S(2)}, u32[]{:S(2)}) %collective-permute-start.2) | collective-permute-done | bytes 131104 | tf_op jit(solution)/shard_map/ppermute | solution.py:29
  41.7 1.6 %collective-permute-start.5 = (bf16[2,6,128,256]{3,2,1,0:T(8,128)(2,1)S(1)}, bf16[2,6,128,256]{3,2,1,0:T(8,128)(2,1)S(1)}, u32[]{:S(2)}, u32[]{:S(2)}) collective-permute-start(bf16[2,6,128,256]{3,2,1,0:T(8,128)(2,1)S(1)} %pad_maximum_fusion.own), channel_id=1, source_target_pairs={{0,64},{1,65},{2,66},{3,67},{4,68},{5,69},{6,70},{7,71},{8,72},{9,... | collective-permute-start | bytes 2359304 | tf_op jit(solution)/shard_map/ppermute | solution.py:29
  43.3 1.7 %collective-permute-start.3 = (bf16[2,6,128,256]{3,2,1,0:T(8,128)(2,1)S(1)}, bf16[2,6,128,256]{3,2,1,0:T(8,128)(2,1)}, u32[]{:S(2)}, u32[]{:S(2)}) collective-permute-start(bf16[2,6,128,256]{3,2,1,0:T(8,128)(2,1)S(1)} %pad_maximum_fusion.own), channel_id=1, source_target_pairs={{0,192},{1,193},{2,194},{3,195},{4,196},{5,197},{6,198},{7,199},{8... | collective-permute-start | bytes 2359304 | tf_op jit(solution)/shard_map/ppermute | solution.py:29
  45.6 1.7 %collective-permute-start.15 = (bf16[27,16,256]{2,1,0:T(8,128)(2,1)S(1)}, bf16[27,16,256]{2,1,0:T(8,128)(2,1)S(1)}, u32[]{:S(2)}, u32[]{:S(2)}) collective-permute-start(bf16[27,16,256]{2,1,0:T(8,128)(2,1)S(1)} %bitcast.38), channel_id=1, source_target_pairs={{0,8},{1,9},{2,10},{3,11},{4,12},{5,13},{6,14},{7,15},{8,16},{9,17... | collective-permute-start | bytes 663560 | tf_op jit(solution)/shard_map/ppermute | solution.py:29
  47.4 1.6 %collective-permute-start.12 = (bf16[27,16,256]{2,1,0:T(8,128)(2,1)S(1)}, bf16[27,16,256]{2,1,0:T(8,128)(2,1)S(1)}, u32[]{:S(2)}, u32[]{:S(2)}) collective-permute-start(bf16[27,16,256]{2,1,0:T(8,128)(2,1)S(1)} %collective-permute-done.11.rest_1_), channel_id=1, source_target_pairs={{0,56},{1,57},{2,58},{3,59},{4,60},{5,61},{6,62},{7,63},{8,0},{9,1... | collective-permute-start | bytes 663560 | tf_op jit(solution)/shard_map/ppermute | solution.py:29
  49.1 5.0 %collective-permute-done.15.rest_7_ = bf16[27,16,256]{2,1,0:T(8,128)(2,1)S(1)} collective-permute-done((bf16[27,16,256]{2,1,0:T(8,128)(2,1)S(1)}, bf16[27,16,256]{2,1,0:T(8,128)(2,1)S(1)}, u32[]{:S(2)}, u32[]{:S(2)}) %collective-permute-start.15) | collective-permute-done | bytes 221216 | tf_op jit(solution)/shard_map/ppermute | solution.py:29
  54.1 1.2 %collective-permute-start.16 = (bf16[27,16,256]{2,1,0:T(8,128)(2,1)S(1)}, bf16[27,16,256]{2,1,0:T(8,128)(2,1)}, u32[]{:S(2)}, u32[]{:S(2)}) collective-permute-start(bf16[27,16,256]{2,1,0:T(8,128)(2,1)S(1)} %collective-permute-done.15.rest_7_), channel_id=1, source_target_pairs={{0,8},{1,9},{2,10},{3,11},{4,12},{5,13},{6,14},{7,15},{8,16},{9,17... | collective-permute-start | bytes 663560 | tf_op jit(solution)/shard_map/ppermute | solution.py:29
  55.3 2.5 %collective-permute-start.13 = (bf16[27,16,256]{2,1,0:T(8,128)(2,1)S(1)}, bf16[27,16,256]{2,1,0:T(8,128)(2,1)S(1)}, u32[]{:S(2)}, u32[]{:S(2)}) collective-permute-start(bf16[27,16,256]{2,1,0:T(8,128)(2,1)S(1)} %collective-permute-done.12.rest_2_), channel_id=1, source_target_pairs={{0,56},{1,57},{2,58},{3,59},{4,60},{5,61},{6,62},{7,63},{8,0},{9,1... | collective-permute-start | bytes 663560 | tf_op jit(solution)/shard_map/ppermute | solution.py:29
  58.0 5.5 %collective-permute-done.16.rest_6_ = bf16[27,16,256]{2,1,0:T(8,128)(2,1)} collective-permute-done((bf16[27,16,256]{2,1,0:T(8,128)(2,1)S(1)}, bf16[27,16,256]{2,1,0:T(8,128)(2,1)}, u32[]{:S(2)}, u32[]{:S(2)}) %collective-permute-start.16) | collective-permute-done | bytes 221216 | tf_op jit(solution)/shard_map/ppermute | solution.py:29
  63.8 3.0 %collective-permute-start.14 = (bf16[14,16,256]{2,1,0:T(8,128)(2,1)S(1)}, bf16[14,16,256]{2,1,0:T(8,128)(2,1)S(1)}, u32[]{:S(2)}, u32[]{:S(2)}) collective-permute-start(bf16[14,16,256]{2,1,0:T(8,128)(2,1)S(1)} %slice.38), channel_id=1, source_target_pairs={{0,56},{1,57},{2,58},{3,59},{4,60},{5,61},{6,62},{7,63},{8,0},{9,1... | collective-permute-start | bytes 344072 | tf_op jit(solution)/shard_map/ppermute | solution.py:29
  67.7 1.0 slice.36
  68.8 2.6 %collective-permute-start.4 = (bf16[1,6,128,256]{3,2,1,0:T(8,128)(2,1)S(1)}, bf16[1,6,128,256]{3,2,1,0:T(8,128)(2,1)S(1)}, u32[]{:S(2)}, u32[]{:S(2)}) collective-permute-start(bf16[1,6,128,256]{3,2,1,0:T(8,128)(2,1)S(1)} %slice.36), channel_id=1, source_target_pairs={{0,192},{1,193},{2,194},{3,195},{4,196},{5,197},{6,198},{7,199},{8... | collective-permute-start | bytes 1179656 | tf_op jit(solution)/shard_map/ppermute | solution.py:29
  72.9 4.7 %collective-permute-done.18 = bf16[13,16,256]{2,1,0:T(8,128)(2,1)S(1)} collective-permute-done((bf16[13,16,256]{2,1,0:T(8,128)(2,1)S(1)}, bf16[13,16,256]{2,1,0:T(8,128)(2,1)S(1)}, u32[]{:S(2)}, u32[]{:S(2)}) %collective-permute-start.18) | collective-permute-done | bytes 106528 | tf_op jit(solution)/shard_map/ppermute | solution.py:29
  79.1 19.9 %shard_map.55 = (f32[8,2,128,128]{3,2,1,0:T(8,128)}, f32[8,2,128,128]{3,2,1,0:T(8,128)}) custom-call(s32[5]{0:T(128)} %stack.49.info, f32[4,3,256]{2,1,0:T(4,128)} %fusion.3.stat, bf16[2,6,128,256]{3,2,1,0:T(8,128)(2,1)} %copy-done.1, bf16[2,6,128,256]{3,2,1,0:T(8,128)(2,1)} %collective-permute-done.3.after, bf16[1,6,128,256]{3,2,1,0:T(8,128)(2,1)} %copy-done.8, ...), custom_call_target="tpu_custom_call" | custom-call | flops 7247757312 | bytes 8388608 | tf_op jit(solution)/shard_map/pallas_call | solution.py:120
  99.7 2.1 %collective-permute-done.19 = f32[8,2,128,128]{3,2,1,0:T(8,128)S(1)} collective-permute-done((f32[8,2,128,128]{3,2,1,0:T(8,128)}, f32[8,2,128,128]{3,2,1,0:T(8,128)S(1)}, u32[]{:S(2)}, u32[]{:S(2)}) %collective-permute-start.19) | collective-permute-done | bytes 1048608 | tf_op jit(solution)/shard_map/ppermute | solution.py:29
  101.8 1.4 %add_convert_fusion = bf16[8,2,128,128]{3,2,1,0:T(8,128)(2,1)S(1)} fusion(f32[8,2,128,128]{3,2,1,0:T(8,128)} %get-tuple-element.7, f32[8,2,128,128]{3,2,1,0:T(8,128)S(1)} %collective-permute-done.19, f32[128]{0:T(128)S(1)} %dynamic_slice.23), kind=kLoop, calls=%fused_computation.4 | loop fusion | flops 786432 | bytes 2621952 | tf_op jit(solution)/shard_map/convert_element_type | solution.py:201
  103.2 12.9 %all_to_all.10 = bf16[4,2,2,128,128]{4,3,2,1,0:T(8,128)(2,1)S(1)} all-to-all(bf16[4,2,2,128,128]{4,3,2,1,0:T(8,128)(2,1)S(1)} %bitcast.36), channel_id=1, replica_groups=mesh['tm'=4,'tile'=64] {'tm'}, dimensions={0} | all-to-all | bytes 1048576 | tf_op jit(solution)/shard_map/all_to_all | solution.py:202
  (92 shorter events, 11.1 us)
Async XLA Ops:
  0.9 17.9 %collective-permute-start.7 = (bf16[2,27,256]{2,0,1:T(2,128)(2,1)S(1)}, bf16[2,27,256]{2,0,1:T(2,128)(2,1)S(1)}, u32[]{:S(2)}, u32[]{:S(2)}) collective-permute-start(bf16[2,27,256]{2,0,1:T(2,128)(2,1)S(1)} %get-tuple-element.16), channel_id=1, source_target_pairs={{0,1},{1,0},{2,3},{3,2},{4,5},{5,4},{6,7},{7,6},{8,9},{9,8},{10,11... | collective-permute-start | bytes 82952 | tf_op jit(solution)/shard_map/ppermute | solution.py:29
  3.7 43.6 %all-to-all-start = ((f32[256,1,128]{2,1,0:T(1,128)}), f32[256,1,128]{2,1,0:T(1,128)S(1)}, u32[]{:S(2)}, u32[]{:S(2)}) async-start(f32[256,1,128]{2,1,0:T(1,128)} %broadcast_in_dim.37), calls=%async_computation | async-start | bytes 262144 | tf_op jit(solution)/shard_map/all_to_all | solution.py:182
  18.5 9.6 %collective-permute-start = (bf16[2,2,128,256]{3,2,1,0:T(8,128)(2,1)S(1)}, bf16[2,2,128,256]{3,2,1,0:T(8,128)(2,1)S(1)}, u32[]{:S(2)}, u32[]{:S(2)}) collective-permute-start(bf16[2,2,128,256]{3,2,1,0:T(8,128)(2,1)S(1)} %get-tuple-element.13), channel_id=1, source_target_pairs={{0,1},{1,0},{2,3},{3,2},{4,5},{5,4},{6,7},{7,6},{8,9},{9,8},{10,11... | collective-permute-start | bytes 786440 | tf_op jit(solution)/shard_map/ppermute | solution.py:29
  19.0 15.0 %collective-permute-start.10 = (bf16[4,27,256]{2,0,1:T(4,128)(2,1)S(1)}, bf16[4,27,256]{2,0,1:T(4,128)(2,1)S(1)}, u32[]{:S(2)}, u32[]{:S(2)}) collective-permute-start(bf16[4,27,256]{2,0,1:T(4,128)(2,1)S(1)} %select_n.100), channel_id=1, source_target_pairs={{0,2},{1,3},{2,4},{3,5},{4,6},{5,7},{6,0},{7,1},{8,10},{9,11},{10,... | collective-permute-start | bytes 165896 | tf_op jit(solution)/shard_map/ppermute | solution.py:29
  21.2 6.8 %collective-permute-start.9 = (bf16[4,27,256]{2,0,1:T(4,128)(2,1)S(1)}, bf16[4,27,256]{2,0,1:T(4,128)(2,1)S(1)}, u32[]{:S(2)}, u32[]{:S(2)}) collective-permute-start(bf16[4,27,256]{2,0,1:T(4,128)(2,1)S(1)} %select_n.100), channel_id=1, source_target_pairs={{0,4},{1,5},{2,6},{3,7},{4,0},{5,1},{6,2},{7,3},{8,12},{9,13},{10,... | collective-permute-start | bytes 165896 | tf_op jit(solution)/shard_map/ppermute | solution.py:29
  22.0 6.0 %collective-permute-start.8 = (bf16[4,27,256]{2,0,1:T(4,128)(2,1)S(1)}, bf16[4,27,256]{2,0,1:T(4,128)(2,1)S(1)}, u32[]{:S(2)}, u32[]{:S(2)}) collective-permute-start(bf16[4,27,256]{2,0,1:T(4,128)(2,1)S(1)} %select_n.100), channel_id=1, source_target_pairs={{0,6},{1,7},{2,0},{3,1},{4,2},{5,3},{6,4},{7,5},{8,14},{9,15},{10,... | collective-permute-start | bytes 165896 | tf_op jit(solution)/shard_map/ppermute | solution.py:29
  28.2 9.9 %collective-permute-start.1 = (bf16[2,1,128,256]{3,2,1,0:T(8,128)(2,1)S(1)}, bf16[2,1,128,256]{3,2,1,0:T(8,128)(2,1)S(1)}, u32[]{:S(2)}, u32[]{:S(2)}) collective-permute-start(bf16[2,1,128,256]{3,2,1,0:T(8,128)(2,1)S(1)} %get-tuple-element.11), channel_id=1, source_target_pairs={{0,2},{1,3},{2,4},{3,5},{4,6},{5,7},{6,8},{7,9},{8,10},{9,11},{10,... | collective-permute-start | bytes 393224 | tf_op jit(solution)/shard_map/ppermute | solution.py:29
  31.1 10.4 %collective-permute-start.2 = (bf16[2,1,128,256]{3,2,1,0:T(8,128)(2,1)S(1)}, bf16[2,1,128,256]{3,2,1,0:T(8,128)(2,1)S(1)}, u32[]{:S(2)}, u32[]{:S(2)}) collective-permute-start(bf16[2,1,128,256]{3,2,1,0:T(8,128)(2,1)S(1)} %get-tuple-element.12), channel_id=1, source_target_pairs={{2,0},{3,1},{4,2},{5,3},{6,4},{7,5},{8,6},{9,7},{10,8},{11,9},{12,... | collective-permute-start | bytes 393224 | tf_op jit(solution)/shard_map/ppermute | solution.py:29
  34.2 13.2 %collective-permute-start.11 = (bf16[27,16,256]{2,1,0:T(8,128)(2,1)S(1)}, bf16[27,16,256]{2,1,0:T(8,128)(2,1)S(1)}, u32[]{:S(2)}, u32[]{:S(2)}) collective-permute-start(bf16[27,16,256]{2,1,0:T(8,128)(2,1)S(1)} %bitcast.37), channel_id=1, source_target_pairs={{0,56},{1,57},{2,58},{3,59},{4,60},{5,61},{6,62},{7,63},{8,0},{9,1... | collective-permute-start | bytes 663560 | tf_op jit(solution)/shard_map/ppermute | solution.py:29
  41.7 25.2 %copy-start.1 = (bf16[2,6,128,256]{3,2,1,0:T(8,128)(2,1)}, bf16[2,6,128,256]{3,2,1,0:T(8,128)(2,1)S(1)}, u32[]{:S(2)}) copy-start(bf16[2,6,128,256]{3,2,1,0:T(8,128)(2,1)S(1)} %pad_maximum_fusion.own) | copy-start | bytes 2359300
  41.7 25.2 %collective-permute-start.5 = (bf16[2,6,128,256]{3,2,1,0:T(8,128)(2,1)S(1)}, bf16[2,6,128,256]{3,2,1,0:T(8,128)(2,1)S(1)}, u32[]{:S(2)}, u32[]{:S(2)}) collective-permute-start(bf16[2,6,128,256]{3,2,1,0:T(8,128)(2,1)S(1)} %pad_maximum_fusion.own), channel_id=1, source_target_pairs={{0,64},{1,65},{2,66},{3,67},{4,68},{5,69},{6,70},{7,71},{8,72},{9,... | collective-permute-start | bytes 2359304 | tf_op jit(solution)/shard_map/ppermute | solution.py:29
  43.3 24.4 %collective-permute-start.3 = (bf16[2,6,128,256]{3,2,1,0:T(8,128)(2,1)S(1)}, bf16[2,6,128,256]{3,2,1,0:T(8,128)(2,1)}, u32[]{:S(2)}, u32[]{:S(2)}) collective-permute-start(bf16[2,6,128,256]{3,2,1,0:T(8,128)(2,1)S(1)} %pad_maximum_fusion.own), channel_id=1, source_target_pairs={{0,192},{1,193},{2,194},{3,195},{4,196},{5,197},{6,198},{7,199},{8... | collective-permute-start | bytes 2359304 | tf_op jit(solution)/shard_map/ppermute | solution.py:29
  45.6 8.5 %collective-permute-start.15 = (bf16[27,16,256]{2,1,0:T(8,128)(2,1)S(1)}, bf16[27,16,256]{2,1,0:T(8,128)(2,1)S(1)}, u32[]{:S(2)}, u32[]{:S(2)}) collective-permute-start(bf16[27,16,256]{2,1,0:T(8,128)(2,1)S(1)} %bitcast.38), channel_id=1, source_target_pairs={{0,8},{1,9},{2,10},{3,11},{4,12},{5,13},{6,14},{7,15},{8,16},{9,17... | collective-permute-start | bytes 663560 | tf_op jit(solution)/shard_map/ppermute | solution.py:29
  47.4 8.0 %collective-permute-start.12 = (bf16[27,16,256]{2,1,0:T(8,128)(2,1)S(1)}, bf16[27,16,256]{2,1,0:T(8,128)(2,1)S(1)}, u32[]{:S(2)}, u32[]{:S(2)}) collective-permute-start(bf16[27,16,256]{2,1,0:T(8,128)(2,1)S(1)} %collective-permute-done.11.rest_1_), channel_id=1, source_target_pairs={{0,56},{1,57},{2,58},{3,59},{4,60},{5,61},{6,62},{7,63},{8,0},{9,1... | collective-permute-start | bytes 663560 | tf_op jit(solution)/shard_map/ppermute | solution.py:29
  54.1 12.7 %copy-start.10 = (bf16[27,16,256]{2,1,0:T(8,128)(2,1)}, bf16[27,16,256]{2,1,0:T(8,128)(2,1)S(1)}, u32[]{:S(2)}) copy-start(bf16[27,16,256]{2,1,0:T(8,128)(2,1)S(1)} %collective-permute-done.15.rest_7_) | copy-start | bytes 663556
  54.1 9.4 %collective-permute-start.16 = (bf16[27,16,256]{2,1,0:T(8,128)(2,1)S(1)}, bf16[27,16,256]{2,1,0:T(8,128)(2,1)}, u32[]{:S(2)}, u32[]{:S(2)}) collective-permute-start(bf16[27,16,256]{2,1,0:T(8,128)(2,1)S(1)} %collective-permute-done.15.rest_7_), channel_id=1, source_target_pairs={{0,8},{1,9},{2,10},{3,11},{4,12},{5,13},{6,14},{7,15},{8,16},{9,17... | collective-permute-start | bytes 663560 | tf_op jit(solution)/shard_map/ppermute | solution.py:29
  55.3 11.6 %copy-start.11 = (bf16[27,16,256]{2,1,0:T(8,128)(2,1)}, bf16[27,16,256]{2,1,0:T(8,128)(2,1)S(1)}, u32[]{:S(2)}) copy-start(bf16[27,16,256]{2,1,0:T(8,128)(2,1)S(1)} %collective-permute-done.12.rest_2_) | copy-start | bytes 663556
  55.3 8.4 %collective-permute-start.13 = (bf16[27,16,256]{2,1,0:T(8,128)(2,1)S(1)}, bf16[27,16,256]{2,1,0:T(8,128)(2,1)S(1)}, u32[]{:S(2)}, u32[]{:S(2)}) collective-permute-start(bf16[27,16,256]{2,1,0:T(8,128)(2,1)S(1)} %collective-permute-done.12.rest_2_), channel_id=1, source_target_pairs={{0,56},{1,57},{2,58},{3,59},{4,60},{5,61},{6,62},{7,63},{8,0},{9,1... | collective-permute-start | bytes 663560 | tf_op jit(solution)/shard_map/ppermute | solution.py:29
  63.5 8.1 %collective-permute-start.17 = (bf16[27,16,256]{2,1,0:T(8,128)(2,1)}, bf16[27,16,256]{2,1,0:T(8,128)(2,1)S(1)}, u32[]{:S(2)}, u32[]{:S(2)}) collective-permute-start(bf16[27,16,256]{2,1,0:T(8,128)(2,1)} %collective-permute-done.16.rest_6_), channel_id=1, source_target_pairs={{0,8},{1,9},{2,10},{3,11},{4,12},{5,13},{6,14},{7,15},{8,16},{9,17... | collective-permute-start | bytes 663560 | tf_op jit(solution)/shard_map/ppermute | solution.py:29
  63.8 13.8 %collective-permute-start.14 = (bf16[14,16,256]{2,1,0:T(8,128)(2,1)S(1)}, bf16[14,16,256]{2,1,0:T(8,128)(2,1)S(1)}, u32[]{:S(2)}, u32[]{:S(2)}) collective-permute-start(bf16[14,16,256]{2,1,0:T(8,128)(2,1)S(1)} %slice.38), channel_id=1, source_target_pairs={{0,56},{1,57},{2,58},{3,59},{4,60},{5,61},{6,62},{7,63},{8,0},{9,1... | collective-permute-start | bytes 344072 | tf_op jit(solution)/shard_map/ppermute | solution.py:29
  66.9 11.4 %collective-permute-start.6 = (bf16[1,6,128,256]{3,2,1,0:T(8,128)(2,1)S(1)}, bf16[1,6,128,256]{3,2,1,0:T(8,128)(2,1)}, u32[]{:S(2)}, u32[]{:S(2)}) collective-permute-start(bf16[1,6,128,256]{3,2,1,0:T(8,128)(2,1)S(1)} %slice.37), channel_id=1, source_target_pairs={{0,64},{1,65},{2,66},{3,67},{4,68},{5,69},{6,70},{7,71},{8,72},{9,... | collective-permute-start | bytes 1179656 | tf_op jit(solution)/shard_map/ppermute | solution.py:29
  68.8 9.5 %collective-permute-start.4 = (bf16[1,6,128,256]{3,2,1,0:T(8,128)(2,1)S(1)}, bf16[1,6,128,256]{3,2,1,0:T(8,128)(2,1)S(1)}, u32[]{:S(2)}, u32[]{:S(2)}) collective-permute-start(bf16[1,6,128,256]{3,2,1,0:T(8,128)(2,1)S(1)} %slice.36), channel_id=1, source_target_pairs={{0,192},{1,193},{2,194},{3,195},{4,196},{5,197},{6,198},{7,199},{8... | collective-permute-start | bytes 1179656 | tf_op jit(solution)/shard_map/ppermute | solution.py:29
  71.6 6.0 %collective-permute-start.18 = (bf16[13,16,256]{2,1,0:T(8,128)(2,1)S(1)}, bf16[13,16,256]{2,1,0:T(8,128)(2,1)S(1)}, u32[]{:S(2)}, u32[]{:S(2)}) collective-permute-start(bf16[13,16,256]{2,1,0:T(8,128)(2,1)S(1)} %slice.39), channel_id=1, source_target_pairs={{0,8},{1,9},{2,10},{3,11},{4,12},{5,13},{6,14},{7,15},{8,16},{9,17... | collective-permute-start | bytes 319496 | tf_op jit(solution)/shard_map/ppermute | solution.py:29
  98.9 2.9 %collective-permute-start.19 = (f32[8,2,128,128]{3,2,1,0:T(8,128)}, f32[8,2,128,128]{3,2,1,0:T(8,128)S(1)}, u32[]{:S(2)}, u32[]{:S(2)}) collective-permute-start(f32[8,2,128,128]{3,2,1,0:T(8,128)} %get-tuple-element.8), channel_id=1, source_target_pairs={{0,1},{1,0},{2,3},{3,2},{4,5},{5,4},{6,7},{7,6},{8,9},{9,8},{10,11... | collective-permute-start | bytes 3145736 | tf_op jit(solution)/shard_map/ppermute | solution.py:29
  (9 other events, 42.1 us)

commit v2 on v0

v2 whole, which is shorter than its diff:
```python
import jax
import jax.numpy as jnp
from jax import lax
from jax.experimental import pallas as pl
from jax.experimental.pallas import tpu as pltpu
from jax.sharding import Mesh, PartitionSpec as P

GROUPS = 32
EPSILON = 1e-06
NY, NZ, NX, NC = 4, 8, 4, 2
CHIPS = NZ * NX
TAPS = 27

AXES = ("y", "z", "x", "core")
FRAMES, ROWS, WIDTH, HALF, OUTS = 8, 4, 128, 256, 128
CELLS = 2 * ROWS * WIDTH * 16
VMEM = pl.BlockSpec(memory_space=pltpu.VMEM)
HBM = pl.BlockSpec(memory_space=pltpu.HBM)
SMEM = pl.BlockSpec(memory_space=pltpu.SMEM)
LIMIT = pltpu.CompilerParams(vmem_limit_bytes=24 * 2**20)


def send(array, move):
    pairs = []
    for y in range(NY):
        for z in range(NZ):
            for x in range(NX):
                for c in range(NC):
                    to = move(y, z, x, c)
                    if to is not None:
                        ty, tz, tx, tc = to
                        source = ((y * NZ + z) * NX + x) * NC + c
                        target = ((ty % NY * NZ + tz % NZ) * NX + tx % NX) * NC + tc % NC
                        pairs.append((source, target))
    return lax.ppermute(array, AXES, pairs)


def along_y(by):
    return lambda y, z, x, c: (y + by, z, x, c)


def along_z(by):
    return lambda y, z, x, c: (y, z + by, x, c)


def along_x(by):
    return lambda y, z, x, c: (y, z, x + by, c)


def sibling(y, z, x, c):
    return (y, z, x, 1 - c)


def strip(by):
    def move(y, z, x, c):
        chip = (z * NX + x + by) % CHIPS
        return (y, chip // NX, chip % NX, c)

    return move


def pack(info, latent, shard):
    def body(info, latent, shard, latent_out, shard_out, sems):
        at = pl.multiple_of((1 - info[4]) * HALF, HALF)
        copies = [
            pltpu.make_async_copy(shard.at[:, :, pl.ds(at, HALF)], shard_out, sems.at[0]),
            pltpu.make_async_copy(latent.at[:, :, :, pl.ds(at, HALF)], latent_out, sems.at[1]),
        ]
        for copy in copies:
            copy.start()
        for copy in copies:
            copy.wait()

    return pl.pallas_call(
        body,
        out_shape=[
            jax.ShapeDtypeStruct(latent.shape[:3] + (HALF,), latent.dtype),
            jax.ShapeDtypeStruct(shard.shape[:2] + (HALF,), shard.dtype),
        ],
        in_specs=[SMEM, HBM, HBM],
        out_specs=[HBM, HBM],
        scratch_shapes=[pltpu.SemaphoreType.DMA((2,))],
        compiler_params=LIMIT,
    )(info, latent, shard)


def unpack(info, latent, theirs):
    def body(info, latent, theirs, rows, last, first, stat, sems):
        core = info[4]
        at = pl.multiple_of(core * HALF, HALF)
        copies = [
            pltpu.make_async_copy(
                latent.at[:, :, :, pl.ds(at, HALF)], rows.at[:, pl.ds(2 * core, 2)], sems.at[0]
            ),
            pltpu.make_async_copy(theirs, rows.at[:, pl.ds(2 - 2 * core, 2)], sems.at[1]),
        ]
        for copy in copies:
            copy.start()
        for copy in copies:
            copy.wait()
        last[...] = rows[:, ROWS - 1 :]
        first[...] = rows[:, :1]
        group = [lax.broadcasted_iota(jnp.int32, (HALF, HALF), i) // 16 for i in range(2)]
        same = (group[0] == group[1]).astype(jnp.float32)

        def over_group(values):
            values = jnp.broadcast_to(jnp.sum(values, axis=0, keepdims=True), (8, HALF))
            return lax.dot_general(
                values, same, (((1,), (0,)), ((), ())), precision=lax.Precision.HIGHEST,
                preferred_element_type=jnp.float32,
            )[:1]

        def total(of):
            sums = None
            for frame in range(2):
                for r in range(ROWS):
                    part = of(rows[frame, r].astype(jnp.float32))
                    part = jnp.sum(part.reshape(WIDTH // 8, 8, HALF), axis=0)
                    sums = part if sums is None else sums + part
            return over_group(sums)

        mean = total(lambda v: v) / CELLS
        squares = total(lambda v: (v - mean) * (v - mean))
        stat[0:1] = mean
        stat[1:2] = squares

    edge = jax.ShapeDtypeStruct((2, 1, WIDTH, HALF), latent.dtype)
    return pl.pallas_call(
        body,
        out_shape=[
            jax.ShapeDtypeStruct((2, ROWS, WIDTH, HALF), latent.dtype), edge, edge,
            jax.ShapeDtypeStruct((2, HALF), jnp.float32),
        ],
        in_specs=[SMEM, HBM, HBM],
        out_specs=[VMEM] * 4,
        scratch_shapes=[pltpu.SemaphoreType.DMA((2,))],
        compiler_params=LIMIT,
    )(info, latent, theirs)


def border(above, rows, below):
    edge = 2 * WIDTH

    def body(above, rows, below, own, sems):
        copies = [pltpu.make_async_copy(rows, own.at[:, pl.ds(1, ROWS)], sems.at[0])]
        for frame in range(2):
            at = pl.ds(frame * WIDTH, WIDTH)
            copies.append(pltpu.make_async_copy(above.at[at], own.at[frame, 0], sems.at[1 + frame]))
            copies.append(pltpu.make_async_copy(below.at[at], own.at[frame, ROWS + 1], sems.at[3 + frame]))
        for copy in copies:
            copy.start()
        for copy in copies:
            copy.wait()

    return pl.pallas_call(
        body,
        out_shape=jax.ShapeDtypeStruct((2, ROWS + 2, WIDTH, HALF), rows.dtype),
        in_specs=[HBM] * 3,
        out_specs=HBM,
        scratch_shapes=[pltpu.SemaphoreType.DMA((5,))],
        compiler_params=LIMIT,
    )(above, rows, below)


def activate(info, stats, gain, shift, pieces):
    def body(info, stats, gain, shift, *refs):
        sources, results = refs[: len(pieces)], refs[len(pieces) :]
        for (_, ahead), source, result in zip(pieces, sources, results):
            means, squares = stats[:, 2 * ahead], stats[:, 2 * ahead + 1]
            mean = jnp.sum(means, axis=0, keepdims=True) / CHIPS
            deviation = means - mean
            variance = jnp.sum(squares / CELLS + deviation * deviation, axis=0, keepdims=True) / CHIPS
            scale = lax.rsqrt(variance + EPSILON) * gain[...]
            offset = shift[...]

            def row(i, _):
                frame, r = i // 6, lax.rem(i, 6)
                v = (source[frame, r].astype(jnp.float32) - mean) * scale + offset
                s = v / (1.0 + jnp.exp(-v))
                inside = jnp.logical_and(
                    jnp.logical_or(r != 0, info[2] == 0), jnp.logical_or(r != 5, info[3] == 0)
                )
                result[frame, r] = jnp.where(inside, s, 0.0).astype(jnp.bfloat16)
                return 0

            lax.fori_loop(0, 6 * source.shape[0], row, 0, unroll=2)

    arrays = [a for a, _ in pieces]
    cells = sum(a.size for a in arrays)
    return pl.pallas_call(
        body,
        out_shape=[jax.ShapeDtypeStruct(a.shape, a.dtype) for a in arrays],
        in_specs=[SMEM] + [VMEM] * (3 + len(arrays)),
        out_specs=[VMEM] * len(arrays),
        compiler_params=LIMIT,
        cost_estimate=pl.CostEstimate(flops=16 * cells, bytes_accessed=4 * cells, transcendentals=2 * cells),
    )(info, stats, gain, shift, *arrays)


def convolve(info, act, chunks, order):
    sizes = [len(piece) for piece in act]

    def body(info, *refs):
        pieces, at = [], 0
        for size in sizes:
            piece = refs[at : at + size]
            pieces.append([(piece[0], 0), (piece[0], 1)] if size == 1 else [(piece[0], 0), (piece[1], 0)])
            at += size
        taps, (keep, give) = refs[at:-2], refs[-2:]
        column = lax.broadcasted_iota(jnp.int32, (1, WIDTH, OUTS), 1)

        def matrix(tap):
            rows = [c[tap] for c in taps[:4]]
            rows.append(jnp.concatenate([taps[4][tap], taps[5][tap]], 1))
            return jnp.concatenate(rows + [c[tap] for c in taps[6:]], 0)

        def run(slot, frames):
            for t in range(2):
                total = None
                for a in range(3):
                    ref, at = frames[t + a]
                    for b in range(3):
                        lhs = ref[at, b : b + ROWS].reshape(ROWS * WIDTH, HALF)
                        rhs = jnp.concatenate([matrix((a * 3 + b) * 3 + c) for c in range(3)], 0)
                        term = lax.dot_general(
                            lhs, rhs, (((1,), (1,)), ((), ())), preferred_element_type=jnp.float32
                        )
                        total = term if total is None else total + term
                total = total.reshape(ROWS, WIDTH, 3 * OUTS)
                left, middle, right = (total[..., c * OUTS : (c + 1) * OUTS] for c in range(3))
                left = jnp.where(column == 0, 0.0, pltpu.roll(left, 1, 1))
                right = jnp.where(column == WIDTH - 1, 0.0, pltpu.roll(right, WIDTH - 1, 1))
                total = pltpu.roll((left + middle + right).reshape(ROWS * WIDTH, OUTS), info[1], 1)
                total = total.reshape(ROWS, WIDTH, OUTS)

                @pl.when(info[4] == 0)
                def _():
                    keep[slot, t] = total[:2]
                    give[slot, t] = total[2:]

                @pl.when(info[4] == 1)
                def _():
                    keep[slot, t] = total[2:]
                    give[slot, t] = total[:2]

        for slot, ahead in enumerate(order):
            now, before = pieces[ahead], pieces[ahead - 1]
            span = lax.rem(info[0] + ahead, NY)

            @pl.when(span == 0)
            def _():
                run(slot, [now[0], now[0]] + now)

            @pl.when(span != 0)
            def _():
                run(slot, before + now)

    shape = jax.ShapeDtypeStruct((len(order), 2, 2, WIDTH, OUTS), jnp.float32)
    arrays = [a for piece in act for a in piece]
    return pl.pallas_call(
        body,
        out_shape=[shape, shape],
        in_specs=[SMEM] + [VMEM] * (len(arrays) + len(chunks)),
        out_specs=[VMEM, VMEM],
        compiler_params=LIMIT,
        cost_estimate=pl.CostEstimate(
            flops=len(order) * 2 * 1024 * HALF * 27 * OUTS, bytes_accessed=5 * 2**20, transcendentals=0
        ),
    )(info, *arrays, *chunks)


def assemble(info, quarters):
    def body(info, *refs):
        out = refs[-1]
        for k in range(NY):
            at = pl.multiple_of(lax.rem(info[0] + k, NY) * OUTS, OUTS)
            out[:, :, :, pl.ds(at, OUTS)] = refs[k][...]

    return pl.pallas_call(
        body,
        out_shape=jax.ShapeDtypeStruct((2, 2, WIDTH, NY * OUTS), jnp.bfloat16),
        in_specs=[SMEM] + [VMEM] * NY,
        out_specs=VMEM,
        compiler_params=LIMIT,
    )(info, *quarters)


def per_device(latent, kernel, norm_gain, norm_shift, conv_bias):
    time_index, plane, x_index, core = (lax.axis_index(a) for a in AXES)
    chip = plane * NX + x_index
    channels = latent.shape[3]
    turn = 4 * ((chip + CHIPS - 1) % CHIPS)
    info = jnp.stack([time_index, turn, chip == 0, chip == CHIPS - 1, core]).astype(jnp.int32)
    half = lambda a: lax.dynamic_slice_in_dim(a, core * HALF, HALF, axis=a.ndim - 1)

    shard = kernel.transpose(1, 2, 3, 0, 4).reshape(TAPS, 2, channels)
    latent_give, shard_give = pack(info, latent, shard)
    other = send(shard_give, sibling)
    theirs = send(latent_give, sibling)

    near = half(shard)
    pair = jnp.where(core == 0, jnp.concatenate([near, other], 1), jnp.concatenate([other, near], 1))
    rows, last, first, stat = unpack(info, latent, theirs)
    flat = pair.reshape(TAPS * 4, HALF)
    edge = 2 * WIDTH
    from_above = send(jnp.concatenate([last.reshape(edge, HALF), flat]), strip(1))
    from_below = send(jnp.concatenate([first.reshape(edge, HALF), flat]), strip(-1))
    from_second = send(pair, strip(-2))
    block = jnp.concatenate(
        [from_above[edge:].reshape(TAPS, 4, HALF), pair, from_below[edge:].reshape(TAPS, 4, HALF), from_second], 1
    )
    own = border(from_above, rows, from_below)

    spans = [stat] + [send(stat, along_y(-k)) for k in range(1, NY)]
    spans = jnp.concatenate(spans, 0)
    spans, block, own = lax.optimization_barrier((spans, block, own))
    stats = lax.all_to_all(jnp.broadcast_to(spans[None], (CHIPS, 2 * NY, HALF)), ("z", "x"), 0, 0)

    ring = {0: block}
    for by in range(1, 4):
        ring[by] = send(ring[by - 1], along_z(-1))
        ring[-by] = send(ring[1 - by], along_z(1))
    after = send(own, along_y(-1))
    before = send(own, along_y(1))
    across_a = send(after[:1], along_y(-1))
    across_b = send(before[1:], along_y(1))

    gain, shift = half(norm_gain[None]), half(norm_shift[None])
    act_own, act_after, act_before = activate(info, stats, gain, shift, [(own, 0), (after, 1), (before, 3)])
    third, minus_third, act_own, act_after, act_before = lax.optimization_barrier(
        (ring[3], ring[-3], act_own, act_after, act_before)
    )
    far_a = send(third[..., :WIDTH], along_z(-1))
    far_b = send(minus_third[..., WIDTH:], along_z(1))
    chunks = [ring[0], ring[1], ring[2], ring[3], far_a, far_b, ring[-3], ring[-2], ring[-1]]
    act_a, act_b = activate(info, stats, gain, shift, [(across_a, 2), (across_b, 2)])
    act = [[act_own], [act_after], [act_a, act_b], [act_before]]
    bias = lax.dynamic_slice_in_dim(conv_bias, time_index * OUTS, OUTS)
    keep, give = convolve(info, act, chunks, range(NY))
    mixed = (keep + send(give, sibling) + bias).astype(jnp.bfloat16)
    quarters = [mixed[0]] + [None] * (NY - 1)
    for ahead in (2, 1, 3):
        quarters[-ahead] = send(mixed[ahead], along_y(ahead))
    return assemble(info, quarters)


def solution(mesh):
    mesh = Mesh(mesh.devices.reshape(NY, NZ, NX, NC), AXES)
    return jax.shard_map(
        per_device,
        mesh=mesh,
        in_specs=(
            P("y", ("z", "x", "core"), None, None),
            P(AXES, None, None, None, None),
            P(),
            P(),
            P(),
        ),
        out_specs=P("y", ("z", "x", "core"), None, None),
        check_vma=False,
    )
```

time: 441 us -> 97.3 us (0.22)
  blocking collectives: 250 us -> 0 us
  waiting for transfers between devices: 103 us -> 21.5 us
  matrix products: 41.7 us -> 0 us
  starting transfers between devices: 8.11 us -> 44.9 us
  Pallas kernels: 0 us -> 22.2 us
  between operations: 13.7 us -> 0.23 us
  local copies, waits for them, and re-layouts: 12 us -> 5.24 us
  other arithmetic: 7.38 us -> 1.73 us
    psum x2 -> x0, blocking collectives: 250 us -> none  [the longest x1 127 us: per_device(): spread = lax.psum(jnp.sum(centered * centered, axis=(0, 2)), 'tile')]
    all_gather x2 -> x0, waiting for transfers between devices: 85.5 us -> none  [the longest x1 85.5 us: per_device(): kernel_block = lax.all_gather(kernel, 'tile', axis=0, tiled=True)]
    dot_general x27 -> x0, matrix products: 41.7 us -> none  [convolve(): lax.dot_general(sliced, piece[:, time_tap, row_tap, col_tap, :], (((1,),...]
    ppermute x3 -> x24, starting transfers between devices: 8.07 us -> 38.4 us  [send(): return lax.ppermute(array, AXES, pairs)]
    pallas_call x0 -> x7, Pallas kernels: none -> 22.2 us  [the longest x1 13.3 us: convolve(): pl.pallas_call(body, out_shape=[shape, shape], in_specs=[SMEM] + [VMEM] *...]
    all_to_all x0 -> x1, starting transfers between devices: none -> 6.52 us  [per_device(): lax.all_to_all(jnp.broadcast_to(spans[None], (CHIPS, 2 * NY, HALF)), ('z'...]
    all_gather x1 -> x0, local copies, waits for them, and re-layouts: 5.1 us -> none  [per_device(): kernel_block = lax.all_gather(kernel, 'tile', axis=0, tiled=True)]
    ppermute x3 -> x24, waiting for transfers between devices: 17.2 us -> 21.5 us  [send(): return lax.ppermute(array, AXES, pairs)]
  transfers between devices with their start and end apart: 5 -> 25, of which waited for: 4 -> 13; matrix products, arithmetic and copies ran while one was open for 3% -> 4% of each run, Pallas kernels for 0% -> 6%
where the time goes in v2:
time: 97.3 us; the launch traced here: 95.9 us
  starting transfers between devices  44.9 us (46%)
  Pallas kernels  22.2 us (23%)
  waiting for transfers between devices  21.5 us (22%)
  local copies, waits for them, and re-layouts  5.24 us (5%)
  other arithmetic  1.73 us (2%)
    ppermute x24, starting transfers between devices, send(): return lax.ppermute(array, AXES, pairs)  38.4 us
    ppermute x24, waiting for transfers between devices, send(): return lax.ppermute(array, AXES, pairs)  21.5 us
    pallas_call x1, Pallas kernels, convolve(): pl.pallas_call(body, out_shape=[shape, shape], in_specs=[SMEM] + [VMEM] *...  13.3 us
    all_to_all x1, starting transfers between devices, per_device(): lax.all_to_all(jnp.broadcast_to(spans[None], (CHIPS, 2 * NY, HALF)), ('z'...  6.52 us
    pallas_call x2, Pallas kernels, activate(): pl.pallas_call(body, out_shape=[jax.ShapeDtypeStruct(a.shape, a.dtype) fo...  4.89 us
  transfers between devices with their start and end apart: 25, of which 13 were waited for; matrix products, arithmetic and copies ran while one was open for 4% of the time, Pallas kernels for 6%

profile of v2, /device:TPU:1, one launch (start us, length us, event | category | flops | bytes accessed | tf_op | source)
XLA Modules:
  0.0 95.9 jit_solution(16026066643663446744)
XLA Ops:
  2.5 3.3 %collective-permute-start = (bf16[2,2,128,256]{3,2,1,0:T(8,128)(2,1)S(1)}, bf16[2,2,128,256]{3,2,1,0:T(8,128)(2,1)S(1)}, u32[]{:S(2)}, u32[]{:S(2)}) collective-permute-start(bf16[2,2,128,256]{3,2,1,0:T(8,128)(2,1)S(1)} %get-tuple-element.26), channel_id=1, source_target_pairs={{0,1},{1,0},{2,3},{3,2},{4,5},{5,4},{6,7},{7,6},{8,9},{9,8},{10,11... | collective-permute-start | bytes 786440 | tf_op jit(solution)/shard_map/ppermute | solution.py:35
  7.1 1.5 %shard_map.56 = (bf16[2,4,128,256]{3,2,1,0:T(8,128)(2,1)S(1)}, bf16[2,1,128,256]{3,2,1,0:T(8,128)(2,1)S(1)}, bf16[2,1,128,256]{3,2,1,0:T(8,128)(2,1)S(1)}, f32[2,256]{1,0:T(2,128)S(1)}) custom-call(s32[5]{0:T(128)S(1)} %stack.31.info, bf16[2,2,128,512]{3,2,1,0:T(8,128)(2,1)S(1)} %copy-done.1, bf16[2,2,128,256]{3,2,1,0:T(8,128)(2,1)S(1)} %collective-permute-done.theirs), custom_call_target="tpu_custom_call" | custom-call | tf_op jit(solution)/shard_map/pallas_call | solution.py:128
  8.8 6.1 %collective-permute-start.6 = (bf16[364,256]{1,0:T(8,128)(2,1)S(1)}, bf16[364,256]{1,0:T(8,128)(2,1)S(1)}, u32[]{:S(2)}, u32[]{:S(2)}) collective-permute-start(bf16[364,256]{1,0:T(8,128)(2,1)S(1)} %get-tuple-element.52), channel_id=1, source_target_pairs={{0,62},{1,63},{2,0},{3,1},{4,2},{5,3},{6,4},{7,5},{8,6},{9,7},{10,... | collective-permute-start | bytes 559112 | tf_op jit(solution)/shard_map/ppermute | solution.py:35
  14.9 2.7 %collective-permute-start.1 = (f32[2,256]{1,0:T(2,128)S(1)}, f32[2,256]{1,0:T(2,128)S(1)}, u32[]{:S(2)}, u32[]{:S(2)}) collective-permute-start(f32[2,256]{1,0:T(2,128)S(1)} %get-tuple-element.27), channel_id=1, source_target_pairs={{0,192},{1,193},{2,194},{3,195},{4,196},{5,197},{6,198},{7,199},{8... | collective-permute-start | bytes 6152 | tf_op jit(solution)/shard_map/ppermute | solution.py:35
  18.7 1.6 %collective-permute-start.7 = (bf16[27,4,256]{2,1,0:T(4,128)(2,1)S(1)}, bf16[27,4,256]{2,1,0:T(4,128)(2,1)S(1)}, u32[]{:S(2)}, u32[]{:S(2)}) collective-permute-start(bf16[27,4,256]{2,1,0:T(4,128)(2,1)S(1)} %maximum_select_fusion), channel_id=1, source_target_pairs={{0,60},{1,61},{2,62},{3,63},{4,0},{5,1},{6,2},{7,3},{8,4},{9,5},{1... | collective-permute-start | bytes 165896 | tf_op jit(solution)/shard_map/ppermute | solution.py:35
  23.4 2.9 %collective-permute-start.14 = (bf16[2,6,128,256]{3,2,1,0:T(8,128)(2,1)S(1)}, bf16[2,6,128,256]{3,2,1,0:T(8,128)(2,1)S(1)}, u32[]{:S(2)}, u32[]{:S(2)}) collective-permute-start(bf16[2,6,128,256]{3,2,1,0:T(8,128)(2,1)S(1)} %shard_map.57.refs_0_), channel_id=1, source_target_pairs={{0,192},{1,193},{2,194},{3,195},{4,196},{5,197},{6,198},{7,199},{8... | collective-permute-start | bytes 2359304 | tf_op jit(solution)/shard_map/ppermute | solution.py:35
  26.3 1.3 %collective-permute-start.8 = (bf16[27,16,256]{2,1,0:T(8,128)(2,1)S(1)}, bf16[27,16,256]{2,1,0:T(8,128)(2,1)S(1)}, u32[]{:S(2)}, u32[]{:S(2)}) collective-permute-start(bf16[27,16,256]{2,1,0:T(8,128)(2,1)S(1)} %pad_maximum_fusion.2.refs_5_), channel_id=1, source_target_pairs={{0,56},{1,57},{2,58},{3,59},{4,60},{5,61},{6,62},{7,63},{8,0},{9,1... | collective-permute-start | bytes 663560 | tf_op jit(solution)/shard_map/ppermute | solution.py:35
  28.5 6.5 %all-to-all-start = ((f32[32,8,256]{2,1,0:T(8,128)}), f32[32,8,256]{2,1,0:T(8,128)S(1)}, u32[]{:S(2)}, u32[]{:S(2)}) async-start(f32[32,8,256]{2,1,0:T(8,128)} %broadcast_in_dim.2), calls=%async_computation | async-start | bytes 524288 | tf_op jit(solution)/shard_map/all_to_all | solution.py:317
  35.0 2.6 %collective-permute-start.9 = (bf16[27,16,256]{2,1,0:T(8,128)(2,1)S(1)}, bf16[27,16,256]{2,1,0:T(8,128)(2,1)}, u32[]{:S(2)}, u32[]{:S(2)}) collective-permute-start(bf16[27,16,256]{2,1,0:T(8,128)(2,1)S(1)} %collective-permute-done.8.refs_6_), channel_id=1, source_target_pairs={{0,56},{1,57},{2,58},{3,59},{4,60},{5,61},{6,62},{7,63},{8,0},{9,1... | collective-permute-start | bytes 663560 | tf_op jit(solution)/shard_map/ppermute | solution.py:35
  37.6 2.8 %collective-permute-done.14.refs_1_ = bf16[2,6,128,256]{3,2,1,0:T(8,128)(2,1)S(1)} collective-permute-done((bf16[2,6,128,256]{3,2,1,0:T(8,128)(2,1)S(1)}, bf16[2,6,128,256]{3,2,1,0:T(8,128)(2,1)S(1)}, u32[]{:S(2)}, u32[]{:S(2)}) %collective-permute-start.14) | collective-permute-done | bytes 786464 | tf_op jit(solution)/shard_map/ppermute | solution.py:35
  41.3 3.4 %collective-permute-start.16 = (bf16[1,6,128,256]{3,2,1,0:T(8,128)(2,1)}, bf16[1,6,128,256]{3,2,1,0:T(8,128)(2,1)}, u32[]{:S(2)}, u32[]{:S(2)}) collective-permute-start(bf16[1,6,128,256]{3,2,1,0:T(8,128)(2,1)} %slice.42), channel_id=1, source_target_pairs={{0,192},{1,193},{2,194},{3,195},{4,196},{5,197},{6,198},{7,199},{8... | collective-permute-start | bytes 1179656 | tf_op jit(solution)/shard_map/ppermute | solution.py:35
  47.2 2.9 %shard_map.58 = (bf16[2,6,128,256]{3,2,1,0:T(8,128)(2,1)S(1)}, bf16[2,6,128,256]{3,2,1,0:T(8,128)(2,1)S(1)}, bf16[2,6,128,256]{3,2,1,0:T(8,128)(2,1)S(1)}) custom-call(s32[5]{0:T(128)S(1)} %stack.31.info, f32[32,8,256]{2,1,0:T(8,128)S(1)} %all-to-all-done.stats, f32[1,256]{1,0:T(1,128)S(1)} %bitcast.24, f32[1,256]{1,0:T(1,128)S(1)} %bitcast.26, ...), custom_call_target="tpu_custom_call" | custom-call | flops 18874368 | bytes 4718592 | tf_op jit(solution)/shard_map/pallas_call | solution.py:190
  50.9 2.0 %collective-permute-done.13.refs_11_ = bf16[27,16,256]{2,1,0:T(8,128)(2,1)S(1)} collective-permute-done((bf16[27,16,256]{2,1,0:T(8,128)(2,1)}, bf16[27,16,256]{2,1,0:T(8,128)(2,1)S(1)}, u32[]{:S(2)}, u32[]{:S(2)}) %collective-permute-start.13) | collective-permute-done | bytes 221216 | tf_op jit(solution)/shard_map/ppermute | solution.py:35
  53.1 1.5 %collective-permute-start.19 = (bf16[27,16,128]{2,1,0:T(8,128)(2,1)S(1)}, bf16[27,16,128]{2,1,0:T(8,128)(2,1)S(1)}, u32[]{:S(2)}, u32[]{:S(2)}) collective-permute-start(bf16[27,16,128]{2,1,0:T(8,128)(2,1)S(1)} %slice.35), channel_id=1, source_target_pairs={{0,8},{1,9},{2,10},{3,11},{4,12},{5,13},{6,14},{7,15},{8,16},{9,17... | collective-permute-start | bytes 331784 | tf_op jit(solution)/shard_map/ppermute | solution.py:35
  54.6 2.0 %shard_map.59 = (bf16[1,6,128,256]{3,2,1,0:T(8,128)(2,1)S(1)}, bf16[1,6,128,256]{3,2,1,0:T(8,128)(2,1)S(1)}) custom-call(s32[5]{0:T(128)S(1)} %stack.31.info, f32[32,8,256]{2,1,0:T(8,128)S(1)} %all-to-all-done.stats, f32[1,256]{1,0:T(1,128)S(1)} %bitcast.25, f32[1,256]{1,0:T(1,128)S(1)} %bitcast.27, ...), custom_call_target="tpu_custom_call" | custom-call | flops 6291456 | bytes 1572864 | tf_op jit(solution)/shard_map/pallas_call | solution.py:190
  57.0 1.8 %collective-permute-done.19.refs_10_ = bf16[27,16,128]{2,1,0:T(8,128)(2,1)S(1)} collective-permute-done((bf16[27,16,128]{2,1,0:T(8,128)(2,1)S(1)}, bf16[27,16,128]{2,1,0:T(8,128)(2,1)S(1)}, u32[]{:S(2)}, u32[]{:S(2)}) %collective-permute-start.19) | collective-permute-done | bytes 110624 | tf_op jit(solution)/shard_map/ppermute | solution.py:35
  58.8 13.3 %shard_map.60 = (f32[4,2,2,128,128]{4,3,2,1,0:T(8,128)S(1)}, f32[4,2,2,128,128]{4,3,2,1,0:T(8,128)S(1)}) custom-call(s32[5]{0:T(128)S(1)} %stack.31.info, bf16[2,6,128,256]{3,2,1,0:T(8,128)(2,1)S(1)} %get-tuple-element.38.refs_0_, bf16[2,6,128,256]{3,2,1,0:T(8,128)(2,1)S(1)} %get-tuple-element.39.refs_1_, ...), custom_call_target="tpu_custom_call" | custom-call | flops 7247757312 | bytes 5242880 | tf_op jit(solution)/shard_map/pallas_call | solution.py:260
  72.2 6.4 %collective-permute-start.20 = (f32[4,2,2,128,128]{4,3,2,1,0:T(8,128)S(1)}, f32[4,2,2,128,128]{4,3,2,1,0:T(8,128)}, u32[]{:S(2)}, u32[]{:S(2)}) collective-permute-start(f32[4,2,2,128,128]{4,3,2,1,0:T(8,128)S(1)} %get-tuple-element.46), channel_id=1, source_target_pairs={{0,1},{1,0},{2,3},{3,2},{4,5},{5,4},{6,7},{7,6},{8,9},{9,8},{10,11... | collective-permute-start | bytes 3145736 | tf_op jit(solution)/shard_map/ppermute | solution.py:35
  79.4 1.7 %collective-permute-done.20 = f32[4,2,2,128,128]{4,3,2,1,0:T(8,128)} collective-permute-done((f32[4,2,2,128,128]{4,3,2,1,0:T(8,128)S(1)}, f32[4,2,2,128,128]{4,3,2,1,0:T(8,128)}, u32[]{:S(2)}, u32[]{:S(2)}) %collective-permute-start.20) | collective-permute-done | bytes 1048608 | tf_op jit(solution)/shard_map/ppermute | solution.py:35
  81.0 1.4 %add_convert_fusion = bf16[4,2,2,128,128]{4,3,2,1,0:T(8,128)(2,1)S(1)} fusion(f32[4,2,2,128,128]{4,3,2,1,0:T(8,128)S(1)} %get-tuple-element.45, f32[4,2,2,128,128]{4,3,2,1,0:T(8,128)} %collective-permute-done.20, f32[128]{0:T(128)S(1)} %dynamic_slice.15), kind=kLoop, calls=%fused_computation | loop fusion | flops 786432 | bytes 2621952 | tf_op jit(solution)/shard_map/convert_element_type | solution.py:340
  82.5 2.8 %collective-permute-start.21 = (bf16[2,2,128,128]{3,2,1,0:T(8,128)(2,1)S(1)}, bf16[2,2,128,128]{3,2,1,0:T(8,128)(2,1)S(1)}, u32[]{:S(2)}, u32[]{:S(2)}) collective-permute-start(bf16[2,2,128,128]{3,2,1,0:T(8,128)(2,1)S(1)} %get-tuple-element.49), channel_id=1, source_target_pairs={{0,192},{1,193},{2,194},{3,195},{4,196},{5,197},{6,198},{7,199},{8... | collective-permute-start | bytes 393224 | tf_op jit(solution)/shard_map/ppermute | solution.py:35
  86.0 4.7 %collective-permute-done.21.refs_1_ = bf16[2,2,128,128]{3,2,1,0:T(8,128)(2,1)S(1)} collective-permute-done((bf16[2,2,128,128]{3,2,1,0:T(8,128)(2,1)S(1)}, bf16[2,2,128,128]{3,2,1,0:T(8,128)(2,1)S(1)}, u32[]{:S(2)}, u32[]{:S(2)}) %collective-permute-start.21) | collective-permute-done | bytes 131104 | tf_op jit(solution)/shard_map/ppermute | solution.py:35
  91.3 3.2 %collective-permute-done.23.refs_3_ = bf16[2,2,128,128]{3,2,1,0:T(8,128)(2,1)S(1)} collective-permute-done((bf16[2,2,128,128]{3,2,1,0:T(8,128)(2,1)S(1)}, bf16[2,2,128,128]{3,2,1,0:T(8,128)(2,1)S(1)}, u32[]{:S(2)}, u32[]{:S(2)}) %collective-permute-start.23) | collective-permute-done | bytes 131104 | tf_op jit(solution)/shard_map/ppermute | solution.py:35
  94.4 1.5 %shard_map.61 = bf16[2,2,128,512]{3,2,1,0:T(8,128)(2,1)} custom-call(s32[5]{0:T(128)S(1)} %stack.31.info, bf16[2,2,128,128]{3,2,1,0:T(8,128)(2,1)S(1)} %get-tuple-element.50.refs_0_, bf16[2,2,128,128]{3,2,1,0:T(8,128)(2,1)S(1)} %collective-permute-done.21.refs_1_, bf16[2,2,128,128]{3,2,1,0:T(8,128)(2,1)S(1)} %collective-permute-done.22.refs_2_, ...), custom_call_target="tpu_custom_call" | custom-call | tf_op jit(solution)/shard_map/pallas_call | solution.py:279
  (68 shorter events, 15.7 us)
Async XLA Ops:
  2.5 4.7 %collective-permute-start = (bf16[2,2,128,256]{3,2,1,0:T(8,128)(2,1)S(1)}, bf16[2,2,128,256]{3,2,1,0:T(8,128)(2,1)S(1)}, u32[]{:S(2)}, u32[]{:S(2)}) collective-permute-start(bf16[2,2,128,256]{3,2,1,0:T(8,128)(2,1)S(1)} %get-tuple-element.26), channel_id=1, source_target_pairs={{0,1},{1,0},{2,3},{3,2},{4,5},{5,4},{6,7},{7,6},{8,9},{9,8},{10,11... | collective-permute-start | bytes 786440 | tf_op jit(solution)/shard_map/ppermute | solution.py:35
  8.7 12.9 %collective-permute-start.5 = (bf16[364,256]{1,0:T(8,128)(2,1)S(1)}, bf16[364,256]{1,0:T(8,128)(2,1)S(1)}, u32[]{:S(2)}, u32[]{:S(2)}) collective-permute-start(bf16[364,256]{1,0:T(8,128)(2,1)S(1)} %get-tuple-element.51), channel_id=1, source_target_pairs={{0,2},{1,3},{2,4},{3,5},{4,6},{5,7},{6,8},{7,9},{8,10},{9,11},{10,... | collective-permute-start | bytes 559112 | tf_op jit(solution)/shard_map/ppermute | solution.py:35
  8.8 12.9 %collective-permute-start.6 = (bf16[364,256]{1,0:T(8,128)(2,1)S(1)}, bf16[364,256]{1,0:T(8,128)(2,1)S(1)}, u32[]{:S(2)}, u32[]{:S(2)}) collective-permute-start(bf16[364,256]{1,0:T(8,128)(2,1)S(1)} %get-tuple-element.52), channel_id=1, source_target_pairs={{0,62},{1,63},{2,0},{3,1},{4,2},{5,3},{6,4},{7,5},{8,6},{9,7},{10,... | collective-permute-start | bytes 559112 | tf_op jit(solution)/shard_map/ppermute | solution.py:35
  14.9 3.8 %collective-permute-start.1 = (f32[2,256]{1,0:T(2,128)S(1)}, f32[2,256]{1,0:T(2,128)S(1)}, u32[]{:S(2)}, u32[]{:S(2)}) collective-permute-start(f32[2,256]{1,0:T(2,128)S(1)} %get-tuple-element.27), channel_id=1, source_target_pairs={{0,192},{1,193},{2,194},{3,195},{4,196},{5,197},{6,198},{7,199},{8... | collective-permute-start | bytes 6152 | tf_op jit(solution)/shard_map/ppermute | solution.py:35
  17.6 3.9 %collective-permute-start.2 = (f32[2,256]{1,0:T(2,128)S(1)}, f32[2,256]{1,0:T(2,128)S(1)}, u32[]{:S(2)}, u32[]{:S(2)}) collective-permute-start(f32[2,256]{1,0:T(2,128)S(1)} %get-tuple-element.27), channel_id=1, source_target_pairs={{0,128},{1,129},{2,130},{3,131},{4,132},{5,133},{6,134},{7,135},{8... | collective-permute-start | bytes 6152 | tf_op jit(solution)/shard_map/ppermute | solution.py:35
  18.0 3.6 %collective-permute-start.3 = (f32[2,256]{1,0:T(2,128)S(1)}, f32[2,256]{1,0:T(2,128)S(1)}, u32[]{:S(2)}, u32[]{:S(2)}) collective-permute-start(f32[2,256]{1,0:T(2,128)S(1)} %get-tuple-element.27), channel_id=1, source_target_pairs={{0,64},{1,65},{2,66},{3,67},{4,68},{5,69},{6,70},{7,71},{8,72},{9,... | collective-permute-start | bytes 6152 | tf_op jit(solution)/shard_map/ppermute | solution.py:35
  18.7 4.6 %collective-permute-start.7 = (bf16[27,4,256]{2,1,0:T(4,128)(2,1)S(1)}, bf16[27,4,256]{2,1,0:T(4,128)(2,1)S(1)}, u32[]{:S(2)}, u32[]{:S(2)}) collective-permute-start(bf16[27,4,256]{2,1,0:T(4,128)(2,1)S(1)} %maximum_select_fusion), channel_id=1, source_target_pairs={{0,60},{1,61},{2,62},{3,63},{4,0},{5,1},{6,2},{7,3},{8,4},{9,5},{1... | collective-permute-start | bytes 165896 | tf_op jit(solution)/shard_map/ppermute | solution.py:35
  23.4 17.1 %collective-permute-start.14 = (bf16[2,6,128,256]{3,2,1,0:T(8,128)(2,1)S(1)}, bf16[2,6,128,256]{3,2,1,0:T(8,128)(2,1)S(1)}, u32[]{:S(2)}, u32[]{:S(2)}) collective-permute-start(bf16[2,6,128,256]{3,2,1,0:T(8,128)(2,1)S(1)} %shard_map.57.refs_0_), channel_id=1, source_target_pairs={{0,192},{1,193},{2,194},{3,195},{4,196},{5,197},{6,198},{7,199},{8... | collective-permute-start | bytes 2359304 | tf_op jit(solution)/shard_map/ppermute | solution.py:35
  26.3 18.4 %collective-permute-start.15 = (bf16[2,6,128,256]{3,2,1,0:T(8,128)(2,1)S(1)}, bf16[2,6,128,256]{3,2,1,0:T(8,128)(2,1)S(1)}, u32[]{:S(2)}, u32[]{:S(2)}) collective-permute-start(bf16[2,6,128,256]{3,2,1,0:T(8,128)(2,1)S(1)} %shard_map.57.refs_0_), channel_id=1, source_target_pairs={{0,64},{1,65},{2,66},{3,67},{4,68},{5,69},{6,70},{7,71},{8,72},{9,... | collective-permute-start | bytes 2359304 | tf_op jit(solution)/shard_map/ppermute | solution.py:35
  26.3 8.7 %collective-permute-start.8 = (bf16[27,16,256]{2,1,0:T(8,128)(2,1)S(1)}, bf16[27,16,256]{2,1,0:T(8,128)(2,1)S(1)}, u32[]{:S(2)}, u32[]{:S(2)}) collective-permute-start(bf16[27,16,256]{2,1,0:T(8,128)(2,1)S(1)} %pad_maximum_fusion.2.refs_5_), channel_id=1, source_target_pairs={{0,56},{1,57},{2,58},{3,59},{4,60},{5,61},{6,62},{7,63},{8,0},{9,1... | collective-permute-start | bytes 663560 | tf_op jit(solution)/shard_map/ppermute | solution.py:35
  27.6 10.0 %collective-permute-start.11 = (bf16[27,16,256]{2,1,0:T(8,128)(2,1)S(1)}, bf16[27,16,256]{2,1,0:T(8,128)(2,1)S(1)}, u32[]{:S(2)}, u32[]{:S(2)}) collective-permute-start(bf16[27,16,256]{2,1,0:T(8,128)(2,1)S(1)} %pad_maximum_fusion.2.refs_5_), channel_id=1, source_target_pairs={{0,8},{1,9},{2,10},{3,11},{4,12},{5,13},{6,14},{7,15},{8,16},{9,17... | collective-permute-start | bytes 663560 | tf_op jit(solution)/shard_map/ppermute | solution.py:35
  28.5 18.7 %all-to-all-start = ((f32[32,8,256]{2,1,0:T(8,128)}), f32[32,8,256]{2,1,0:T(8,128)S(1)}, u32[]{:S(2)}, u32[]{:S(2)}) async-start(f32[32,8,256]{2,1,0:T(8,128)} %broadcast_in_dim.2), calls=%async_computation | async-start | bytes 524288 | tf_op jit(solution)/shard_map/all_to_all | solution.py:317
  35.0 10.4 %collective-permute-start.9 = (bf16[27,16,256]{2,1,0:T(8,128)(2,1)S(1)}, bf16[27,16,256]{2,1,0:T(8,128)(2,1)}, u32[]{:S(2)}, u32[]{:S(2)}) collective-permute-start(bf16[27,16,256]{2,1,0:T(8,128)(2,1)S(1)} %collective-permute-done.8.refs_6_), channel_id=1, source_target_pairs={{0,56},{1,57},{2,58},{3,59},{4,60},{5,61},{6,62},{7,63},{8,0},{9,1... | collective-permute-start | bytes 663560 | tf_op jit(solution)/shard_map/ppermute | solution.py:35
  37.6 9.1 %collective-permute-start.12 = (bf16[27,16,256]{2,1,0:T(8,128)(2,1)S(1)}, bf16[27,16,256]{2,1,0:T(8,128)(2,1)}, u32[]{:S(2)}, u32[]{:S(2)}) collective-permute-start(bf16[27,16,256]{2,1,0:T(8,128)(2,1)S(1)} %collective-permute-done.11.refs_13_), channel_id=1, source_target_pairs={{0,8},{1,9},{2,10},{3,11},{4,12},{5,13},{6,14},{7,15},{8,16},{9,17... | collective-permute-start | bytes 663560 | tf_op jit(solution)/shard_map/ppermute | solution.py:35
  41.3 13.4 %collective-permute-start.16 = (bf16[1,6,128,256]{3,2,1,0:T(8,128)(2,1)}, bf16[1,6,128,256]{3,2,1,0:T(8,128)(2,1)}, u32[]{:S(2)}, u32[]{:S(2)}) collective-permute-start(bf16[1,6,128,256]{3,2,1,0:T(8,128)(2,1)} %slice.42), channel_id=1, source_target_pairs={{0,192},{1,193},{2,194},{3,195},{4,196},{5,197},{6,198},{7,199},{8... | collective-permute-start | bytes 1179656 | tf_op jit(solution)/shard_map/ppermute | solution.py:35
  45.5 9.2 %collective-permute-start.17 = (bf16[1,6,128,256]{3,2,1,0:T(8,128)(2,1)}, bf16[1,6,128,256]{3,2,1,0:T(8,128)(2,1)}, u32[]{:S(2)}, u32[]{:S(2)}) collective-permute-start(bf16[1,6,128,256]{3,2,1,0:T(8,128)(2,1)} %slice.43), channel_id=1, source_target_pairs={{0,64},{1,65},{2,66},{3,67},{4,68},{5,69},{6,70},{7,71},{8,72},{9,... | collective-permute-start | bytes 1179656 | tf_op jit(solution)/shard_map/ppermute | solution.py:35
  45.5 5.5 %collective-permute-start.10 = (bf16[27,16,256]{2,1,0:T(8,128)(2,1)}, bf16[27,16,256]{2,1,0:T(8,128)(2,1)S(1)}, u32[]{:S(2)}, u32[]{:S(2)}) collective-permute-start(bf16[27,16,256]{2,1,0:T(8,128)(2,1)} %collective-permute-done.9.refs_7_), channel_id=1, source_target_pairs={{0,56},{1,57},{2,58},{3,59},{4,60},{5,61},{6,62},{7,63},{8,0},{9,1... | collective-permute-start | bytes 663560 | tf_op jit(solution)/shard_map/ppermute | solution.py:35
  46.7 6.2 %collective-permute-start.13 = (bf16[27,16,256]{2,1,0:T(8,128)(2,1)}, bf16[27,16,256]{2,1,0:T(8,128)(2,1)S(1)}, u32[]{:S(2)}, u32[]{:S(2)}) collective-permute-start(bf16[27,16,256]{2,1,0:T(8,128)(2,1)} %collective-permute-done.12.refs_12_), channel_id=1, source_target_pairs={{0,8},{1,9},{2,10},{3,11},{4,12},{5,13},{6,14},{7,15},{8,16},{9,17... | collective-permute-start | bytes 663560 | tf_op jit(solution)/shard_map/ppermute | solution.py:35
  53.0 4.1 %collective-permute-start.18 = (bf16[27,16,128]{2,1,0:T(8,128)(2,1)S(1)}, bf16[27,16,128]{2,1,0:T(8,128)(2,1)S(1)}, u32[]{:S(2)}, u32[]{:S(2)}) collective-permute-start(bf16[27,16,128]{2,1,0:T(8,128)(2,1)S(1)} %slice.34), channel_id=1, source_target_pairs={{0,56},{1,57},{2,58},{3,59},{4,60},{5,61},{6,62},{7,63},{8,0},{9,1... | collective-permute-start | bytes 331784 | tf_op jit(solution)/shard_map/ppermute | solution.py:35
  53.1 5.7 %collective-permute-start.19 = (bf16[27,16,128]{2,1,0:T(8,128)(2,1)S(1)}, bf16[27,16,128]{2,1,0:T(8,128)(2,1)S(1)}, u32[]{:S(2)}, u32[]{:S(2)}) collective-permute-start(bf16[27,16,128]{2,1,0:T(8,128)(2,1)S(1)} %slice.35), channel_id=1, source_target_pairs={{0,8},{1,9},{2,10},{3,11},{4,12},{5,13},{6,14},{7,15},{8,16},{9,17... | collective-permute-start | bytes 331784 | tf_op jit(solution)/shard_map/ppermute | solution.py:35
  72.2 8.8 %collective-permute-start.20 = (f32[4,2,2,128,128]{4,3,2,1,0:T(8,128)S(1)}, f32[4,2,2,128,128]{4,3,2,1,0:T(8,128)}, u32[]{:S(2)}, u32[]{:S(2)}) collective-permute-start(f32[4,2,2,128,128]{4,3,2,1,0:T(8,128)S(1)} %get-tuple-element.46), channel_id=1, source_target_pairs={{0,1},{1,0},{2,3},{3,2},{4,5},{5,4},{6,7},{7,6},{8,9},{9,8},{10,11... | collective-permute-start | bytes 3145736 | tf_op jit(solution)/shard_map/ppermute | solution.py:35
  82.5 8.1 %collective-permute-start.21 = (bf16[2,2,128,128]{3,2,1,0:T(8,128)(2,1)S(1)}, bf16[2,2,128,128]{3,2,1,0:T(8,128)(2,1)S(1)}, u32[]{:S(2)}, u32[]{:S(2)}) collective-permute-start(bf16[2,2,128,128]{3,2,1,0:T(8,128)(2,1)S(1)} %get-tuple-element.49), channel_id=1, source_target_pairs={{0,192},{1,193},{2,194},{3,195},{4,196},{5,197},{6,198},{7,199},{8... | collective-permute-start | bytes 393224 | tf_op jit(solution)/shard_map/ppermute | solution.py:35
  85.3 6.0 %collective-permute-start.22 = (bf16[2,2,128,128]{3,2,1,0:T(8,128)(2,1)S(1)}, bf16[2,2,128,128]{3,2,1,0:T(8,128)(2,1)S(1)}, u32[]{:S(2)}, u32[]{:S(2)}) collective-permute-start(bf16[2,2,128,128]{3,2,1,0:T(8,128)(2,1)S(1)} %get-tuple-element.48), channel_id=1, source_target_pairs={{0,128},{1,129},{2,130},{3,131},{4,132},{5,133},{6,134},{7,135},{8... | collective-permute-start | bytes 393224 | tf_op jit(solution)/shard_map/ppermute | solution.py:35
  85.3 9.1 %collective-permute-start.23 = (bf16[2,2,128,128]{3,2,1,0:T(8,128)(2,1)S(1)}, bf16[2,2,128,128]{3,2,1,0:T(8,128)(2,1)S(1)}, u32[]{:S(2)}, u32[]{:S(2)}) collective-permute-start(bf16[2,2,128,128]{3,2,1,0:T(8,128)(2,1)S(1)} %get-tuple-element.47), channel_id=1, source_target_pairs={{0,64},{1,65},{2,66},{3,67},{4,68},{5,69},{6,70},{7,71},{8,72},{9,... | collective-permute-start | bytes 393224 | tf_op jit(solution)/shard_map/ppermute | solution.py:35
  (8 other events, 25.1 us)

commit v3 on v2

--- a/solution.py
+++ b/solution.py
@@ -17,7 +17,8 @@
 VMEM = pl.BlockSpec(memory_space=pltpu.VMEM)
 HBM = pl.BlockSpec(memory_space=pltpu.HBM)
 SMEM = pl.BlockSpec(memory_space=pltpu.SMEM)
-LIMIT = pltpu.CompilerParams(vmem_limit_bytes=24 * 2**20)
+LIMIT = pltpu.CompilerParams(vmem_limit_bytes=14 * 2**20)
+WIDE = pltpu.CompilerParams(vmem_limit_bytes=60 * 2**20)
 
 
 def send(array, move):
@@ -197,22 +198,30 @@
     )(info, stats, gain, shift, *arrays)
 
 
-def convolve(info, act, chunks, order):
+def convolve(info, bias, act, chunks, order, params):
     sizes = [len(piece) for piece in act]
-
-    def body(info, *refs):
+    outs = 2 if len(order) > 1 else 3
+
+    def body(info, bias, *refs):
         pieces, at = [], 0
+        offset = bias[0:1, pl.ds(pl.multiple_of(info[0] * OUTS, OUTS), OUTS)]
         for size in sizes:
             piece = refs[at : at + size]
             pieces.append([(piece[0], 0), (piece[0], 1)] if size == 1 else [(piece[0], 0), (piece[1], 0)])
             at += size
-        taps, (keep, give) = refs[at:-2], refs[-2:]
+        taps, (keep, *give) = refs[at:-outs], refs[-outs:]
         column = lax.broadcasted_iota(jnp.int32, (1, WIDTH, OUTS), 1)
 
         def matrix(tap):
             rows = [c[tap] for c in taps[:4]]
             rows.append(jnp.concatenate([taps[4][tap], taps[5][tap]], 1))
             return jnp.concatenate(rows + [c[tap] for c in taps[6:]], 0)
+
+        def hand(slot, t, value):
+            if outs == 2:
+                give[0][slot, t] = value.astype(jnp.bfloat16)
+            else:
+                give[t][...] = value.astype(jnp.bfloat16)
 
         def run(slot, frames):
             for t in range(2):
@@ -235,13 +244,13 @@
 
                 @pl.when(info[4] == 0)
                 def _():
-                    keep[slot, t] = total[:2]
-                    give[slot, t] = total[2:]
+                    keep[slot, t] = total[:2] + offset
+                    hand(slot, t, total[2:])
 
                 @pl.when(info[4] == 1)
                 def _():
-                    keep[slot, t] = total[2:]
-                    give[slot, t] = total[:2]
+                    keep[slot, t] = total[2:] + offset
+                    hand(slot, t, total[:2])
 
         for slot, ahead in enumerate(order):
             now, before = pieces[ahead], pieces[ahead - 1]
@@ -255,34 +264,53 @@
             def _():
                 run(slot, before + now)
 
-    shape = jax.ShapeDtypeStruct((len(order), 2, 2, WIDTH, OUTS), jnp.float32)
+    shape = (len(order), 2, 2, WIDTH, OUTS)
     arrays = [a for piece in act for a in piece]
     return pl.pallas_call(
         body,
-        out_shape=[shape, shape],
-        in_specs=[SMEM] + [VMEM] * (len(arrays) + len(chunks)),
-        out_specs=[VMEM, VMEM],
-        compiler_params=LIMIT,
+        out_shape=[jax.ShapeDtypeStruct(shape, jnp.float32)]
+        + [jax.ShapeDtypeStruct(shape if outs == 2 else shape[2:], jnp.bfloat16)] * (outs - 1),
+        in_specs=[SMEM, VMEM] + [VMEM] * (len(arrays) + len(chunks)),
+        out_specs=[VMEM] * outs,
+        compiler_params=params,
         cost_estimate=pl.CostEstimate(
             flops=len(order) * 2 * 1024 * HALF * 27 * OUTS, bytes_accessed=5 * 2**20, transcendentals=0
         ),
-    )(info, *arrays, *chunks)
-
-
-def assemble(info, quarters):
-    def body(info, *refs):
+    )(info, bias, *arrays, *chunks)
+
+
+def mix(keep, taken):
+    count = keep.shape[0]
+
+    def body(keep, taken, *outs):
+        for k in range(count):
+            outs[k][...] = (keep[k] + taken[k].astype(jnp.float32)).astype(jnp.bfloat16)
+
+    return pl.pallas_call(
+        body, out_shape=[jax.ShapeDtypeStruct(taken.shape[1:], jnp.bfloat16)] * count,
+        in_specs=[VMEM, VMEM], out_specs=[VMEM] * count, compiler_params=LIMIT,
+    )(keep, taken)
+
+
+def assemble(info, keep, taken, quarters):
+    def body(info, keep, first, second, *refs):
         out = refs[-1]
         for k in range(NY):
             at = pl.multiple_of(lax.rem(info[0] + k, NY) * OUTS, OUTS)
-            out[:, :, :, pl.ds(at, OUTS)] = refs[k][...]
+            if k == 0:
+                for t, taken in enumerate((first, second)):
+                    value = keep[0, t] + taken[...].astype(jnp.float32)
+                    out[t, :, :, pl.ds(at, OUTS)] = value.astype(jnp.bfloat16)
+            else:
+                out[:, :, :, pl.ds(at, OUTS)] = refs[k - 1][...]
 
     return pl.pallas_call(
         body,
         out_shape=jax.ShapeDtypeStruct((2, 2, WIDTH, NY * OUTS), jnp.bfloat16),
-        in_specs=[SMEM] + [VMEM] * NY,
+        in_specs=[SMEM] + [VMEM] * (NY + 2),
         out_specs=VMEM,
         compiler_params=LIMIT,
-    )(info, *quarters)
+    )(info, keep, *taken, *quarters)
 
 
 def per_device(latent, kernel, norm_gain, norm_shift, conv_bias):
@@ -335,13 +363,16 @@
     chunks = [ring[0], ring[1], ring[2], ring[3], far_a, far_b, ring[-3], ring[-2], ring[-1]]
     act_a, act_b = activate(info, stats, gain, shift, [(across_a, 2), (across_b, 2)])
     act = [[act_own], [act_after], [act_a, act_b], [act_before]]
-    bias = lax.dynamic_slice_in_dim(conv_bias, time_index * OUTS, OUTS)
-    keep, give = convolve(info, act, chunks, range(NY))
-    mixed = (keep + send(give, sibling) + bias).astype(jnp.bfloat16)
-    quarters = [mixed[0]] + [None] * (NY - 1)
-    for ahead in (2, 1, 3):
-        quarters[-ahead] = send(mixed[ahead], along_y(ahead))
-    return assemble(info, quarters)
+    order = (2, 1, 3)
+    bias = conv_bias[None]
+    keep, give = convolve(info, bias, act, chunks, order, LIMIT)
+    mixed = mix(keep, send(give, sibling))
+    quarters = [None] * NY
+    late, *mixed = lax.optimization_barrier((info, *mixed))
+    for slot, ahead in enumerate(order):
+        quarters[-ahead] = send(mixed[slot], along_y(ahead))
+    keep_own, *give_own = convolve(late, bias, act, chunks, (0,), LIMIT)
+    return assemble(info, keep_own, [send(a, sibling) for a in give_own], quarters[1:])
 
 
 def solution(mesh):

time: 97.3 us -> 92.6 us (0.952)
  waiting for transfers between devices: 21.5 us -> 16 us
  other arithmetic: 1.73 us -> 0.29 us
  starting transfers between devices: 44.9 us -> 46.2 us
  Pallas kernels: 22.2 us -> 23.3 us
    ppermute x24 -> x26, waiting for transfers between devices: 21.5 us -> 16 us  [send(): return lax.ppermute(array, AXES, pairs)]
    convert_element_type x1 -> x0, other arithmetic: 1.44 us -> none  [per_device(): mixed = (keep + send(give, sibling) + bias).astype(jnp.bfloat16)]
    ppermute x24 -> x26, starting transfers between devices: 38.4 us -> 39.6 us  [send(): return lax.ppermute(array, AXES, pairs)]
    pallas_call x1 -> x3, Pallas kernels: 13.3 us -> 14.4 us  [the longest x2 14.4 us: convolve(): pl.pallas_call(body, out_shape=[jax.ShapeDtypeStruct(shape, jnp.float32)]...]
    unnamed x14 -> x16, local copies, waits for them, and re-layouts: 1.79 us -> 2.47 us
  transfers between devices with their start and end apart: 25 -> 27, of which waited for: 13 -> 13; matrix products, arithmetic and copies ran while one was open for 4% -> 3% of each run, Pallas kernels for 6% -> 10%
where the time goes in v3:
time: 92.6 us; the launch traced here: 91.2 us
  starting transfers between devices  46.2 us (50%)
  Pallas kernels  23.3 us (25%)
  waiting for transfers between devices  16 us (17%)
  local copies, waits for them, and re-layouts  5.1 us (6%)
    ppermute x26, starting transfers between devices, send(): return lax.ppermute(array, AXES, pairs)  39.6 us
    ppermute x26, waiting for transfers between devices, send(): return lax.ppermute(array, AXES, pairs)  16 us
    pallas_call x2, Pallas kernels, convolve(): pl.pallas_call(body, out_shape=[jax.ShapeDtypeStruct(shape, jnp.float32)]...  14.4 us
    all_to_all x1, starting transfers between devices, per_device(): lax.all_to_all(jnp.broadcast_to(spans[None], (CHIPS, 2 * NY, HALF)), ('z'...  6.53 us
    pallas_call x2, Pallas kernels, activate(): pl.pallas_call(body, out_shape=[jax.ShapeDtypeStruct(a.shape, a.dtype) fo...  4.89 us
    unnamed x16, local copies, waits for them, and re-layouts  2.47 us
  transfers between devices with their start and end apart: 27, of which 13 were waited for; matrix products, arithmetic and copies ran while one was open for 3% of the time, Pallas kernels for 10%

profile of v3, /device:TPU:1, one launch (start us, length us, event | category | flops | bytes accessed | tf_op | source)
XLA Modules:
  0.0 91.2 jit_solution(6822155169407329357)
XLA Ops:
  2.5 3.3 %collective-permute-start = (bf16[2,2,128,256]{3,2,1,0:T(8,128)(2,1)S(1)}, bf16[2,2,128,256]{3,2,1,0:T(8,128)(2,1)S(1)}, u32[]{:S(2)}, u32[]{:S(2)}) collective-permute-start(bf16[2,2,128,256]{3,2,1,0:T(8,128)(2,1)S(1)} %get-tuple-element.36), channel_id=1, source_target_pairs={{0,1},{1,0},{2,3},{3,2},{4,5},{5,4},{6,7},{7,6},{8,9},{9,8},{10,11... | collective-permute-start | bytes 786440 | tf_op jit(solution)/shard_map/ppermute | solution.py:36
  7.1 1.5 %shard_map.56 = (bf16[2,4,128,256]{3,2,1,0:T(8,128)(2,1)S(1)}, bf16[2,1,128,256]{3,2,1,0:T(8,128)(2,1)S(1)}, bf16[2,1,128,256]{3,2,1,0:T(8,128)(2,1)S(1)}, f32[2,256]{1,0:T(2,128)S(1)}) custom-call(s32[5]{0:T(128)S(1)} %stack.31.info, bf16[2,2,128,512]{3,2,1,0:T(8,128)(2,1)S(1)} %copy-done.1, bf16[2,2,128,256]{3,2,1,0:T(8,128)(2,1)S(1)} %collective-permute-done.theirs), custom_call_target="tpu_custom_call" | custom-call | tf_op jit(solution)/shard_map/pallas_call | solution.py:129
  8.8 6.1 %collective-permute-start.6 = (bf16[364,256]{1,0:T(8,128)(2,1)S(1)}, bf16[364,256]{1,0:T(8,128)(2,1)S(1)}, u32[]{:S(2)}, u32[]{:S(2)}) collective-permute-start(bf16[364,256]{1,0:T(8,128)(2,1)S(1)} %get-tuple-element.68), channel_id=1, source_target_pairs={{0,62},{1,63},{2,0},{3,1},{4,2},{5,3},{6,4},{7,5},{8,6},{9,7},{10,... | collective-permute-start | bytes 559112 | tf_op jit(solution)/shard_map/ppermute | solution.py:36
  14.9 2.7 %collective-permute-start.1 = (f32[2,256]{1,0:T(2,128)S(1)}, f32[2,256]{1,0:T(2,128)S(1)}, u32[]{:S(2)}, u32[]{:S(2)}) collective-permute-start(f32[2,256]{1,0:T(2,128)S(1)} %get-tuple-element.37), channel_id=1, source_target_pairs={{0,192},{1,193},{2,194},{3,195},{4,196},{5,197},{6,198},{7,199},{8... | collective-permute-start | bytes 6152 | tf_op jit(solution)/shard_map/ppermute | solution.py:36
  18.7 1.6 %collective-permute-start.7 = (bf16[27,4,256]{2,1,0:T(4,128)(2,1)S(1)}, bf16[27,4,256]{2,1,0:T(4,128)(2,1)S(1)}, u32[]{:S(2)}, u32[]{:S(2)}) collective-permute-start(bf16[27,4,256]{2,1,0:T(4,128)(2,1)S(1)} %maximum_select_fusion), channel_id=1, source_target_pairs={{0,60},{1,61},{2,62},{3,63},{4,0},{5,1},{6,2},{7,3},{8,4},{9,5},{1... | collective-permute-start | bytes 165896 | tf_op jit(solution)/shard_map/ppermute | solution.py:36
  23.4 2.9 %collective-permute-start.14 = (bf16[2,6,128,256]{3,2,1,0:T(8,128)(2,1)S(1)}, bf16[2,6,128,256]{3,2,1,0:T(8,128)(2,1)S(1)}, u32[]{:S(2)}, u32[]{:S(2)}) collective-permute-start(bf16[2,6,128,256]{3,2,1,0:T(8,128)(2,1)S(1)} %shard_map.57.refs_0_), channel_id=1, source_target_pairs={{0,192},{1,193},{2,194},{3,195},{4,196},{5,197},{6,198},{7,199},{8... | collective-permute-start | bytes 2359304 | tf_op jit(solution)/shard_map/ppermute | solution.py:36
  26.3 1.3 %collective-permute-start.8 = (bf16[27,16,256]{2,1,0:T(8,128)(2,1)S(1)}, bf16[27,16,256]{2,1,0:T(8,128)(2,1)S(1)}, u32[]{:S(2)}, u32[]{:S(2)}) collective-permute-start(bf16[27,16,256]{2,1,0:T(8,128)(2,1)S(1)} %pad_maximum_fusion.2.refs_5_), channel_id=1, source_target_pairs={{0,56},{1,57},{2,58},{3,59},{4,60},{5,61},{6,62},{7,63},{8,0},{9,1... | collective-permute-start | bytes 663560 | tf_op jit(solution)/shard_map/ppermute | solution.py:36
  28.5 6.5 %all-to-all-start = ((f32[32,8,256]{2,1,0:T(8,128)}), f32[32,8,256]{2,1,0:T(8,128)S(1)}, u32[]{:S(2)}, u32[]{:S(2)}) async-start(f32[32,8,256]{2,1,0:T(8,128)} %broadcast_in_dim.5), calls=%async_computation | async-start | bytes 524288 | tf_op jit(solution)/shard_map/all_to_all | solution.py:345
  35.0 2.6 %collective-permute-start.9 = (bf16[27,16,256]{2,1,0:T(8,128)(2,1)S(1)}, bf16[27,16,256]{2,1,0:T(8,128)(2,1)}, u32[]{:S(2)}, u32[]{:S(2)}) collective-permute-start(bf16[27,16,256]{2,1,0:T(8,128)(2,1)S(1)} %collective-permute-done.8.refs_6_), channel_id=1, source_target_pairs={{0,56},{1,57},{2,58},{3,59},{4,60},{5,61},{6,62},{7,63},{8,0},{9,1... | collective-permute-start | bytes 663560 | tf_op jit(solution)/shard_map/ppermute | solution.py:36
  37.6 2.8 %collective-permute-done.14.refs_1_ = bf16[2,6,128,256]{3,2,1,0:T(8,128)(2,1)S(1)} collective-permute-done((bf16[2,6,128,256]{3,2,1,0:T(8,128)(2,1)S(1)}, bf16[2,6,128,256]{3,2,1,0:T(8,128)(2,1)S(1)}, u32[]{:S(2)}, u32[]{:S(2)}) %collective-permute-start.14) | collective-permute-done | bytes 786464 | tf_op jit(solution)/shard_map/ppermute | solution.py:36
  41.3 3.4 %collective-permute-start.16 = (bf16[1,6,128,256]{3,2,1,0:T(8,128)(2,1)}, bf16[1,6,128,256]{3,2,1,0:T(8,128)(2,1)}, u32[]{:S(2)}, u32[]{:S(2)}) collective-permute-start(bf16[1,6,128,256]{3,2,1,0:T(8,128)(2,1)} %slice.26), channel_id=1, source_target_pairs={{0,192},{1,193},{2,194},{3,195},{4,196},{5,197},{6,198},{7,199},{8... | collective-permute-start | bytes 1179656 | tf_op jit(solution)/shard_map/ppermute | solution.py:36
  45.5 1.3 %collective-permute-start.10 = (bf16[27,16,256]{2,1,0:T(8,128)(2,1)}, bf16[27,16,256]{2,1,0:T(8,128)(2,1)S(1)}, u32[]{:S(2)}, u32[]{:S(2)}) collective-permute-start(bf16[27,16,256]{2,1,0:T(8,128)(2,1)} %collective-permute-done.9.refs_7_), channel_id=1, source_target_pairs={{0,56},{1,57},{2,58},{3,59},{4,60},{5,61},{6,62},{7,63},{8,0},{9,1... | collective-permute-start | bytes 663560 | tf_op jit(solution)/shard_map/ppermute | solution.py:36
  47.2 2.9 %shard_map.58 = (bf16[2,6,128,256]{3,2,1,0:T(8,128)(2,1)S(1)}, bf16[2,6,128,256]{3,2,1,0:T(8,128)(2,1)S(1)}, bf16[2,6,128,256]{3,2,1,0:T(8,128)(2,1)S(1)}) custom-call(s32[5]{0:T(128)S(1)} %stack.31.info, f32[32,8,256]{2,1,0:T(8,128)S(1)} %all-to-all-done.stats, f32[1,256]{1,0:T(1,128)S(1)} %bitcast.17, f32[1,256]{1,0:T(1,128)S(1)} %bitcast.19, ...), custom_call_target="tpu_custom_call" | custom-call | flops 18874368 | bytes 4718592 | tf_op jit(solution)/shard_map/pallas_call | solution.py:191
  50.9 2.0 %collective-permute-done.13.refs_11_ = bf16[27,16,256]{2,1,0:T(8,128)(2,1)S(1)} collective-permute-done((bf16[27,16,256]{2,1,0:T(8,128)(2,1)}, bf16[27,16,256]{2,1,0:T(8,128)(2,1)S(1)}, u32[]{:S(2)}, u32[]{:S(2)}) %collective-permute-start.13) | collective-permute-done | bytes 221216 | tf_op jit(solution)/shard_map/ppermute | solution.py:36
  53.1 1.5 %collective-permute-start.19 = (bf16[27,16,128]{2,1,0:T(8,128)(2,1)S(1)}, bf16[27,16,128]{2,1,0:T(8,128)(2,1)S(1)}, u32[]{:S(2)}, u32[]{:S(2)}) collective-permute-start(bf16[27,16,128]{2,1,0:T(8,128)(2,1)S(1)} %slice.23), channel_id=1, source_target_pairs={{0,8},{1,9},{2,10},{3,11},{4,12},{5,13},{6,14},{7,15},{8,16},{9,17... | collective-permute-start | bytes 331784 | tf_op jit(solution)/shard_map/ppermute | solution.py:36
  54.6 2.0 %shard_map.59 = (bf16[1,6,128,256]{3,2,1,0:T(8,128)(2,1)S(1)}, bf16[1,6,128,256]{3,2,1,0:T(8,128)(2,1)S(1)}) custom-call(s32[5]{0:T(128)S(1)} %stack.31.info, f32[32,8,256]{2,1,0:T(8,128)S(1)} %all-to-all-done.stats, f32[1,256]{1,0:T(1,128)S(1)} %bitcast.18, f32[1,256]{1,0:T(1,128)S(1)} %bitcast.20, ...), custom_call_target="tpu_custom_call" | custom-call | flops 6291456 | bytes 1572864 | tf_op jit(solution)/shard_map/pallas_call | solution.py:191
  57.0 1.8 %collective-permute-done.19.refs_10_ = bf16[27,16,128]{2,1,0:T(8,128)(2,1)S(1)} collective-permute-done((bf16[27,16,128]{2,1,0:T(8,128)(2,1)S(1)}, bf16[27,16,128]{2,1,0:T(8,128)(2,1)S(1)}, u32[]{:S(2)}, u32[]{:S(2)}) %collective-permute-start.19) | collective-permute-done | bytes 110624 | tf_op jit(solution)/shard_map/ppermute | solution.py:36
  59.5 10.3 %shard_map.60 = (f32[3,2,2,128,128]{4,3,2,1,0:T(8,128)S(1)}, bf16[3,2,2,128,128]{4,3,2,1,0:T(8,128)(2,1)S(1)}) custom-call(s32[5]{0:T(128)S(1)} %stack.31.info, f32[1,512]{1,0:T(1,128)S(1)} %bitcast.21, bf16[2,6,128,256]{3,2,1,0:T(8,128)(2,1)S(1)} %get-tuple-element.48.refs_0_, bf16[2,6,128,256]{3,2,1,0:T(8,128)(2,1)S(1)} %get-tuple-element.49.refs_1_, ...), custom_call_target="tpu_custom_call" | custom-call | flops 5435817984 | bytes 5242880 | tf_op jit(solution)/shard_map/pallas_call | solution.py:269
  69.8 6.5 %collective-permute-start.20 = (bf16[3,2,2,128,128]{4,3,2,1,0:T(8,128)(2,1)S(1)}, bf16[3,2,2,128,128]{4,3,2,1,0:T(8,128)(2,1)S(1)}, u32[]{:S(2)}, u32[]{:S(2)}) collective-permute-start(bf16[3,2,2,128,128]{4,3,2,1,0:T(8,128)(2,1)S(1)} %get-tuple-element.56), channel_id=1, source_target_pairs={{0,1},{1,0},{2,3},{3,2},{4,5},{5,4},{6,7},{7,6},{8,9},{9,8},{10,11... | collective-permute-start | bytes 1179656 | tf_op jit(solution)/shard_map/ppermute | solution.py:36
  76.4 1.3 %collective-permute-done.20.taken = bf16[3,2,2,128,128]{4,3,2,1,0:T(8,128)(2,1)S(1)} collective-permute-done((bf16[3,2,2,128,128]{4,3,2,1,0:T(8,128)(2,1)S(1)}, bf16[3,2,2,128,128]{4,3,2,1,0:T(8,128)(2,1)S(1)}, u32[]{:S(2)}, u32[]{:S(2)}) %collective-permute-start.20) | collective-permute-done | bytes 393248 | tf_op jit(solution)/shard_map/ppermute | solution.py:36
  77.8 2.8 %collective-permute-start.23 = (bf16[2,2,128,128]{3,2,1,0:T(8,128)(2,1)S(1)}, bf16[2,2,128,128]{3,2,1,0:T(8,128)(2,1)S(1)}, u32[]{:S(2)}, u32[]{:S(2)}) collective-permute-start(bf16[2,2,128,128]{3,2,1,0:T(8,128)(2,1)S(1)} %get-tuple-element.64), channel_id=1, source_target_pairs={{0,192},{1,193},{2,194},{3,195},{4,196},{5,197},{6,198},{7,199},{8... | collective-permute-start | bytes 393224 | tf_op jit(solution)/shard_map/ppermute | solution.py:36
  81.2 4.1 %shard_map.62 = (f32[1,2,2,128,128]{4,3,2,1,0:T(8,128)S(1)}, bf16[2,128,128]{2,1,0:T(8,128)(2,1)S(1)}, bf16[2,128,128]{2,1,0:T(8,128)(2,1)S(1)}) custom-call(s32[5]{0:T(128)S(1)} %stack.31.info, f32[1,512]{1,0:T(1,128)S(1)} %bitcast.22, bf16[2,6,128,256]{3,2,1,0:T(8,128)(2,1)S(1)} %get-tuple-element.48.refs_0_, ...), custom_call_target="tpu_custom_call" | custom-call | flops 1811939328 | bytes 5242880 | tf_op jit(solution)/shard_map/pallas_call | solution.py:269
  87.6 2.1 %collective-permute-done.25.refs_2_ = bf16[2,2,128,128]{3,2,1,0:T(8,128)(2,1)S(1)} collective-permute-done((bf16[2,2,128,128]{3,2,1,0:T(8,128)(2,1)S(1)}, bf16[2,2,128,128]{3,2,1,0:T(8,128)(2,1)S(1)}, u32[]{:S(2)}, u32[]{:S(2)}) %collective-permute-start.25) | collective-permute-done | bytes 131104 | tf_op jit(solution)/shard_map/ppermute | solution.py:36
  89.7 1.5 %shard_map.63 = bf16[2,2,128,512]{3,2,1,0:T(8,128)(2,1)} custom-call(s32[5]{0:T(128)S(1)} %stack.31.info, f32[1,2,2,128,128]{4,3,2,1,0:T(8,128)S(1)} %get-tuple-element.61.keep, bf16[2,128,128]{2,1,0:T(8,128)(2,1)S(1)} %collective-permute-done.21.first, bf16[2,128,128]{2,1,0:T(8,128)(2,1)S(1)} %collective-permute-done.22.second, ...), custom_call_target="tpu_custom_call" | custom-call | tf_op jit(solution)/shard_map/pallas_call | solution.py:307
  (73 shorter events, 16.0 us)
Async XLA Ops:
  2.5 4.7 %collective-permute-start = (bf16[2,2,128,256]{3,2,1,0:T(8,128)(2,1)S(1)}, bf16[2,2,128,256]{3,2,1,0:T(8,128)(2,1)S(1)}, u32[]{:S(2)}, u32[]{:S(2)}) collective-permute-start(bf16[2,2,128,256]{3,2,1,0:T(8,128)(2,1)S(1)} %get-tuple-element.36), channel_id=1, source_target_pairs={{0,1},{1,0},{2,3},{3,2},{4,5},{5,4},{6,7},{7,6},{8,9},{9,8},{10,11... | collective-permute-start | bytes 786440 | tf_op jit(solution)/shard_map/ppermute | solution.py:36
  8.7 12.9 %collective-permute-start.5 = (bf16[364,256]{1,0:T(8,128)(2,1)S(1)}, bf16[364,256]{1,0:T(8,128)(2,1)S(1)}, u32[]{:S(2)}, u32[]{:S(2)}) collective-permute-start(bf16[364,256]{1,0:T(8,128)(2,1)S(1)} %get-tuple-element.67), channel_id=1, source_target_pairs={{0,2},{1,3},{2,4},{3,5},{4,6},{5,7},{6,8},{7,9},{8,10},{9,11},{10,... | collective-permute-start | bytes 559112 | tf_op jit(solution)/shard_map/ppermute | solution.py:36
  8.8 12.9 %collective-permute-start.6 = (bf16[364,256]{1,0:T(8,128)(2,1)S(1)}, bf16[364,256]{1,0:T(8,128)(2,1)S(1)}, u32[]{:S(2)}, u32[]{:S(2)}) collective-permute-start(bf16[364,256]{1,0:T(8,128)(2,1)S(1)} %get-tuple-element.68), channel_id=1, source_target_pairs={{0,62},{1,63},{2,0},{3,1},{4,2},{5,3},{6,4},{7,5},{8,6},{9,7},{10,... | collective-permute-start | bytes 559112 | tf_op jit(solution)/shard_map/ppermute | solution.py:36
  14.9 3.8 %collective-permute-start.1 = (f32[2,256]{1,0:T(2,128)S(1)}, f32[2,256]{1,0:T(2,128)S(1)}, u32[]{:S(2)}, u32[]{:S(2)}) collective-permute-start(f32[2,256]{1,0:T(2,128)S(1)} %get-tuple-element.37), channel_id=1, source_target_pairs={{0,192},{1,193},{2,194},{3,195},{4,196},{5,197},{6,198},{7,199},{8... | collective-permute-start | bytes 6152 | tf_op jit(solution)/shard_map/ppermute | solution.py:36
  17.6 3.9 %collective-permute-start.2 = (f32[2,256]{1,0:T(2,128)S(1)}, f32[2,256]{1,0:T(2,128)S(1)}, u32[]{:S(2)}, u32[]{:S(2)}) collective-permute-start(f32[2,256]{1,0:T(2,128)S(1)} %get-tuple-element.37), channel_id=1, source_target_pairs={{0,128},{1,129},{2,130},{3,131},{4,132},{5,133},{6,134},{7,135},{8... | collective-permute-start | bytes 6152 | tf_op jit(solution)/shard_map/ppermute | solution.py:36
  18.0 3.6 %collective-permute-start.3 = (f32[2,256]{1,0:T(2,128)S(1)}, f32[2,256]{1,0:T(2,128)S(1)}, u32[]{:S(2)}, u32[]{:S(2)}) collective-permute-start(f32[2,256]{1,0:T(2,128)S(1)} %get-tuple-element.37), channel_id=1, source_target_pairs={{0,64},{1,65},{2,66},{3,67},{4,68},{5,69},{6,70},{7,71},{8,72},{9,... | collective-permute-start | bytes 6152 | tf_op jit(solution)/shard_map/ppermute | solution.py:36
  18.7 4.6 %collective-permute-start.7 = (bf16[27,4,256]{2,1,0:T(4,128)(2,1)S(1)}, bf16[27,4,256]{2,1,0:T(4,128)(2,1)S(1)}, u32[]{:S(2)}, u32[]{:S(2)}) collective-permute-start(bf16[27,4,256]{2,1,0:T(4,128)(2,1)S(1)} %maximum_select_fusion), channel_id=1, source_target_pairs={{0,60},{1,61},{2,62},{3,63},{4,0},{5,1},{6,2},{7,3},{8,4},{9,5},{1... | collective-permute-start | bytes 165896 | tf_op jit(solution)/shard_map/ppermute | solution.py:36
  23.4 17.1 %collective-permute-start.14 = (bf16[2,6,128,256]{3,2,1,0:T(8,128)(2,1)S(1)}, bf16[2,6,128,256]{3,2,1,0:T(8,128)(2,1)S(1)}, u32[]{:S(2)}, u32[]{:S(2)}) collective-permute-start(bf16[2,6,128,256]{3,2,1,0:T(8,128)(2,1)S(1)} %shard_map.57.refs_0_), channel_id=1, source_target_pairs={{0,192},{1,193},{2,194},{3,195},{4,196},{5,197},{6,198},{7,199},{8... | collective-permute-start | bytes 2359304 | tf_op jit(solution)/shard_map/ppermute | solution.py:36
  26.3 18.4 %collective-permute-start.15 = (bf16[2,6,128,256]{3,2,1,0:T(8,128)(2,1)S(1)}, bf16[2,6,128,256]{3,2,1,0:T(8,128)(2,1)S(1)}, u32[]{:S(2)}, u32[]{:S(2)}) collective-permute-start(bf16[2,6,128,256]{3,2,1,0:T(8,128)(2,1)S(1)} %shard_map.57.refs_0_), channel_id=1, source_target_pairs={{0,64},{1,65},{2,66},{3,67},{4,68},{5,69},{6,70},{7,71},{8,72},{9,... | collective-permute-start | bytes 2359304 | tf_op jit(solution)/shard_map/ppermute | solution.py:36
  26.3 8.7 %collective-permute-start.8 = (bf16[27,16,256]{2,1,0:T(8,128)(2,1)S(1)}, bf16[27,16,256]{2,1,0:T(8,128)(2,1)S(1)}, u32[]{:S(2)}, u32[]{:S(2)}) collective-permute-start(bf16[27,16,256]{2,1,0:T(8,128)(2,1)S(1)} %pad_maximum_fusion.2.refs_5_), channel_id=1, source_target_pairs={{0,56},{1,57},{2,58},{3,59},{4,60},{5,61},{6,62},{7,63},{8,0},{9,1... | collective-permute-start | bytes 663560 | tf_op jit(solution)/shard_map/ppermute | solution.py:36
  27.6 10.0 %collective-permute-start.11 = (bf16[27,16,256]{2,1,0:T(8,128)(2,1)S(1)}, bf16[27,16,256]{2,1,0:T(8,128)(2,1)S(1)}, u32[]{:S(2)}, u32[]{:S(2)}) collective-permute-start(bf16[27,16,256]{2,1,0:T(8,128)(2,1)S(1)} %pad_maximum_fusion.2.refs_5_), channel_id=1, source_target_pairs={{0,8},{1,9},{2,10},{3,11},{4,12},{5,13},{6,14},{7,15},{8,16},{9,17... | collective-permute-start | bytes 663560 | tf_op jit(solution)/shard_map/ppermute | solution.py:36
  28.5 18.7 %all-to-all-start = ((f32[32,8,256]{2,1,0:T(8,128)}), f32[32,8,256]{2,1,0:T(8,128)S(1)}, u32[]{:S(2)}, u32[]{:S(2)}) async-start(f32[32,8,256]{2,1,0:T(8,128)} %broadcast_in_dim.5), calls=%async_computation | async-start | bytes 524288 | tf_op jit(solution)/shard_map/all_to_all | solution.py:345
  35.0 10.4 %collective-permute-start.9 = (bf16[27,16,256]{2,1,0:T(8,128)(2,1)S(1)}, bf16[27,16,256]{2,1,0:T(8,128)(2,1)}, u32[]{:S(2)}, u32[]{:S(2)}) collective-permute-start(bf16[27,16,256]{2,1,0:T(8,128)(2,1)S(1)} %collective-permute-done.8.refs_6_), channel_id=1, source_target_pairs={{0,56},{1,57},{2,58},{3,59},{4,60},{5,61},{6,62},{7,63},{8,0},{9,1... | collective-permute-start | bytes 663560 | tf_op jit(solution)/shard_map/ppermute | solution.py:36
  37.6 9.1 %collective-permute-start.12 = (bf16[27,16,256]{2,1,0:T(8,128)(2,1)S(1)}, bf16[27,16,256]{2,1,0:T(8,128)(2,1)}, u32[]{:S(2)}, u32[]{:S(2)}) collective-permute-start(bf16[27,16,256]{2,1,0:T(8,128)(2,1)S(1)} %collective-permute-done.11.refs_13_), channel_id=1, source_target_pairs={{0,8},{1,9},{2,10},{3,11},{4,12},{5,13},{6,14},{7,15},{8,16},{9,17... | collective-permute-start | bytes 663560 | tf_op jit(solution)/shard_map/ppermute | solution.py:36
  41.3 13.4 %collective-permute-start.16 = (bf16[1,6,128,256]{3,2,1,0:T(8,128)(2,1)}, bf16[1,6,128,256]{3,2,1,0:T(8,128)(2,1)}, u32[]{:S(2)}, u32[]{:S(2)}) collective-permute-start(bf16[1,6,128,256]{3,2,1,0:T(8,128)(2,1)} %slice.26), channel_id=1, source_target_pairs={{0,192},{1,193},{2,194},{3,195},{4,196},{5,197},{6,198},{7,199},{8... | collective-permute-start | bytes 1179656 | tf_op jit(solution)/shard_map/ppermute | solution.py:36
  45.4 9.2 %collective-permute-start.17 = (bf16[1,6,128,256]{3,2,1,0:T(8,128)(2,1)}, bf16[1,6,128,256]{3,2,1,0:T(8,128)(2,1)}, u32[]{:S(2)}, u32[]{:S(2)}) collective-permute-start(bf16[1,6,128,256]{3,2,1,0:T(8,128)(2,1)} %slice.27), channel_id=1, source_target_pairs={{0,64},{1,65},{2,66},{3,67},{4,68},{5,69},{6,70},{7,71},{8,72},{9,... | collective-permute-start | bytes 1179656 | tf_op jit(solution)/shard_map/ppermute | solution.py:36
  45.5 5.5 %collective-permute-start.10 = (bf16[27,16,256]{2,1,0:T(8,128)(2,1)}, bf16[27,16,256]{2,1,0:T(8,128)(2,1)S(1)}, u32[]{:S(2)}, u32[]{:S(2)}) collective-permute-start(bf16[27,16,256]{2,1,0:T(8,128)(2,1)} %collective-permute-done.9.refs_7_), channel_id=1, source_target_pairs={{0,56},{1,57},{2,58},{3,59},{4,60},{5,61},{6,62},{7,63},{8,0},{9,1... | collective-permute-start | bytes 663560 | tf_op jit(solution)/shard_map/ppermute | solution.py:36
  46.7 6.2 %collective-permute-start.13 = (bf16[27,16,256]{2,1,0:T(8,128)(2,1)}, bf16[27,16,256]{2,1,0:T(8,128)(2,1)S(1)}, u32[]{:S(2)}, u32[]{:S(2)}) collective-permute-start(bf16[27,16,256]{2,1,0:T(8,128)(2,1)} %collective-permute-done.12.refs_12_), channel_id=1, source_target_pairs={{0,8},{1,9},{2,10},{3,11},{4,12},{5,13},{6,14},{7,15},{8,16},{9,17... | collective-permute-start | bytes 663560 | tf_op jit(solution)/shard_map/ppermute | solution.py:36
  53.0 4.1 %collective-permute-start.18 = (bf16[27,16,128]{2,1,0:T(8,128)(2,1)S(1)}, bf16[27,16,128]{2,1,0:T(8,128)(2,1)S(1)}, u32[]{:S(2)}, u32[]{:S(2)}) collective-permute-start(bf16[27,16,128]{2,1,0:T(8,128)(2,1)S(1)} %slice.22), channel_id=1, source_target_pairs={{0,56},{1,57},{2,58},{3,59},{4,60},{5,61},{6,62},{7,63},{8,0},{9,1... | collective-permute-start | bytes 331784 | tf_op jit(solution)/shard_map/ppermute | solution.py:36
  53.1 5.7 %collective-permute-start.19 = (bf16[27,16,128]{2,1,0:T(8,128)(2,1)S(1)}, bf16[27,16,128]{2,1,0:T(8,128)(2,1)S(1)}, u32[]{:S(2)}, u32[]{:S(2)}) collective-permute-start(bf16[27,16,128]{2,1,0:T(8,128)(2,1)S(1)} %slice.23), channel_id=1, source_target_pairs={{0,8},{1,9},{2,10},{3,11},{4,12},{5,13},{6,14},{7,15},{8,16},{9,17... | collective-permute-start | bytes 331784 | tf_op jit(solution)/shard_map/ppermute | solution.py:36
  69.8 7.9 %collective-permute-start.20 = (bf16[3,2,2,128,128]{4,3,2,1,0:T(8,128)(2,1)S(1)}, bf16[3,2,2,128,128]{4,3,2,1,0:T(8,128)(2,1)S(1)}, u32[]{:S(2)}, u32[]{:S(2)}) collective-permute-start(bf16[3,2,2,128,128]{4,3,2,1,0:T(8,128)(2,1)S(1)} %get-tuple-element.56), channel_id=1, source_target_pairs={{0,1},{1,0},{2,3},{3,2},{4,5},{5,4},{6,7},{7,6},{8,9},{9,8},{10,11... | collective-permute-start | bytes 1179656 | tf_op jit(solution)/shard_map/ppermute | solution.py:36
  77.8 9.8 %collective-permute-start.23 = (bf16[2,2,128,128]{3,2,1,0:T(8,128)(2,1)S(1)}, bf16[2,2,128,128]{3,2,1,0:T(8,128)(2,1)S(1)}, u32[]{:S(2)}, u32[]{:S(2)}) collective-permute-start(bf16[2,2,128,128]{3,2,1,0:T(8,128)(2,1)S(1)} %get-tuple-element.64), channel_id=1, source_target_pairs={{0,192},{1,193},{2,194},{3,195},{4,196},{5,197},{6,198},{7,199},{8... | collective-permute-start | bytes 393224 | tf_op jit(solution)/shard_map/ppermute | solution.py:36
  80.5 7.0 %collective-permute-start.24 = (bf16[2,2,128,128]{3,2,1,0:T(8,128)(2,1)S(1)}, bf16[2,2,128,128]{3,2,1,0:T(8,128)(2,1)S(1)}, u32[]{:S(2)}, u32[]{:S(2)}) collective-permute-start(bf16[2,2,128,128]{3,2,1,0:T(8,128)(2,1)S(1)} %get-tuple-element.65), channel_id=1, source_target_pairs={{0,128},{1,129},{2,130},{3,131},{4,132},{5,133},{6,134},{7,135},{8... | collective-permute-start | bytes 393224 | tf_op jit(solution)/shard_map/ppermute | solution.py:36
  80.5 9.1 %collective-permute-start.25 = (bf16[2,2,128,128]{3,2,1,0:T(8,128)(2,1)S(1)}, bf16[2,2,128,128]{3,2,1,0:T(8,128)(2,1)S(1)}, u32[]{:S(2)}, u32[]{:S(2)}) collective-permute-start(bf16[2,2,128,128]{3,2,1,0:T(8,128)(2,1)S(1)} %get-tuple-element.66), channel_id=1, source_target_pairs={{0,64},{1,65},{2,66},{3,67},{4,68},{5,69},{6,70},{7,71},{8,72},{9,... | collective-permute-start | bytes 393224 | tf_op jit(solution)/shard_map/ppermute | solution.py:36
  (11 other events, 28.9 us)

commit v4 on v3

--- a/solution.py
+++ b/solution.py
@@ -40,6 +40,10 @@
     return lambda y, z, x, c: (y + by, z, x, c)
 
 
+def across_y(bit):
+    return lambda y, z, x, c: (y ^ bit, z, x, c)
+
+
 def along_z(by):
     return lambda y, z, x, c: (y, z + by, x, c)
 
@@ -60,33 +64,8 @@
     return move
 
 
-def pack(info, latent, shard):
-    def body(info, latent, shard, latent_out, shard_out, sems):
-        at = pl.multiple_of((1 - info[4]) * HALF, HALF)
-        copies = [
-            pltpu.make_async_copy(shard.at[:, :, pl.ds(at, HALF)], shard_out, sems.at[0]),
-            pltpu.make_async_copy(latent.at[:, :, :, pl.ds(at, HALF)], latent_out, sems.at[1]),
-        ]
-        for copy in copies:
-            copy.start()
-        for copy in copies:
-            copy.wait()
-
-    return pl.pallas_call(
-        body,
-        out_shape=[
-            jax.ShapeDtypeStruct(latent.shape[:3] + (HALF,), latent.dtype),
-            jax.ShapeDtypeStruct(shard.shape[:2] + (HALF,), shard.dtype),
-        ],
-        in_specs=[SMEM, HBM, HBM],
-        out_specs=[HBM, HBM],
-        scratch_shapes=[pltpu.SemaphoreType.DMA((2,))],
-        compiler_params=LIMIT,
-    )(info, latent, shard)
-
-
 def unpack(info, latent, theirs):
-    def body(info, latent, theirs, rows, last, first, stat, sems):
+    def body(info, latent, theirs, rows, last, first, sems):
         core = info[4]
         at = pl.multiple_of(core * HALF, HALF)
         copies = [
@@ -101,6 +80,20 @@
             copy.wait()
         last[...] = rows[:, ROWS - 1 :]
         first[...] = rows[:, :1]
+
+    edge = jax.ShapeDtypeStruct((2, 1, WIDTH, HALF), latent.dtype)
+    return pl.pallas_call(
+        body,
+        out_shape=[jax.ShapeDtypeStruct((2, ROWS, WIDTH, HALF), latent.dtype), edge, edge],
+        in_specs=[SMEM, HBM, HBM],
+        out_specs=[VMEM] * 3,
+        scratch_shapes=[pltpu.SemaphoreType.DMA((2,))],
+        compiler_params=LIMIT,
+    )(info, latent, theirs)
+
+
+def moments(rows):
+    def body(rows, stat):
         group = [lax.broadcasted_iota(jnp.int32, (HALF, HALF), i) // 16 for i in range(2)]
         same = (group[0] == group[1]).astype(jnp.float32)
 
@@ -125,18 +118,13 @@
         stat[0:1] = mean
         stat[1:2] = squares
 
-    edge = jax.ShapeDtypeStruct((2, 1, WIDTH, HALF), latent.dtype)
-    return pl.pallas_call(
-        body,
-        out_shape=[
-            jax.ShapeDtypeStruct((2, ROWS, WIDTH, HALF), latent.dtype), edge, edge,
-            jax.ShapeDtypeStruct((2, HALF), jnp.float32),
-        ],
-        in_specs=[SMEM, HBM, HBM],
-        out_specs=[VMEM] * 4,
-        scratch_shapes=[pltpu.SemaphoreType.DMA((2,))],
-        compiler_params=LIMIT,
-    )(info, latent, theirs)
+    return pl.pallas_call(
+        body,
+        out_shape=jax.ShapeDtypeStruct((2, HALF), jnp.float32),
+        in_specs=[VMEM],
+        out_specs=VMEM,
+        compiler_params=LIMIT,
+    )(rows)
 
 
 def border(above, rows, below):
@@ -167,7 +155,10 @@
     def body(info, stats, gain, shift, *refs):
         sources, results = refs[: len(pieces)], refs[len(pieces) :]
         for (_, ahead), source, result in zip(pieces, sources, results):
-            means, squares = stats[:, 2 * ahead], stats[:, 2 * ahead + 1]
+            even = lax.rem(info[0], 2) == 0
+            behind = (NY - ahead) % NY
+            means = jnp.where(even, stats[:, 2 * ahead], stats[:, 2 * behind])
+            squares = jnp.where(even, stats[:, 2 * ahead + 1], stats[:, 2 * behind + 1])
             mean = jnp.sum(means, axis=0, keepdims=True) / CHIPS
             deviation = means - mean
             variance = jnp.sum(squares / CELLS + deviation * deviation, axis=0, keepdims=True) / CHIPS
@@ -319,16 +310,16 @@
     channels = latent.shape[3]
     turn = 4 * ((chip + CHIPS - 1) % CHIPS)
     info = jnp.stack([time_index, turn, chip == 0, chip == CHIPS - 1, core]).astype(jnp.int32)
-    half = lambda a: lax.dynamic_slice_in_dim(a, core * HALF, HALF, axis=a.ndim - 1)
+    half = lambda a, which: lax.dynamic_slice_in_dim(a, which * HALF, HALF, axis=a.ndim - 1)
 
     shard = kernel.transpose(1, 2, 3, 0, 4).reshape(TAPS, 2, channels)
-    latent_give, shard_give = pack(info, latent, shard)
-    other = send(shard_give, sibling)
-    theirs = send(latent_give, sibling)
-
-    near = half(shard)
+    other = send(half(shard, 1 - core), sibling)
+    theirs = send(half(latent, 1 - core), sibling)
+
+    near = half(shard, core)
     pair = jnp.where(core == 0, jnp.concatenate([near, other], 1), jnp.concatenate([other, near], 1))
-    rows, last, first, stat = unpack(info, latent, theirs)
+    rows, last, first = unpack(info, latent, theirs)
+    stat = moments(rows)
     flat = pair.reshape(TAPS * 4, HALF)
     edge = 2 * WIDTH
     from_above = send(jnp.concatenate([last.reshape(edge, HALF), flat]), strip(1))
@@ -339,8 +330,8 @@
     )
     own = border(from_above, rows, from_below)
 
-    spans = [stat] + [send(stat, along_y(-k)) for k in range(1, NY)]
-    spans = jnp.concatenate(spans, 0)
+    spans = jnp.concatenate([stat, send(stat, across_y(1))], 0)
+    spans = jnp.concatenate([spans, send(spans, across_y(2))], 0)
     spans, block, own = lax.optimization_barrier((spans, block, own))
     stats = lax.all_to_all(jnp.broadcast_to(spans[None], (CHIPS, 2 * NY, HALF)), ("z", "x"), 0, 0)
 
@@ -353,7 +344,7 @@
     across_a = send(after[:1], along_y(-1))
     across_b = send(before[1:], along_y(1))
 
-    gain, shift = half(norm_gain[None]), half(norm_shift[None])
+    gain, shift = half(norm_gain[None], core), half(norm_shift[None], core)
     act_own, act_after, act_before = activate(info, stats, gain, shift, [(own, 0), (after, 1), (before, 3)])
     third, minus_third, act_own, act_after, act_before = lax.optimization_barrier(
         (ring[3], ring[-3], act_own, act_after, act_before)

time: 92.6 us -> 91.7 us (level); the launches traced: 91.2 us -> 91.4 us
    dynamic_slice x1 -> x2, local copies, waits for them, and re-layouts: 0.02 us -> 1.84 us  [per_device(): lax.dynamic_slice_in_dim(a, which * HALF, HALF, axis=a.ndim - 1)]
    unnamed x16 -> x12, local copies, waits for them, and re-layouts: 2.47 us -> 0.7 us
    ppermute x26 -> x25, starting transfers between devices: 39.6 us -> 40.3 us  [send(): return lax.ppermute(array, AXES, pairs)]
    ppermute x26 -> x25, waiting for transfers between devices: 16 us -> 16.5 us  [send(): return lax.ppermute(array, AXES, pairs)]
  transfers between devices with their start and end apart: 27 -> 26, of which waited for: 13 -> 11; matrix products, arithmetic and copies ran while one was open for 3% -> 4% of each run, Pallas kernels for 10% -> 10%
where the time goes in v4:
time: 91.7 us; the launch traced here: 91.4 us
  starting transfers between devices  46.4 us (51%)
  Pallas kernels  22.8 us (25%)
  waiting for transfers between devices  16.5 us (18%)
  local copies, waits for them, and re-layouts  5.17 us (6%)
    ppermute x25, starting transfers between devices, send(): return lax.ppermute(array, AXES, pairs)  40.3 us
    ppermute x25, waiting for transfers between devices, send(): return lax.ppermute(array, AXES, pairs)  16.5 us
    pallas_call x2, Pallas kernels, convolve(): pl.pallas_call(body, out_shape=[jax.ShapeDtypeStruct(shape, jnp.float32)]...  14.4 us
    all_to_all x1, starting transfers between devices, per_device(): lax.all_to_all(jnp.broadcast_to(spans[None], (CHIPS, 2 * NY, HALF)), ('z'...  6.08 us
    pallas_call x2, Pallas kernels, activate(): pl.pallas_call(body, out_shape=[jax.ShapeDtypeStruct(a.shape, a.dtype) fo...  4.96 us
    dynamic_slice x2, local copies, waits for them, and re-layouts, per_device(): lax.dynamic_slice_in_dim(a, which * HALF, HALF, axis=a.ndim - 1)  1.84 us
  transfers between devices with their start and end apart: 26, of which 11 were waited for; matrix products, arithmetic and copies ran while one was open for 4% of the time, Pallas kernels for 10%

profile of v4, /device:TPU:1, one launch (start us, length us, event | category | flops | bytes accessed | tf_op | source)
XLA Modules:
  0.0 91.4 jit_solution(10658405024279746765)
XLA Ops:
  1.0 3.3 %collective-permute-start = (bf16[2,2,128,256]{3,2,1,0:T(8,128)(2,1)S(1)}, bf16[2,2,128,256]{3,2,1,0:T(8,128)(2,1)S(1)}, u32[]{:S(2)}, u32[]{:S(2)}) collective-permute-start(bf16[2,2,128,256]{3,2,1,0:T(8,128)(2,1)S(1)} %constant_dynamic-slice_fusion.2), channel_id=1, source_target_pairs={{0,1},{1,0},{2,3},{3,2},{4,5},{5,4},{6,7},{7,6},{8,9},{9,8},{10,11... | collective-permute-start | bytes 786440 | tf_op jit(solution)/shard_map/ppermute | solution.py:36
  9.0 6.6 %collective-permute-start.5 = (bf16[364,256]{1,0:T(8,128)(2,1)S(1)}, bf16[364,256]{1,0:T(8,128)(2,1)S(1)}, u32[]{:S(2)}, u32[]{:S(2)}) collective-permute-start(bf16[364,256]{1,0:T(8,128)(2,1)S(1)} %get-tuple-element.62), channel_id=1, source_target_pairs={{0,62},{1,63},{2,0},{3,1},{4,2},{5,3},{6,4},{7,5},{8,6},{9,7},{10,... | collective-permute-start | bytes 559112 | tf_op jit(solution)/shard_map/ppermute | solution.py:36
  15.7 2.7 %collective-permute-start.2 = (f32[4,256]{1,0:T(4,128)S(1)}, f32[4,256]{1,0:T(4,128)S(1)}, u32[]{:S(2)}, u32[]{:S(2)}) collective-permute-start(f32[4,256]{1,0:T(4,128)S(1)} %pad_maximum_fusion.4), channel_id=1, source_target_pairs={{0,128},{1,129},{2,130},{3,131},{4,132},{5,133},{6,134},{7,135},{8... | collective-permute-start | bytes 12296 | tf_op jit(solution)/shard_map/ppermute | solution.py:36
  18.4 1.6 %collective-permute-start.6 = (bf16[27,4,256]{2,1,0:T(4,128)(2,1)S(1)}, bf16[27,4,256]{2,1,0:T(4,128)(2,1)S(1)}, u32[]{:S(2)}, u32[]{:S(2)}) collective-permute-start(bf16[27,4,256]{2,1,0:T(4,128)(2,1)S(1)} %maximum_select_fusion), channel_id=1, source_target_pairs={{0,60},{1,61},{2,62},{3,63},{4,0},{5,1},{6,2},{7,3},{8,4},{9,5},{1... | collective-permute-start | bytes 165896 | tf_op jit(solution)/shard_map/ppermute | solution.py:36
  20.8 2.1 %collective-permute-done.6 = bf16[27,4,256]{2,1,0:T(4,128)(2,1)S(1)} collective-permute-done((bf16[27,4,256]{2,1,0:T(4,128)(2,1)S(1)}, bf16[27,4,256]{2,1,0:T(4,128)(2,1)S(1)}, u32[]{:S(2)}, u32[]{:S(2)}) %collective-permute-start.6) | collective-permute-done | bytes 55328 | tf_op jit(solution)/shard_map/ppermute | solution.py:36
  24.6 2.7 %collective-permute-start.7 = (bf16[27,16,256]{2,1,0:T(8,128)(2,1)S(1)}, bf16[27,16,256]{2,1,0:T(8,128)(2,1)S(1)}, u32[]{:S(2)}, u32[]{:S(2)}) collective-permute-start(bf16[27,16,256]{2,1,0:T(8,128)(2,1)S(1)} %pad_maximum_fusion.2.refs_5_), channel_id=1, source_target_pairs={{0,56},{1,57},{2,58},{3,59},{4,60},{5,61},{6,62},{7,63},{8,0},{9,1... | collective-permute-start | bytes 663560 | tf_op jit(solution)/shard_map/ppermute | solution.py:36
  28.0 6.1 %all-to-all-start = ((f32[32,8,256]{2,1,0:T(8,128)}), f32[32,8,256]{2,1,0:T(8,128)S(1)}, u32[]{:S(2)}, u32[]{:S(2)}) async-start(f32[32,8,256]{2,1,0:T(8,128)} %broadcast_in_dim.5), calls=%async_computation | async-start | bytes 524288 | tf_op jit(solution)/shard_map/all_to_all | solution.py:336
  34.1 1.3 %collective-permute-start.11 = (bf16[27,16,256]{2,1,0:T(8,128)(2,1)S(1)}, bf16[27,16,256]{2,1,0:T(8,128)(2,1)}, u32[]{:S(2)}, u32[]{:S(2)}) collective-permute-start(bf16[27,16,256]{2,1,0:T(8,128)(2,1)S(1)} %collective-permute-done.10.refs_13_), channel_id=1, source_target_pairs={{0,8},{1,9},{2,10},{3,11},{4,12},{5,13},{6,14},{7,15},{8,16},{9,17... | collective-permute-start | bytes 663560 | tf_op jit(solution)/shard_map/ppermute | solution.py:36
  35.4 1.4 %collective-permute-start.8 = (bf16[27,16,256]{2,1,0:T(8,128)(2,1)S(1)}, bf16[27,16,256]{2,1,0:T(8,128)(2,1)}, u32[]{:S(2)}, u32[]{:S(2)}) collective-permute-start(bf16[27,16,256]{2,1,0:T(8,128)(2,1)S(1)} %collective-permute-done.7.refs_6_), channel_id=1, source_target_pairs={{0,56},{1,57},{2,58},{3,59},{4,60},{5,61},{6,62},{7,63},{8,0},{9,1... | collective-permute-start | bytes 663560 | tf_op jit(solution)/shard_map/ppermute | solution.py:36
  36.8 3.2 %collective-permute-done.13.refs_1_ = bf16[2,6,128,256]{3,2,1,0:T(8,128)(2,1)S(1)} collective-permute-done((bf16[2,6,128,256]{3,2,1,0:T(8,128)(2,1)S(1)}, bf16[2,6,128,256]{3,2,1,0:T(8,128)(2,1)S(1)}, u32[]{:S(2)}, u32[]{:S(2)}) %collective-permute-start.13) | collective-permute-done | bytes 786464 | tf_op jit(solution)/shard_map/ppermute | solution.py:36
  40.8 1.7 %collective-permute-start.15 = (bf16[1,6,128,256]{3,2,1,0:T(8,128)(2,1)}, bf16[1,6,128,256]{3,2,1,0:T(8,128)(2,1)}, u32[]{:S(2)}, u32[]{:S(2)}) collective-permute-start(bf16[1,6,128,256]{3,2,1,0:T(8,128)(2,1)} %slice.26), channel_id=1, source_target_pairs={{0,192},{1,193},{2,194},{3,195},{4,196},{5,197},{6,198},{7,199},{8... | collective-permute-start | bytes 1179656 | tf_op jit(solution)/shard_map/ppermute | solution.py:36
  43.3 1.9 %collective-permute-done.11.refs_12_ = bf16[27,16,256]{2,1,0:T(8,128)(2,1)} collective-permute-done((bf16[27,16,256]{2,1,0:T(8,128)(2,1)S(1)}, bf16[27,16,256]{2,1,0:T(8,128)(2,1)}, u32[]{:S(2)}, u32[]{:S(2)}) %collective-permute-start.11) | collective-permute-done | bytes 221216 | tf_op jit(solution)/shard_map/ppermute | solution.py:36
  45.2 2.7 %collective-permute-start.9 = (bf16[27,16,256]{2,1,0:T(8,128)(2,1)}, bf16[27,16,256]{2,1,0:T(8,128)(2,1)S(1)}, u32[]{:S(2)}, u32[]{:S(2)}) collective-permute-start(bf16[27,16,256]{2,1,0:T(8,128)(2,1)} %collective-permute-done.8.refs_7_), channel_id=1, source_target_pairs={{0,56},{1,57},{2,58},{3,59},{4,60},{5,61},{6,62},{7,63},{8,0},{9,1... | collective-permute-start | bytes 663560 | tf_op jit(solution)/shard_map/ppermute | solution.py:36
  48.0 3.0 %shard_map.58 = (bf16[2,6,128,256]{3,2,1,0:T(8,128)(2,1)S(1)}, bf16[2,6,128,256]{3,2,1,0:T(8,128)(2,1)S(1)}, bf16[2,6,128,256]{3,2,1,0:T(8,128)(2,1)S(1)}) custom-call(s32[5]{0:T(128)S(1)} %stack.31.info, f32[32,8,256]{2,1,0:T(8,128)S(1)} %all-to-all-done.stats, f32[1,256]{1,0:T(1,128)S(1)} %bitcast.15, f32[1,256]{1,0:T(1,128)S(1)} %bitcast.17, ...), custom_call_target="tpu_custom_call" | custom-call | flops 18874368 | bytes 4718592 | tf_op jit(solution)/shard_map/pallas_call | solution.py:182
  51.8 2.8 %collective-permute-start.17 = (bf16[27,16,128]{2,1,0:T(8,128)(2,1)S(1)}, bf16[27,16,128]{2,1,0:T(8,128)(2,1)S(1)}, u32[]{:S(2)}, u32[]{:S(2)}) collective-permute-start(bf16[27,16,128]{2,1,0:T(8,128)(2,1)S(1)} %slice.22), channel_id=1, source_target_pairs={{0,56},{1,57},{2,58},{3,59},{4,60},{5,61},{6,62},{7,63},{8,0},{9,1... | collective-permute-start | bytes 331784 | tf_op jit(solution)/shard_map/ppermute | solution.py:36
  54.7 2.0 %shard_map.59 = (bf16[1,6,128,256]{3,2,1,0:T(8,128)(2,1)S(1)}, bf16[1,6,128,256]{3,2,1,0:T(8,128)(2,1)S(1)}) custom-call(s32[5]{0:T(128)S(1)} %stack.31.info, f32[32,8,256]{2,1,0:T(8,128)S(1)} %all-to-all-done.stats, f32[1,256]{1,0:T(1,128)S(1)} %bitcast.16, f32[1,256]{1,0:T(1,128)S(1)} %bitcast.18, ...), custom_call_target="tpu_custom_call" | custom-call | flops 6291456 | bytes 1572864 | tf_op jit(solution)/shard_map/pallas_call | solution.py:182
  56.7 2.8 %collective-permute-done.18.refs_10_ = bf16[27,16,128]{2,1,0:T(8,128)(2,1)S(1)} collective-permute-done((bf16[27,16,128]{2,1,0:T(8,128)(2,1)S(1)}, bf16[27,16,128]{2,1,0:T(8,128)(2,1)S(1)}, u32[]{:S(2)}, u32[]{:S(2)}) %collective-permute-start.18) | collective-permute-done | bytes 110624 | tf_op jit(solution)/shard_map/ppermute | solution.py:36
  60.1 10.3 %shard_map.60 = (f32[3,2,2,128,128]{4,3,2,1,0:T(8,128)S(1)}, bf16[3,2,2,128,128]{4,3,2,1,0:T(8,128)(2,1)S(1)}) custom-call(s32[5]{0:T(128)S(1)} %stack.31.info, f32[1,512]{1,0:T(1,128)S(1)} %bitcast.19, bf16[2,6,128,256]{3,2,1,0:T(8,128)(2,1)S(1)} %get-tuple-element.42.refs_0_, bf16[2,6,128,256]{3,2,1,0:T(8,128)(2,1)S(1)} %get-tuple-element.43.refs_1_, ...), custom_call_target="tpu_custom_call" | custom-call | flops 5435817984 | bytes 5242880 | tf_op jit(solution)/shard_map/pallas_call | solution.py:260
  70.5 6.1 %collective-permute-start.19 = (bf16[3,2,2,128,128]{4,3,2,1,0:T(8,128)(2,1)S(1)}, bf16[3,2,2,128,128]{4,3,2,1,0:T(8,128)(2,1)S(1)}, u32[]{:S(2)}, u32[]{:S(2)}) collective-permute-start(bf16[3,2,2,128,128]{4,3,2,1,0:T(8,128)(2,1)S(1)} %get-tuple-element.50), channel_id=1, source_target_pairs={{0,1},{1,0},{2,3},{3,2},{4,5},{5,4},{6,7},{7,6},{8,9},{9,8},{10,11... | collective-permute-start | bytes 1179656 | tf_op jit(solution)/shard_map/ppermute | solution.py:36
  76.6 1.3 %collective-permute-done.19.taken = bf16[3,2,2,128,128]{4,3,2,1,0:T(8,128)(2,1)S(1)} collective-permute-done((bf16[3,2,2,128,128]{4,3,2,1,0:T(8,128)(2,1)S(1)}, bf16[3,2,2,128,128]{4,3,2,1,0:T(8,128)(2,1)S(1)}, u32[]{:S(2)}, u32[]{:S(2)}) %collective-permute-start.19) | collective-permute-done | bytes 393248 | tf_op jit(solution)/shard_map/ppermute | solution.py:36
  78.0 2.8 %collective-permute-start.22 = (bf16[2,2,128,128]{3,2,1,0:T(8,128)(2,1)S(1)}, bf16[2,2,128,128]{3,2,1,0:T(8,128)(2,1)S(1)}, u32[]{:S(2)}, u32[]{:S(2)}) collective-permute-start(bf16[2,2,128,128]{3,2,1,0:T(8,128)(2,1)S(1)} %get-tuple-element.58), channel_id=1, source_target_pairs={{0,192},{1,193},{2,194},{3,195},{4,196},{5,197},{6,198},{7,199},{8... | collective-permute-start | bytes 393224 | tf_op jit(solution)/shard_map/ppermute | solution.py:36
  81.5 4.1 %shard_map.62 = (f32[1,2,2,128,128]{4,3,2,1,0:T(8,128)S(1)}, bf16[2,128,128]{2,1,0:T(8,128)(2,1)S(1)}, bf16[2,128,128]{2,1,0:T(8,128)(2,1)S(1)}) custom-call(s32[5]{0:T(128)S(1)} %stack.31.info, f32[1,512]{1,0:T(1,128)S(1)} %bitcast.20, bf16[2,6,128,256]{3,2,1,0:T(8,128)(2,1)S(1)} %get-tuple-element.42.refs_0_, ...), custom_call_target="tpu_custom_call" | custom-call | flops 1811939328 | bytes 5242880 | tf_op jit(solution)/shard_map/pallas_call | solution.py:260
  88.0 2.0 %collective-permute-done.24.refs_2_ = bf16[2,2,128,128]{3,2,1,0:T(8,128)(2,1)S(1)} collective-permute-done((bf16[2,2,128,128]{3,2,1,0:T(8,128)(2,1)S(1)}, bf16[2,2,128,128]{3,2,1,0:T(8,128)(2,1)S(1)}, u32[]{:S(2)}, u32[]{:S(2)}) %collective-permute-start.24) | collective-permute-done | bytes 131104 | tf_op jit(solution)/shard_map/ppermute | solution.py:36
  89.9 1.5 %shard_map.63 = bf16[2,2,128,512]{3,2,1,0:T(8,128)(2,1)} custom-call(s32[5]{0:T(128)S(1)} %stack.31.info, f32[1,2,2,128,128]{4,3,2,1,0:T(8,128)S(1)} %get-tuple-element.55.keep, bf16[2,128,128]{2,1,0:T(8,128)(2,1)S(1)} %collective-permute-done.20.first, bf16[2,128,128]{2,1,0:T(8,128)(2,1)S(1)} %collective-permute-done.21.second, ...), custom_call_target="tpu_custom_call" | custom-call | tf_op jit(solution)/shard_map/pallas_call | solution.py:298
  (69 shorter events, 15.2 us)
Async XLA Ops:
  1.0 5.6 %collective-permute-start = (bf16[2,2,128,256]{3,2,1,0:T(8,128)(2,1)S(1)}, bf16[2,2,128,256]{3,2,1,0:T(8,128)(2,1)S(1)}, u32[]{:S(2)}, u32[]{:S(2)}) collective-permute-start(bf16[2,2,128,256]{3,2,1,0:T(8,128)(2,1)S(1)} %constant_dynamic-slice_fusion.2), channel_id=1, source_target_pairs={{0,1},{1,0},{2,3},{3,2},{4,5},{5,4},{6,7},{7,6},{8,9},{9,8},{10,11... | collective-permute-start | bytes 786440 | tf_op jit(solution)/shard_map/ppermute | solution.py:36
  8.1 7.5 %collective-permute-start.1 = (f32[2,256]{1,0:T(2,128)S(1)}, f32[2,256]{1,0:T(2,128)S(1)}, u32[]{:S(2)}, u32[]{:S(2)}) collective-permute-start(f32[2,256]{1,0:T(2,128)S(1)} %shard_map.56), channel_id=1, source_target_pairs={{0,64},{1,65},{2,66},{3,67},{4,68},{5,69},{6,70},{7,71},{8,72},{9,... | collective-permute-start | bytes 6152 | tf_op jit(solution)/shard_map/ppermute | solution.py:36
  8.2 12.1 %collective-permute-start.4 = (bf16[364,256]{1,0:T(8,128)(2,1)S(1)}, bf16[364,256]{1,0:T(8,128)(2,1)S(1)}, u32[]{:S(2)}, u32[]{:S(2)}) collective-permute-start(bf16[364,256]{1,0:T(8,128)(2,1)S(1)} %get-tuple-element.61), channel_id=1, source_target_pairs={{0,2},{1,3},{2,4},{3,5},{4,6},{5,7},{6,8},{7,9},{8,10},{9,11},{10,... | collective-permute-start | bytes 559112 | tf_op jit(solution)/shard_map/ppermute | solution.py:36
  9.0 11.3 %collective-permute-start.5 = (bf16[364,256]{1,0:T(8,128)(2,1)S(1)}, bf16[364,256]{1,0:T(8,128)(2,1)S(1)}, u32[]{:S(2)}, u32[]{:S(2)}) collective-permute-start(bf16[364,256]{1,0:T(8,128)(2,1)S(1)} %get-tuple-element.62), channel_id=1, source_target_pairs={{0,62},{1,63},{2,0},{3,1},{4,2},{5,3},{6,4},{7,5},{8,6},{9,7},{10,... | collective-permute-start | bytes 559112 | tf_op jit(solution)/shard_map/ppermute | solution.py:36
  15.7 4.4 %collective-permute-start.2 = (f32[4,256]{1,0:T(4,128)S(1)}, f32[4,256]{1,0:T(4,128)S(1)}, u32[]{:S(2)}, u32[]{:S(2)}) collective-permute-start(f32[4,256]{1,0:T(4,128)S(1)} %pad_maximum_fusion.4), channel_id=1, source_target_pairs={{0,128},{1,129},{2,130},{3,131},{4,132},{5,133},{6,134},{7,135},{8... | collective-permute-start | bytes 12296 | tf_op jit(solution)/shard_map/ppermute | solution.py:36
  18.4 4.5 %collective-permute-start.6 = (bf16[27,4,256]{2,1,0:T(4,128)(2,1)S(1)}, bf16[27,4,256]{2,1,0:T(4,128)(2,1)S(1)}, u32[]{:S(2)}, u32[]{:S(2)}) collective-permute-start(bf16[27,4,256]{2,1,0:T(4,128)(2,1)S(1)} %maximum_select_fusion), channel_id=1, source_target_pairs={{0,60},{1,61},{2,62},{3,63},{4,0},{5,1},{6,2},{7,3},{8,4},{9,5},{1... | collective-permute-start | bytes 165896 | tf_op jit(solution)/shard_map/ppermute | solution.py:36
  23.0 17.0 %collective-permute-start.13 = (bf16[2,6,128,256]{3,2,1,0:T(8,128)(2,1)S(1)}, bf16[2,6,128,256]{3,2,1,0:T(8,128)(2,1)S(1)}, u32[]{:S(2)}, u32[]{:S(2)}) collective-permute-start(bf16[2,6,128,256]{3,2,1,0:T(8,128)(2,1)S(1)} %shard_map.57.refs_0_), channel_id=1, source_target_pairs={{0,192},{1,193},{2,194},{3,195},{4,196},{5,197},{6,198},{7,199},{8... | collective-permute-start | bytes 2359304 | tf_op jit(solution)/shard_map/ppermute | solution.py:36
  23.3 19.1 %collective-permute-start.14 = (bf16[2,6,128,256]{3,2,1,0:T(8,128)(2,1)S(1)}, bf16[2,6,128,256]{3,2,1,0:T(8,128)(2,1)S(1)}, u32[]{:S(2)}, u32[]{:S(2)}) collective-permute-start(bf16[2,6,128,256]{3,2,1,0:T(8,128)(2,1)S(1)} %shard_map.57.refs_0_), channel_id=1, source_target_pairs={{0,64},{1,65},{2,66},{3,67},{4,68},{5,69},{6,70},{7,71},{8,72},{9,... | collective-permute-start | bytes 2359304 | tf_op jit(solution)/shard_map/ppermute | solution.py:36
  24.6 9.5 %collective-permute-start.10 = (bf16[27,16,256]{2,1,0:T(8,128)(2,1)S(1)}, bf16[27,16,256]{2,1,0:T(8,128)(2,1)S(1)}, u32[]{:S(2)}, u32[]{:S(2)}) collective-permute-start(bf16[27,16,256]{2,1,0:T(8,128)(2,1)S(1)} %pad_maximum_fusion.2.refs_5_), channel_id=1, source_target_pairs={{0,8},{1,9},{2,10},{3,11},{4,12},{5,13},{6,14},{7,15},{8,16},{9,17... | collective-permute-start | bytes 663560 | tf_op jit(solution)/shard_map/ppermute | solution.py:36
  24.6 10.8 %collective-permute-start.7 = (bf16[27,16,256]{2,1,0:T(8,128)(2,1)S(1)}, bf16[27,16,256]{2,1,0:T(8,128)(2,1)S(1)}, u32[]{:S(2)}, u32[]{:S(2)}) collective-permute-start(bf16[27,16,256]{2,1,0:T(8,128)(2,1)S(1)} %pad_maximum_fusion.2.refs_5_), channel_id=1, source_target_pairs={{0,56},{1,57},{2,58},{3,59},{4,60},{5,61},{6,62},{7,63},{8,0},{9,1... | collective-permute-start | bytes 663560 | tf_op jit(solution)/shard_map/ppermute | solution.py:36
  28.0 20.0 %all-to-all-start = ((f32[32,8,256]{2,1,0:T(8,128)}), f32[32,8,256]{2,1,0:T(8,128)S(1)}, u32[]{:S(2)}, u32[]{:S(2)}) async-start(f32[32,8,256]{2,1,0:T(8,128)} %broadcast_in_dim.5), calls=%async_computation | async-start | bytes 524288 | tf_op jit(solution)/shard_map/all_to_all | solution.py:336
  34.1 11.1 %collective-permute-start.11 = (bf16[27,16,256]{2,1,0:T(8,128)(2,1)S(1)}, bf16[27,16,256]{2,1,0:T(8,128)(2,1)}, u32[]{:S(2)}, u32[]{:S(2)}) collective-permute-start(bf16[27,16,256]{2,1,0:T(8,128)(2,1)S(1)} %collective-permute-done.10.refs_13_), channel_id=1, source_target_pairs={{0,8},{1,9},{2,10},{3,11},{4,12},{5,13},{6,14},{7,15},{8,16},{9,17... | collective-permute-start | bytes 663560 | tf_op jit(solution)/shard_map/ppermute | solution.py:36
  35.4 9.8 %collective-permute-start.8 = (bf16[27,16,256]{2,1,0:T(8,128)(2,1)S(1)}, bf16[27,16,256]{2,1,0:T(8,128)(2,1)}, u32[]{:S(2)}, u32[]{:S(2)}) collective-permute-start(bf16[27,16,256]{2,1,0:T(8,128)(2,1)S(1)} %collective-permute-done.7.refs_6_), channel_id=1, source_target_pairs={{0,56},{1,57},{2,58},{3,59},{4,60},{5,61},{6,62},{7,63},{8,0},{9,1... | collective-permute-start | bytes 663560 | tf_op jit(solution)/shard_map/ppermute | solution.py:36
  40.8 13.9 %collective-permute-start.15 = (bf16[1,6,128,256]{3,2,1,0:T(8,128)(2,1)}, bf16[1,6,128,256]{3,2,1,0:T(8,128)(2,1)}, u32[]{:S(2)}, u32[]{:S(2)}) collective-permute-start(bf16[1,6,128,256]{3,2,1,0:T(8,128)(2,1)} %slice.26), channel_id=1, source_target_pairs={{0,192},{1,193},{2,194},{3,195},{4,196},{5,197},{6,198},{7,199},{8... | collective-permute-start | bytes 1179656 | tf_op jit(solution)/shard_map/ppermute | solution.py:36
  43.3 11.4 %collective-permute-start.16 = (bf16[1,6,128,256]{3,2,1,0:T(8,128)(2,1)}, bf16[1,6,128,256]{3,2,1,0:T(8,128)(2,1)}, u32[]{:S(2)}, u32[]{:S(2)}) collective-permute-start(bf16[1,6,128,256]{3,2,1,0:T(8,128)(2,1)} %slice.27), channel_id=1, source_target_pairs={{0,64},{1,65},{2,66},{3,67},{4,68},{5,69},{6,70},{7,71},{8,72},{9,... | collective-permute-start | bytes 1179656 | tf_op jit(solution)/shard_map/ppermute | solution.py:36
  45.2 6.6 %collective-permute-start.12 = (bf16[27,16,256]{2,1,0:T(8,128)(2,1)}, bf16[27,16,256]{2,1,0:T(8,128)(2,1)S(1)}, u32[]{:S(2)}, u32[]{:S(2)}) collective-permute-start(bf16[27,16,256]{2,1,0:T(8,128)(2,1)} %collective-permute-done.11.refs_12_), channel_id=1, source_target_pairs={{0,8},{1,9},{2,10},{3,11},{4,12},{5,13},{6,14},{7,15},{8,16},{9,17... | collective-permute-start | bytes 663560 | tf_op jit(solution)/shard_map/ppermute | solution.py:36
  45.2 6.6 %collective-permute-start.9 = (bf16[27,16,256]{2,1,0:T(8,128)(2,1)}, bf16[27,16,256]{2,1,0:T(8,128)(2,1)S(1)}, u32[]{:S(2)}, u32[]{:S(2)}) collective-permute-start(bf16[27,16,256]{2,1,0:T(8,128)(2,1)} %collective-permute-done.8.refs_7_), channel_id=1, source_target_pairs={{0,56},{1,57},{2,58},{3,59},{4,60},{5,61},{6,62},{7,63},{8,0},{9,1... | collective-permute-start | bytes 663560 | tf_op jit(solution)/shard_map/ppermute | solution.py:36
  51.8 4.9 %collective-permute-start.17 = (bf16[27,16,128]{2,1,0:T(8,128)(2,1)S(1)}, bf16[27,16,128]{2,1,0:T(8,128)(2,1)S(1)}, u32[]{:S(2)}, u32[]{:S(2)}) collective-permute-start(bf16[27,16,128]{2,1,0:T(8,128)(2,1)S(1)} %slice.22), channel_id=1, source_target_pairs={{0,56},{1,57},{2,58},{3,59},{4,60},{5,61},{6,62},{7,63},{8,0},{9,1... | collective-permute-start | bytes 331784 | tf_op jit(solution)/shard_map/ppermute | solution.py:36
  54.6 4.9 %collective-permute-start.18 = (bf16[27,16,128]{2,1,0:T(8,128)(2,1)S(1)}, bf16[27,16,128]{2,1,0:T(8,128)(2,1)S(1)}, u32[]{:S(2)}, u32[]{:S(2)}) collective-permute-start(bf16[27,16,128]{2,1,0:T(8,128)(2,1)S(1)} %slice.23), channel_id=1, source_target_pairs={{0,8},{1,9},{2,10},{3,11},{4,12},{5,13},{6,14},{7,15},{8,16},{9,17... | collective-permute-start | bytes 331784 | tf_op jit(solution)/shard_map/ppermute | solution.py:36
  70.5 7.5 %collective-permute-start.19 = (bf16[3,2,2,128,128]{4,3,2,1,0:T(8,128)(2,1)S(1)}, bf16[3,2,2,128,128]{4,3,2,1,0:T(8,128)(2,1)S(1)}, u32[]{:S(2)}, u32[]{:S(2)}) collective-permute-start(bf16[3,2,2,128,128]{4,3,2,1,0:T(8,128)(2,1)S(1)} %get-tuple-element.50), channel_id=1, source_target_pairs={{0,1},{1,0},{2,3},{3,2},{4,5},{5,4},{6,7},{7,6},{8,9},{9,8},{10,11... | collective-permute-start | bytes 1179656 | tf_op jit(solution)/shard_map/ppermute | solution.py:36
  78.0 9.9 %collective-permute-start.22 = (bf16[2,2,128,128]{3,2,1,0:T(8,128)(2,1)S(1)}, bf16[2,2,128,128]{3,2,1,0:T(8,128)(2,1)S(1)}, u32[]{:S(2)}, u32[]{:S(2)}) collective-permute-start(bf16[2,2,128,128]{3,2,1,0:T(8,128)(2,1)S(1)} %get-tuple-element.58), channel_id=1, source_target_pairs={{0,192},{1,193},{2,194},{3,195},{4,196},{5,197},{6,198},{7,199},{8... | collective-permute-start | bytes 393224 | tf_op jit(solution)/shard_map/ppermute | solution.py:36
  80.8 7.1 %collective-permute-start.23 = (bf16[2,2,128,128]{3,2,1,0:T(8,128)(2,1)S(1)}, bf16[2,2,128,128]{3,2,1,0:T(8,128)(2,1)S(1)}, u32[]{:S(2)}, u32[]{:S(2)}) collective-permute-start(bf16[2,2,128,128]{3,2,1,0:T(8,128)(2,1)S(1)} %get-tuple-element.59), channel_id=1, source_target_pairs={{0,128},{1,129},{2,130},{3,131},{4,132},{5,133},{6,134},{7,135},{8... | collective-permute-start | bytes 393224 | tf_op jit(solution)/shard_map/ppermute | solution.py:36
  80.8 9.1 %collective-permute-start.24 = (bf16[2,2,128,128]{3,2,1,0:T(8,128)(2,1)S(1)}, bf16[2,2,128,128]{3,2,1,0:T(8,128)(2,1)S(1)}, u32[]{:S(2)}, u32[]{:S(2)}) collective-permute-start(bf16[2,2,128,128]{3,2,1,0:T(8,128)(2,1)S(1)} %get-tuple-element.60), channel_id=1, source_target_pairs={{0,64},{1,65},{2,66},{3,67},{4,68},{5,69},{6,70},{7,71},{8,72},{9,... | collective-permute-start | bytes 393224 | tf_op jit(solution)/shard_map/ppermute | solution.py:36
  85.6 2.0 %collective-permute-start.20 = (bf16[2,128,128]{2,1,0:T(8,128)(2,1)S(1)}, bf16[2,128,128]{2,1,0:T(8,128)(2,1)S(1)}, u32[]{:S(2)}, u32[]{:S(2)}) collective-permute-start(bf16[2,128,128]{2,1,0:T(8,128)(2,1)S(1)} %get-tuple-element.56), channel_id=1, source_target_pairs={{0,1},{1,0},{2,3},{3,2},{4,5},{5,4},{6,7},{7,6},{8,9},{9,8},{10,11... | collective-permute-start | bytes 196616 | tf_op jit(solution)/shard_map/ppermute | solution.py:36
  (8 other events, 31.8 us)

commit v5 on v4

--- a/solution.py
+++ b/solution.py
@@ -313,8 +313,10 @@
     half = lambda a, which: lax.dynamic_slice_in_dim(a, which * HALF, HALF, axis=a.ndim - 1)
 
     shard = kernel.transpose(1, 2, 3, 0, 4).reshape(TAPS, 2, channels)
-    other = send(half(shard, 1 - core), sibling)
-    theirs = send(half(latent, 1 - core), sibling)
+    give = half(latent, 1 - core)
+    give, shard = lax.optimization_barrier((give, shard))
+    theirs = send(give, sibling)
+    other = half(send(shard, sibling), core)
 
     near = half(shard, core)
     pair = jnp.where(core == 0, jnp.concatenate([near, other], 1), jnp.concatenate([other, near], 1))

time: 91.7 us -> 91.5 us (level)
  waiting for transfers between devices: 16.5 us -> 14.7 us
  starting transfers between devices: 46.4 us -> 48 us
    ppermute x25, starting transfers between devices: 40.3 us -> 42.1 us  [send(): return lax.ppermute(array, AXES, pairs)]
    ppermute x25, waiting for transfers between devices: 16.5 us -> 14.7 us  [send(): return lax.ppermute(array, AXES, pairs)]
    dynamic_slice x2 -> x3, local copies, waits for them, and re-layouts: 1.84 us -> 1.83 us  [per_device(): lax.dynamic_slice_in_dim(a, which * HALF, HALF, axis=a.ndim - 1)]
where the time goes in v5:
time: 91.5 us; the launch traced here: 91.2 us
  starting transfers between devices  48 us (52%)
  Pallas kernels  22.8 us (25%)
  waiting for transfers between devices  14.7 us (16%)
  local copies, waits for them, and re-layouts  5.16 us (6%)
    ppermute x25, starting transfers between devices, send(): return lax.ppermute(array, AXES, pairs)  42.1 us
    ppermute x25, waiting for transfers between devices, send(): return lax.ppermute(array, AXES, pairs)  14.7 us
    pallas_call x2, Pallas kernels, convolve(): pl.pallas_call(body, out_shape=[jax.ShapeDtypeStruct(shape, jnp.float32)]...  14.4 us
    all_to_all x1, starting transfers between devices, per_device(): lax.all_to_all(jnp.broadcast_to(spans[None], (CHIPS, 2 * NY, HALF)), ('z'...  5.83 us
    pallas_call x2, Pallas kernels, activate(): pl.pallas_call(body, out_shape=[jax.ShapeDtypeStruct(a.shape, a.dtype) fo...  4.96 us
  transfers between devices with their start and end apart: 26, of which 11 were waited for; matrix products, arithmetic and copies ran while one was open for 4% of the time, Pallas kernels for 10%

profile of v5, /device:TPU:1, one launch (start us, length us, event | category | flops | bytes accessed | tf_op | source)
XLA Modules:
  0.0 91.2 jit_solution(15671141878807496865)
XLA Ops:
  1.0 3.3 %collective-permute-start = (bf16[2,2,128,256]{3,2,1,0:T(8,128)(2,1)S(1)}, bf16[2,2,128,256]{3,2,1,0:T(8,128)(2,1)S(1)}, u32[]{:S(2)}, u32[]{:S(2)}) collective-permute-start(bf16[2,2,128,256]{3,2,1,0:T(8,128)(2,1)S(1)} %constant_dynamic-slice_fusion.2), channel_id=1, source_target_pairs={{0,1},{1,0},{2,3},{3,2},{4,5},{5,4},{6,7},{7,6},{8,9},{9,8},{10,11... | collective-permute-start | bytes 786440 | tf_op jit(solution)/shard_map/ppermute | solution.py:36
  8.4 6.6 %collective-permute-start.5 = (bf16[364,256]{1,0:T(8,128)(2,1)S(1)}, bf16[364,256]{1,0:T(8,128)(2,1)S(1)}, u32[]{:S(2)}, u32[]{:S(2)}) collective-permute-start(bf16[364,256]{1,0:T(8,128)(2,1)S(1)} %get-tuple-element.66), channel_id=1, source_target_pairs={{0,62},{1,63},{2,0},{3,1},{4,2},{5,3},{6,4},{7,5},{8,6},{9,7},{10,... | collective-permute-start | bytes 559112 | tf_op jit(solution)/shard_map/ppermute | solution.py:36
  15.1 2.7 %collective-permute-start.2 = (f32[4,256]{1,0:T(4,128)S(1)}, f32[4,256]{1,0:T(4,128)S(1)}, u32[]{:S(2)}, u32[]{:S(2)}) collective-permute-start(f32[4,256]{1,0:T(4,128)S(1)} %pad_maximum_fusion.4), channel_id=1, source_target_pairs={{0,128},{1,129},{2,130},{3,131},{4,132},{5,133},{6,134},{7,135},{8... | collective-permute-start | bytes 12296 | tf_op jit(solution)/shard_map/ppermute | solution.py:36
  17.8 1.6 %collective-permute-start.6 = (bf16[27,4,256]{2,1,0:T(4,128)(2,1)S(1)}, bf16[27,4,256]{2,1,0:T(4,128)(2,1)S(1)}, u32[]{:S(2)}, u32[]{:S(2)}) collective-permute-start(bf16[27,4,256]{2,1,0:T(4,128)(2,1)S(1)} %maximum_select_fusion), channel_id=1, source_target_pairs={{0,60},{1,61},{2,62},{3,63},{4,0},{5,1},{6,2},{7,3},{8,4},{9,5},{1... | collective-permute-start | bytes 165896 | tf_op jit(solution)/shard_map/ppermute | solution.py:36
  20.0 2.3 %collective-permute-done.6 = bf16[27,4,256]{2,1,0:T(4,128)(2,1)S(1)} collective-permute-done((bf16[27,4,256]{2,1,0:T(4,128)(2,1)S(1)}, bf16[27,4,256]{2,1,0:T(4,128)(2,1)S(1)}, u32[]{:S(2)}, u32[]{:S(2)}) %collective-permute-start.6) | collective-permute-done | bytes 55328 | tf_op jit(solution)/shard_map/ppermute | solution.py:36
  22.7 1.3 %collective-permute-start.14 = (bf16[2,6,128,256]{3,2,1,0:T(8,128)(2,1)S(1)}, bf16[2,6,128,256]{3,2,1,0:T(8,128)(2,1)S(1)}, u32[]{:S(2)}, u32[]{:S(2)}) collective-permute-start(bf16[2,6,128,256]{3,2,1,0:T(8,128)(2,1)S(1)} %shard_map.57.refs_0_), channel_id=1, source_target_pairs={{0,64},{1,65},{2,66},{3,67},{4,68},{5,69},{6,70},{7,71},{8,72},{9,... | collective-permute-start | bytes 2359304 | tf_op jit(solution)/shard_map/ppermute | solution.py:36
  24.0 2.7 %collective-permute-start.7 = (bf16[27,16,256]{2,1,0:T(8,128)(2,1)S(1)}, bf16[27,16,256]{2,1,0:T(8,128)(2,1)S(1)}, u32[]{:S(2)}, u32[]{:S(2)}) collective-permute-start(bf16[27,16,256]{2,1,0:T(8,128)(2,1)S(1)} %pad_maximum_fusion.2.refs_5_), channel_id=1, source_target_pairs={{0,56},{1,57},{2,58},{3,59},{4,60},{5,61},{6,62},{7,63},{8,0},{9,1... | collective-permute-start | bytes 663560 | tf_op jit(solution)/shard_map/ppermute | solution.py:36
  27.4 5.8 %all-to-all-start = ((f32[32,8,256]{2,1,0:T(8,128)}), f32[32,8,256]{2,1,0:T(8,128)S(1)}, u32[]{:S(2)}, u32[]{:S(2)}) async-start(f32[32,8,256]{2,1,0:T(8,128)} %broadcast_in_dim.5), calls=%async_computation | async-start | bytes 524288 | tf_op jit(solution)/shard_map/all_to_all | solution.py:338
  33.2 1.3 %collective-permute-start.11 = (bf16[27,16,256]{2,1,0:T(8,128)(2,1)S(1)}, bf16[27,16,256]{2,1,0:T(8,128)(2,1)}, u32[]{:S(2)}, u32[]{:S(2)}) collective-permute-start(bf16[27,16,256]{2,1,0:T(8,128)(2,1)S(1)} %collective-permute-done.10.refs_13_), channel_id=1, source_target_pairs={{0,8},{1,9},{2,10},{3,11},{4,12},{5,13},{6,14},{7,15},{8,16},{9,17... | collective-permute-start | bytes 663560 | tf_op jit(solution)/shard_map/ppermute | solution.py:36
  34.5 1.4 %collective-permute-start.8 = (bf16[27,16,256]{2,1,0:T(8,128)(2,1)S(1)}, bf16[27,16,256]{2,1,0:T(8,128)(2,1)}, u32[]{:S(2)}, u32[]{:S(2)}) collective-permute-start(bf16[27,16,256]{2,1,0:T(8,128)(2,1)S(1)} %collective-permute-done.7.refs_6_), channel_id=1, source_target_pairs={{0,56},{1,57},{2,58},{3,59},{4,60},{5,61},{6,62},{7,63},{8,0},{9,1... | collective-permute-start | bytes 663560 | tf_op jit(solution)/shard_map/ppermute | solution.py:36
  36.0 3.2 %collective-permute-done.13.refs_1_ = bf16[2,6,128,256]{3,2,1,0:T(8,128)(2,1)S(1)} collective-permute-done((bf16[2,6,128,256]{3,2,1,0:T(8,128)(2,1)S(1)}, bf16[2,6,128,256]{3,2,1,0:T(8,128)(2,1)S(1)}, u32[]{:S(2)}, u32[]{:S(2)}) %collective-permute-start.13) | collective-permute-done | bytes 786464 | tf_op jit(solution)/shard_map/ppermute | solution.py:36
  40.0 1.6 %collective-permute-start.15 = (bf16[1,6,128,256]{3,2,1,0:T(8,128)(2,1)}, bf16[1,6,128,256]{3,2,1,0:T(8,128)(2,1)}, u32[]{:S(2)}, u32[]{:S(2)}) collective-permute-start(bf16[1,6,128,256]{3,2,1,0:T(8,128)(2,1)} %slice.26), channel_id=1, source_target_pairs={{0,192},{1,193},{2,194},{3,195},{4,196},{5,197},{6,198},{7,199},{8... | collective-permute-start | bytes 1179656 | tf_op jit(solution)/shard_map/ppermute | solution.py:36
  43.1 2.7 %collective-permute-start.9 = (bf16[27,16,256]{2,1,0:T(8,128)(2,1)}, bf16[27,16,256]{2,1,0:T(8,128)(2,1)S(1)}, u32[]{:S(2)}, u32[]{:S(2)}) collective-permute-start(bf16[27,16,256]{2,1,0:T(8,128)(2,1)} %collective-permute-done.8.refs_7_), channel_id=1, source_target_pairs={{0,56},{1,57},{2,58},{3,59},{4,60},{5,61},{6,62},{7,63},{8,0},{9,1... | collective-permute-start | bytes 663560 | tf_op jit(solution)/shard_map/ppermute | solution.py:36
  46.0 3.0 %shard_map.58 = (bf16[2,6,128,256]{3,2,1,0:T(8,128)(2,1)S(1)}, bf16[2,6,128,256]{3,2,1,0:T(8,128)(2,1)S(1)}, bf16[2,6,128,256]{3,2,1,0:T(8,128)(2,1)S(1)}) custom-call(s32[5]{0:T(128)S(1)} %stack.31.info, f32[32,8,256]{2,1,0:T(8,128)S(1)} %all-to-all-done.stats, f32[1,256]{1,0:T(1,128)S(1)} %bitcast.15, f32[1,256]{1,0:T(1,128)S(1)} %bitcast.17, ...), custom_call_target="tpu_custom_call" | custom-call | flops 18874368 | bytes 4718592 | tf_op jit(solution)/shard_map/pallas_call | solution.py:182
  49.5 3.0 %collective-permute-start.17 = (bf16[27,16,128]{2,1,0:T(8,128)(2,1)S(1)}, bf16[27,16,128]{2,1,0:T(8,128)(2,1)S(1)}, u32[]{:S(2)}, u32[]{:S(2)}) collective-permute-start(bf16[27,16,128]{2,1,0:T(8,128)(2,1)S(1)} %slice.22), channel_id=1, source_target_pairs={{0,56},{1,57},{2,58},{3,59},{4,60},{5,61},{6,62},{7,63},{8,0},{9,1... | collective-permute-start | bytes 331784 | tf_op jit(solution)/shard_map/ppermute | solution.py:36
  52.6 2.0 %shard_map.59 = (bf16[1,6,128,256]{3,2,1,0:T(8,128)(2,1)S(1)}, bf16[1,6,128,256]{3,2,1,0:T(8,128)(2,1)S(1)}) custom-call(s32[5]{0:T(128)S(1)} %stack.31.info, f32[32,8,256]{2,1,0:T(8,128)S(1)} %all-to-all-done.stats, f32[1,256]{1,0:T(1,128)S(1)} %bitcast.16, f32[1,256]{1,0:T(1,128)S(1)} %bitcast.18, ...), custom_call_target="tpu_custom_call" | custom-call | flops 6291456 | bytes 1572864 | tf_op jit(solution)/shard_map/pallas_call | solution.py:182
  55.4 2.1 %collective-permute-done.18.refs_10_ = bf16[27,16,128]{2,1,0:T(8,128)(2,1)S(1)} collective-permute-done((bf16[27,16,128]{2,1,0:T(8,128)(2,1)S(1)}, bf16[27,16,128]{2,1,0:T(8,128)(2,1)S(1)}, u32[]{:S(2)}, u32[]{:S(2)}) %collective-permute-start.18) | collective-permute-done | bytes 110624 | tf_op jit(solution)/shard_map/ppermute | solution.py:36
  58.1 10.3 %shard_map.60 = (f32[3,2,2,128,128]{4,3,2,1,0:T(8,128)S(1)}, bf16[3,2,2,128,128]{4,3,2,1,0:T(8,128)(2,1)S(1)}) custom-call(s32[5]{0:T(128)S(1)} %stack.31.info, f32[1,512]{1,0:T(1,128)S(1)} %bitcast.19, bf16[2,6,128,256]{3,2,1,0:T(8,128)(2,1)S(1)} %get-tuple-element.46.refs_0_, bf16[2,6,128,256]{3,2,1,0:T(8,128)(2,1)S(1)} %get-tuple-element.47.refs_1_, ...), custom_call_target="tpu_custom_call" | custom-call | flops 5435817984 | bytes 5242880 | tf_op jit(solution)/shard_map/pallas_call | solution.py:260
  68.4 8.5 %collective-permute-start.19 = (bf16[3,2,2,128,128]{4,3,2,1,0:T(8,128)(2,1)S(1)}, bf16[3,2,2,128,128]{4,3,2,1,0:T(8,128)(2,1)S(1)}, u32[]{:S(2)}, u32[]{:S(2)}) collective-permute-start(bf16[3,2,2,128,128]{4,3,2,1,0:T(8,128)(2,1)S(1)} %get-tuple-element.54), channel_id=1, source_target_pairs={{0,1},{1,0},{2,3},{3,2},{4,5},{5,4},{6,7},{7,6},{8,9},{9,8},{10,11... | collective-permute-start | bytes 1179656 | tf_op jit(solution)/shard_map/ppermute | solution.py:36
  76.9 1.3 %collective-permute-done.19.taken = bf16[3,2,2,128,128]{4,3,2,1,0:T(8,128)(2,1)S(1)} collective-permute-done((bf16[3,2,2,128,128]{4,3,2,1,0:T(8,128)(2,1)S(1)}, bf16[3,2,2,128,128]{4,3,2,1,0:T(8,128)(2,1)S(1)}, u32[]{:S(2)}, u32[]{:S(2)}) %collective-permute-start.19) | collective-permute-done | bytes 393248 | tf_op jit(solution)/shard_map/ppermute | solution.py:36
  78.3 2.3 %collective-permute-start.22 = (bf16[2,2,128,128]{3,2,1,0:T(8,128)(2,1)S(1)}, bf16[2,2,128,128]{3,2,1,0:T(8,128)(2,1)S(1)}, u32[]{:S(2)}, u32[]{:S(2)}) collective-permute-start(bf16[2,2,128,128]{3,2,1,0:T(8,128)(2,1)S(1)} %get-tuple-element.62), channel_id=1, source_target_pairs={{0,192},{1,193},{2,194},{3,195},{4,196},{5,197},{6,198},{7,199},{8... | collective-permute-start | bytes 393224 | tf_op jit(solution)/shard_map/ppermute | solution.py:36
  81.3 4.1 %shard_map.62 = (f32[1,2,2,128,128]{4,3,2,1,0:T(8,128)S(1)}, bf16[2,128,128]{2,1,0:T(8,128)(2,1)S(1)}, bf16[2,128,128]{2,1,0:T(8,128)(2,1)S(1)}) custom-call(s32[5]{0:T(128)S(1)} %stack.31.info, f32[1,512]{1,0:T(1,128)S(1)} %bitcast.20, bf16[2,6,128,256]{3,2,1,0:T(8,128)(2,1)S(1)} %get-tuple-element.46.refs_0_, ...), custom_call_target="tpu_custom_call" | custom-call | flops 1811939328 | bytes 5242880 | tf_op jit(solution)/shard_map/pallas_call | solution.py:260
  87.7 2.1 %collective-permute-done.24.refs_2_ = bf16[2,2,128,128]{3,2,1,0:T(8,128)(2,1)S(1)} collective-permute-done((bf16[2,2,128,128]{3,2,1,0:T(8,128)(2,1)S(1)}, bf16[2,2,128,128]{3,2,1,0:T(8,128)(2,1)S(1)}, u32[]{:S(2)}, u32[]{:S(2)}) %collective-permute-start.24) | collective-permute-done | bytes 131104 | tf_op jit(solution)/shard_map/ppermute | solution.py:36
  89.7 1.5 %shard_map.63 = bf16[2,2,128,512]{3,2,1,0:T(8,128)(2,1)} custom-call(s32[5]{0:T(128)S(1)} %stack.31.info, f32[1,2,2,128,128]{4,3,2,1,0:T(8,128)S(1)} %get-tuple-element.59.keep, bf16[2,128,128]{2,1,0:T(8,128)(2,1)S(1)} %collective-permute-done.20.first, bf16[2,128,128]{2,1,0:T(8,128)(2,1)S(1)} %collective-permute-done.21.second, ...), custom_call_target="tpu_custom_call" | custom-call | tf_op jit(solution)/shard_map/pallas_call | solution.py:298
  (70 shorter events, 14.3 us)
Async XLA Ops:
  1.0 4.9 %collective-permute-start = (bf16[2,2,128,256]{3,2,1,0:T(8,128)(2,1)S(1)}, bf16[2,2,128,256]{3,2,1,0:T(8,128)(2,1)S(1)}, u32[]{:S(2)}, u32[]{:S(2)}) collective-permute-start(bf16[2,2,128,256]{3,2,1,0:T(8,128)(2,1)S(1)} %constant_dynamic-slice_fusion.2), channel_id=1, source_target_pairs={{0,1},{1,0},{2,3},{3,2},{4,5},{5,4},{6,7},{7,6},{8,9},{9,8},{10,11... | collective-permute-start | bytes 786440 | tf_op jit(solution)/shard_map/ppermute | solution.py:36
  7.5 7.5 %collective-permute-start.1 = (f32[2,256]{1,0:T(2,128)S(1)}, f32[2,256]{1,0:T(2,128)S(1)}, u32[]{:S(2)}, u32[]{:S(2)}) collective-permute-start(f32[2,256]{1,0:T(2,128)S(1)} %shard_map.56), channel_id=1, source_target_pairs={{0,64},{1,65},{2,66},{3,67},{4,68},{5,69},{6,70},{7,71},{8,72},{9,... | collective-permute-start | bytes 6152 | tf_op jit(solution)/shard_map/ppermute | solution.py:36
  7.6 11.9 %collective-permute-start.4 = (bf16[364,256]{1,0:T(8,128)(2,1)S(1)}, bf16[364,256]{1,0:T(8,128)(2,1)S(1)}, u32[]{:S(2)}, u32[]{:S(2)}) collective-permute-start(bf16[364,256]{1,0:T(8,128)(2,1)S(1)} %get-tuple-element.65), channel_id=1, source_target_pairs={{0,2},{1,3},{2,4},{3,5},{4,6},{5,7},{6,8},{7,9},{8,10},{9,11},{10,... | collective-permute-start | bytes 559112 | tf_op jit(solution)/shard_map/ppermute | solution.py:36
  8.4 11.1 %collective-permute-start.5 = (bf16[364,256]{1,0:T(8,128)(2,1)S(1)}, bf16[364,256]{1,0:T(8,128)(2,1)S(1)}, u32[]{:S(2)}, u32[]{:S(2)}) collective-permute-start(bf16[364,256]{1,0:T(8,128)(2,1)S(1)} %get-tuple-element.66), channel_id=1, source_target_pairs={{0,62},{1,63},{2,0},{3,1},{4,2},{5,3},{6,4},{7,5},{8,6},{9,7},{10,... | collective-permute-start | bytes 559112 | tf_op jit(solution)/shard_map/ppermute | solution.py:36
  15.1 4.4 %collective-permute-start.2 = (f32[4,256]{1,0:T(4,128)S(1)}, f32[4,256]{1,0:T(4,128)S(1)}, u32[]{:S(2)}, u32[]{:S(2)}) collective-permute-start(f32[4,256]{1,0:T(4,128)S(1)} %pad_maximum_fusion.4), channel_id=1, source_target_pairs={{0,128},{1,129},{2,130},{3,131},{4,132},{5,133},{6,134},{7,135},{8... | collective-permute-start | bytes 12296 | tf_op jit(solution)/shard_map/ppermute | solution.py:36
  17.8 4.5 %collective-permute-start.6 = (bf16[27,4,256]{2,1,0:T(4,128)(2,1)S(1)}, bf16[27,4,256]{2,1,0:T(4,128)(2,1)S(1)}, u32[]{:S(2)}, u32[]{:S(2)}) collective-permute-start(bf16[27,4,256]{2,1,0:T(4,128)(2,1)S(1)} %maximum_select_fusion), channel_id=1, source_target_pairs={{0,60},{1,61},{2,62},{3,63},{4,0},{5,1},{6,2},{7,3},{8,4},{9,5},{1... | collective-permute-start | bytes 165896 | tf_op jit(solution)/shard_map/ppermute | solution.py:36
  22.4 16.7 %collective-permute-start.13 = (bf16[2,6,128,256]{3,2,1,0:T(8,128)(2,1)S(1)}, bf16[2,6,128,256]{3,2,1,0:T(8,128)(2,1)S(1)}, u32[]{:S(2)}, u32[]{:S(2)}) collective-permute-start(bf16[2,6,128,256]{3,2,1,0:T(8,128)(2,1)S(1)} %shard_map.57.refs_0_), channel_id=1, source_target_pairs={{0,192},{1,193},{2,194},{3,195},{4,196},{5,197},{6,198},{7,199},{8... | collective-permute-start | bytes 2359304 | tf_op jit(solution)/shard_map/ppermute | solution.py:36
  22.7 18.9 %collective-permute-start.14 = (bf16[2,6,128,256]{3,2,1,0:T(8,128)(2,1)S(1)}, bf16[2,6,128,256]{3,2,1,0:T(8,128)(2,1)S(1)}, u32[]{:S(2)}, u32[]{:S(2)}) collective-permute-start(bf16[2,6,128,256]{3,2,1,0:T(8,128)(2,1)S(1)} %shard_map.57.refs_0_), channel_id=1, source_target_pairs={{0,64},{1,65},{2,66},{3,67},{4,68},{5,69},{6,70},{7,71},{8,72},{9,... | collective-permute-start | bytes 2359304 | tf_op jit(solution)/shard_map/ppermute | solution.py:36
  24.0 9.2 %collective-permute-start.10 = (bf16[27,16,256]{2,1,0:T(8,128)(2,1)S(1)}, bf16[27,16,256]{2,1,0:T(8,128)(2,1)S(1)}, u32[]{:S(2)}, u32[]{:S(2)}) collective-permute-start(bf16[27,16,256]{2,1,0:T(8,128)(2,1)S(1)} %pad_maximum_fusion.2.refs_5_), channel_id=1, source_target_pairs={{0,8},{1,9},{2,10},{3,11},{4,12},{5,13},{6,14},{7,15},{8,16},{9,17... | collective-permute-start | bytes 663560 | tf_op jit(solution)/shard_map/ppermute | solution.py:36
  24.0 10.6 %collective-permute-start.7 = (bf16[27,16,256]{2,1,0:T(8,128)(2,1)S(1)}, bf16[27,16,256]{2,1,0:T(8,128)(2,1)S(1)}, u32[]{:S(2)}, u32[]{:S(2)}) collective-permute-start(bf16[27,16,256]{2,1,0:T(8,128)(2,1)S(1)} %pad_maximum_fusion.2.refs_5_), channel_id=1, source_target_pairs={{0,56},{1,57},{2,58},{3,59},{4,60},{5,61},{6,62},{7,63},{8,0},{9,1... | collective-permute-start | bytes 663560 | tf_op jit(solution)/shard_map/ppermute | solution.py:36
  27.4 18.6 %all-to-all-start = ((f32[32,8,256]{2,1,0:T(8,128)}), f32[32,8,256]{2,1,0:T(8,128)S(1)}, u32[]{:S(2)}, u32[]{:S(2)}) async-start(f32[32,8,256]{2,1,0:T(8,128)} %broadcast_in_dim.5), calls=%async_computation | async-start | bytes 524288 | tf_op jit(solution)/shard_map/all_to_all | solution.py:338
  33.2 9.9 %collective-permute-start.11 = (bf16[27,16,256]{2,1,0:T(8,128)(2,1)S(1)}, bf16[27,16,256]{2,1,0:T(8,128)(2,1)}, u32[]{:S(2)}, u32[]{:S(2)}) collective-permute-start(bf16[27,16,256]{2,1,0:T(8,128)(2,1)S(1)} %collective-permute-done.10.refs_13_), channel_id=1, source_target_pairs={{0,8},{1,9},{2,10},{3,11},{4,12},{5,13},{6,14},{7,15},{8,16},{9,17... | collective-permute-start | bytes 663560 | tf_op jit(solution)/shard_map/ppermute | solution.py:36
  34.5 8.6 %collective-permute-start.8 = (bf16[27,16,256]{2,1,0:T(8,128)(2,1)S(1)}, bf16[27,16,256]{2,1,0:T(8,128)(2,1)}, u32[]{:S(2)}, u32[]{:S(2)}) collective-permute-start(bf16[27,16,256]{2,1,0:T(8,128)(2,1)S(1)} %collective-permute-done.7.refs_6_), channel_id=1, source_target_pairs={{0,56},{1,57},{2,58},{3,59},{4,60},{5,61},{6,62},{7,63},{8,0},{9,1... | collective-permute-start | bytes 663560 | tf_op jit(solution)/shard_map/ppermute | solution.py:36
  40.0 12.7 %collective-permute-start.15 = (bf16[1,6,128,256]{3,2,1,0:T(8,128)(2,1)}, bf16[1,6,128,256]{3,2,1,0:T(8,128)(2,1)}, u32[]{:S(2)}, u32[]{:S(2)}) collective-permute-start(bf16[1,6,128,256]{3,2,1,0:T(8,128)(2,1)} %slice.26), channel_id=1, source_target_pairs={{0,192},{1,193},{2,194},{3,195},{4,196},{5,197},{6,198},{7,199},{8... | collective-permute-start | bytes 1179656 | tf_op jit(solution)/shard_map/ppermute | solution.py:36
  42.4 10.3 %collective-permute-start.16 = (bf16[1,6,128,256]{3,2,1,0:T(8,128)(2,1)}, bf16[1,6,128,256]{3,2,1,0:T(8,128)(2,1)}, u32[]{:S(2)}, u32[]{:S(2)}) collective-permute-start(bf16[1,6,128,256]{3,2,1,0:T(8,128)(2,1)} %slice.27), channel_id=1, source_target_pairs={{0,64},{1,65},{2,66},{3,67},{4,68},{5,69},{6,70},{7,71},{8,72},{9,... | collective-permute-start | bytes 1179656 | tf_op jit(solution)/shard_map/ppermute | solution.py:36
  43.1 6.4 %collective-permute-start.12 = (bf16[27,16,256]{2,1,0:T(8,128)(2,1)}, bf16[27,16,256]{2,1,0:T(8,128)(2,1)S(1)}, u32[]{:S(2)}, u32[]{:S(2)}) collective-permute-start(bf16[27,16,256]{2,1,0:T(8,128)(2,1)} %collective-permute-done.11.refs_12_), channel_id=1, source_target_pairs={{0,8},{1,9},{2,10},{3,11},{4,12},{5,13},{6,14},{7,15},{8,16},{9,17... | collective-permute-start | bytes 663560 | tf_op jit(solution)/shard_map/ppermute | solution.py:36
  43.1 6.4 %collective-permute-start.9 = (bf16[27,16,256]{2,1,0:T(8,128)(2,1)}, bf16[27,16,256]{2,1,0:T(8,128)(2,1)S(1)}, u32[]{:S(2)}, u32[]{:S(2)}) collective-permute-start(bf16[27,16,256]{2,1,0:T(8,128)(2,1)} %collective-permute-done.8.refs_7_), channel_id=1, source_target_pairs={{0,56},{1,57},{2,58},{3,59},{4,60},{5,61},{6,62},{7,63},{8,0},{9,1... | collective-permute-start | bytes 663560 | tf_op jit(solution)/shard_map/ppermute | solution.py:36
  49.5 5.8 %collective-permute-start.17 = (bf16[27,16,128]{2,1,0:T(8,128)(2,1)S(1)}, bf16[27,16,128]{2,1,0:T(8,128)(2,1)S(1)}, u32[]{:S(2)}, u32[]{:S(2)}) collective-permute-start(bf16[27,16,128]{2,1,0:T(8,128)(2,1)S(1)} %slice.22), channel_id=1, source_target_pairs={{0,56},{1,57},{2,58},{3,59},{4,60},{5,61},{6,62},{7,63},{8,0},{9,1... | collective-permute-start | bytes 331784 | tf_op jit(solution)/shard_map/ppermute | solution.py:36
  52.5 4.9 %collective-permute-start.18 = (bf16[27,16,128]{2,1,0:T(8,128)(2,1)S(1)}, bf16[27,16,128]{2,1,0:T(8,128)(2,1)S(1)}, u32[]{:S(2)}, u32[]{:S(2)}) collective-permute-start(bf16[27,16,128]{2,1,0:T(8,128)(2,1)S(1)} %slice.23), channel_id=1, source_target_pairs={{0,8},{1,9},{2,10},{3,11},{4,12},{5,13},{6,14},{7,15},{8,16},{9,17... | collective-permute-start | bytes 331784 | tf_op jit(solution)/shard_map/ppermute | solution.py:36
  68.4 9.8 %collective-permute-start.19 = (bf16[3,2,2,128,128]{4,3,2,1,0:T(8,128)(2,1)S(1)}, bf16[3,2,2,128,128]{4,3,2,1,0:T(8,128)(2,1)S(1)}, u32[]{:S(2)}, u32[]{:S(2)}) collective-permute-start(bf16[3,2,2,128,128]{4,3,2,1,0:T(8,128)(2,1)S(1)} %get-tuple-element.54), channel_id=1, source_target_pairs={{0,1},{1,0},{2,3},{3,2},{4,5},{5,4},{6,7},{7,6},{8,9},{9,8},{10,11... | collective-permute-start | bytes 1179656 | tf_op jit(solution)/shard_map/ppermute | solution.py:36
  78.3 9.3 %collective-permute-start.22 = (bf16[2,2,128,128]{3,2,1,0:T(8,128)(2,1)S(1)}, bf16[2,2,128,128]{3,2,1,0:T(8,128)(2,1)S(1)}, u32[]{:S(2)}, u32[]{:S(2)}) collective-permute-start(bf16[2,2,128,128]{3,2,1,0:T(8,128)(2,1)S(1)} %get-tuple-element.62), channel_id=1, source_target_pairs={{0,192},{1,193},{2,194},{3,195},{4,196},{5,197},{6,198},{7,199},{8... | collective-permute-start | bytes 393224 | tf_op jit(solution)/shard_map/ppermute | solution.py:36
  80.6 7.0 %collective-permute-start.23 = (bf16[2,2,128,128]{3,2,1,0:T(8,128)(2,1)S(1)}, bf16[2,2,128,128]{3,2,1,0:T(8,128)(2,1)S(1)}, u32[]{:S(2)}, u32[]{:S(2)}) collective-permute-start(bf16[2,2,128,128]{3,2,1,0:T(8,128)(2,1)S(1)} %get-tuple-element.63), channel_id=1, source_target_pairs={{0,128},{1,129},{2,130},{3,131},{4,132},{5,133},{6,134},{7,135},{8... | collective-permute-start | bytes 393224 | tf_op jit(solution)/shard_map/ppermute | solution.py:36
  80.6 9.1 %collective-permute-start.24 = (bf16[2,2,128,128]{3,2,1,0:T(8,128)(2,1)S(1)}, bf16[2,2,128,128]{3,2,1,0:T(8,128)(2,1)S(1)}, u32[]{:S(2)}, u32[]{:S(2)}) collective-permute-start(bf16[2,2,128,128]{3,2,1,0:T(8,128)(2,1)S(1)} %get-tuple-element.64), channel_id=1, source_target_pairs={{0,64},{1,65},{2,66},{3,67},{4,68},{5,69},{6,70},{7,71},{8,72},{9,... | collective-permute-start | bytes 393224 | tf_op jit(solution)/shard_map/ppermute | solution.py:36
  85.4 1.9 %collective-permute-start.20 = (bf16[2,128,128]{2,1,0:T(8,128)(2,1)S(1)}, bf16[2,128,128]{2,1,0:T(8,128)(2,1)S(1)}, u32[]{:S(2)}, u32[]{:S(2)}) collective-permute-start(bf16[2,128,128]{2,1,0:T(8,128)(2,1)S(1)} %get-tuple-element.60), channel_id=1, source_target_pairs={{0,1},{1,0},{2,3},{3,2},{4,5},{5,4},{6,7},{7,6},{8,9},{9,8},{10,11... | collective-permute-start | bytes 196616 | tf_op jit(solution)/shard_map/ppermute | solution.py:36
  (8 other events, 29.1 us)

commit v6 on v5

--- a/solution.py
+++ b/solution.py
@@ -18,6 +18,7 @@
 HBM = pl.BlockSpec(memory_space=pltpu.HBM)
 SMEM = pl.BlockSpec(memory_space=pltpu.SMEM)
 LIMIT = pltpu.CompilerParams(vmem_limit_bytes=14 * 2**20)
+SMALL = pltpu.CompilerParams(vmem_limit_bytes=8 * 2**20)
 WIDE = pltpu.CompilerParams(vmem_limit_bytes=60 * 2**20)
 
 
@@ -88,7 +89,7 @@
         in_specs=[SMEM, HBM, HBM],
         out_specs=[VMEM] * 3,
         scratch_shapes=[pltpu.SemaphoreType.DMA((2,))],
-        compiler_params=LIMIT,
+        compiler_params=SMALL,
     )(info, latent, theirs)
 
 
@@ -123,7 +124,7 @@
         out_shape=jax.ShapeDtypeStruct((2, HALF), jnp.float32),
         in_specs=[VMEM],
         out_specs=VMEM,
-        compiler_params=LIMIT,
+        compiler_params=SMALL,
     )(rows)
 
 
@@ -147,7 +148,7 @@
         in_specs=[HBM] * 3,
         out_specs=HBM,
         scratch_shapes=[pltpu.SemaphoreType.DMA((5,))],
-        compiler_params=LIMIT,
+        compiler_params=SMALL,
     )(above, rows, below)
 
 
@@ -184,7 +185,7 @@
         out_shape=[jax.ShapeDtypeStruct(a.shape, a.dtype) for a in arrays],
         in_specs=[SMEM] + [VMEM] * (3 + len(arrays)),
         out_specs=[VMEM] * len(arrays),
-        compiler_params=LIMIT,
+        compiler_params=SMALL,
         cost_estimate=pl.CostEstimate(flops=16 * cells, bytes_accessed=4 * cells, transcendentals=2 * cells),
     )(info, stats, gain, shift, *arrays)
 
@@ -279,28 +280,33 @@
 
     return pl.pallas_call(
         body, out_shape=[jax.ShapeDtypeStruct(taken.shape[1:], jnp.bfloat16)] * count,
-        in_specs=[VMEM, VMEM], out_specs=[VMEM] * count, compiler_params=LIMIT,
+        in_specs=[VMEM, VMEM], out_specs=[VMEM] * count, compiler_params=SMALL,
     )(keep, taken)
 
 
 def assemble(info, keep, taken, quarters):
     def body(info, keep, first, second, *refs):
-        out = refs[-1]
+        parts, out, mixed, sems = refs[: NY - 1], refs[NY - 1], refs[NY], refs[NY + 1]
+        copies = []
         for k in range(NY):
             at = pl.multiple_of(lax.rem(info[0] + k, NY) * OUTS, OUTS)
-            if k == 0:
-                for t, taken in enumerate((first, second)):
-                    value = keep[0, t] + taken[...].astype(jnp.float32)
-                    out[t, :, :, pl.ds(at, OUTS)] = value.astype(jnp.bfloat16)
-            else:
-                out[:, :, :, pl.ds(at, OUTS)] = refs[k - 1][...]
+            source = parts[k - 1] if k else mixed
+            copies.append(pltpu.make_async_copy(source, out.at[:, :, :, pl.ds(at, OUTS)], sems.at[k]))
+        for copy in copies[1:]:
+            copy.start()
+        for t, half in enumerate((first, second)):
+            mixed[t] = (keep[0, t] + half[...].astype(jnp.float32)).astype(jnp.bfloat16)
+        copies[0].start()
+        for copy in copies:
+            copy.wait()
 
     return pl.pallas_call(
         body,
         out_shape=jax.ShapeDtypeStruct((2, 2, WIDTH, NY * OUTS), jnp.bfloat16),
         in_specs=[SMEM] + [VMEM] * (NY + 2),
-        out_specs=VMEM,
-        compiler_params=LIMIT,
+        out_specs=HBM,
+        scratch_shapes=[pltpu.VMEM((2, 2, WIDTH, OUTS), jnp.bfloat16), pltpu.SemaphoreType.DMA((NY,))],
+        compiler_params=SMALL,
     )(info, keep, *taken, *quarters)
 
 

time: 91.5 us -> 91.6 us (level)
  no operation moved by 1% of the time
where the time goes in v6:
time: 91.6 us; the launch traced here: 91.3 us
  starting transfers between devices  48 us (52%)
  Pallas kernels  22.7 us (25%)
  waiting for transfers between devices  14.7 us (16%)
  local copies, waits for them, and re-layouts  5.16 us (6%)
    ppermute x25, starting transfers between devices, send(): return lax.ppermute(array, AXES, pairs)  42.1 us
    ppermute x25, waiting for transfers between devices, send(): return lax.ppermute(array, AXES, pairs)  14.7 us
    pallas_call x2, Pallas kernels, convolve(): pl.pallas_call(body, out_shape=[jax.ShapeDtypeStruct(shape, jnp.float32)]...  14.4 us
    all_to_all x1, starting transfers between devices, per_device(): lax.all_to_all(jnp.broadcast_to(spans[None], (CHIPS, 2 * NY, HALF)), ('z'...  5.83 us
    pallas_call x2, Pallas kernels, activate(): pl.pallas_call(body, out_shape=[jax.ShapeDtypeStruct(a.shape, a.dtype) fo...  4.96 us
  transfers between devices with their start and end apart: 26, of which 11 were waited for; matrix products, arithmetic and copies ran while one was open for 4% of the time, Pallas kernels for 10%

profile of v6, /device:TPU:1, one launch (start us, length us, event | category | flops | bytes accessed | tf_op | source)
XLA Modules:
  0.0 91.3 jit_solution(1011692476385524855)
XLA Ops:
  1.0 3.3 %collective-permute-start = (bf16[2,2,128,256]{3,2,1,0:T(8,128)(2,1)S(1)}, bf16[2,2,128,256]{3,2,1,0:T(8,128)(2,1)S(1)}, u32[]{:S(2)}, u32[]{:S(2)}) collective-permute-start(bf16[2,2,128,256]{3,2,1,0:T(8,128)(2,1)S(1)} %constant_dynamic-slice_fusion.2), channel_id=1, source_target_pairs={{0,1},{1,0},{2,3},{3,2},{4,5},{5,4},{6,7},{7,6},{8,9},{9,8},{10,11... | collective-permute-start | bytes 786440 | tf_op jit(solution)/shard_map/ppermute | solution.py:37
  8.4 6.6 %collective-permute-start.5 = (bf16[364,256]{1,0:T(8,128)(2,1)S(1)}, bf16[364,256]{1,0:T(8,128)(2,1)S(1)}, u32[]{:S(2)}, u32[]{:S(2)}) collective-permute-start(bf16[364,256]{1,0:T(8,128)(2,1)S(1)} %get-tuple-element.66), channel_id=1, source_target_pairs={{0,62},{1,63},{2,0},{3,1},{4,2},{5,3},{6,4},{7,5},{8,6},{9,7},{10,... | collective-permute-start | bytes 559112 | tf_op jit(solution)/shard_map/ppermute | solution.py:37
  15.1 2.7 %collective-permute-start.2 = (f32[4,256]{1,0:T(4,128)S(1)}, f32[4,256]{1,0:T(4,128)S(1)}, u32[]{:S(2)}, u32[]{:S(2)}) collective-permute-start(f32[4,256]{1,0:T(4,128)S(1)} %pad_maximum_fusion.4), channel_id=1, source_target_pairs={{0,128},{1,129},{2,130},{3,131},{4,132},{5,133},{6,134},{7,135},{8... | collective-permute-start | bytes 12296 | tf_op jit(solution)/shard_map/ppermute | solution.py:37
  17.8 1.6 %collective-permute-start.6 = (bf16[27,4,256]{2,1,0:T(4,128)(2,1)S(1)}, bf16[27,4,256]{2,1,0:T(4,128)(2,1)S(1)}, u32[]{:S(2)}, u32[]{:S(2)}) collective-permute-start(bf16[27,4,256]{2,1,0:T(4,128)(2,1)S(1)} %maximum_select_fusion), channel_id=1, source_target_pairs={{0,60},{1,61},{2,62},{3,63},{4,0},{5,1},{6,2},{7,3},{8,4},{9,5},{1... | collective-permute-start | bytes 165896 | tf_op jit(solution)/shard_map/ppermute | solution.py:37
  20.0 2.3 %collective-permute-done.6 = bf16[27,4,256]{2,1,0:T(4,128)(2,1)S(1)} collective-permute-done((bf16[27,4,256]{2,1,0:T(4,128)(2,1)S(1)}, bf16[27,4,256]{2,1,0:T(4,128)(2,1)S(1)}, u32[]{:S(2)}, u32[]{:S(2)}) %collective-permute-start.6) | collective-permute-done | bytes 55328 | tf_op jit(solution)/shard_map/ppermute | solution.py:37
  22.7 1.3 %collective-permute-start.14 = (bf16[2,6,128,256]{3,2,1,0:T(8,128)(2,1)S(1)}, bf16[2,6,128,256]{3,2,1,0:T(8,128)(2,1)S(1)}, u32[]{:S(2)}, u32[]{:S(2)}) collective-permute-start(bf16[2,6,128,256]{3,2,1,0:T(8,128)(2,1)S(1)} %shard_map.57.refs_0_), channel_id=1, source_target_pairs={{0,64},{1,65},{2,66},{3,67},{4,68},{5,69},{6,70},{7,71},{8,72},{9,... | collective-permute-start | bytes 2359304 | tf_op jit(solution)/shard_map/ppermute | solution.py:37
  24.0 2.7 %collective-permute-start.7 = (bf16[27,16,256]{2,1,0:T(8,128)(2,1)S(1)}, bf16[27,16,256]{2,1,0:T(8,128)(2,1)S(1)}, u32[]{:S(2)}, u32[]{:S(2)}) collective-permute-start(bf16[27,16,256]{2,1,0:T(8,128)(2,1)S(1)} %pad_maximum_fusion.2.refs_5_), channel_id=1, source_target_pairs={{0,56},{1,57},{2,58},{3,59},{4,60},{5,61},{6,62},{7,63},{8,0},{9,1... | collective-permute-start | bytes 663560 | tf_op jit(solution)/shard_map/ppermute | solution.py:37
  27.4 5.8 %all-to-all-start = ((f32[32,8,256]{2,1,0:T(8,128)}), f32[32,8,256]{2,1,0:T(8,128)S(1)}, u32[]{:S(2)}, u32[]{:S(2)}) async-start(f32[32,8,256]{2,1,0:T(8,128)} %broadcast_in_dim.5), calls=%async_computation | async-start | bytes 524288 | tf_op jit(solution)/shard_map/all_to_all | solution.py:344
  33.2 1.3 %collective-permute-start.11 = (bf16[27,16,256]{2,1,0:T(8,128)(2,1)S(1)}, bf16[27,16,256]{2,1,0:T(8,128)(2,1)}, u32[]{:S(2)}, u32[]{:S(2)}) collective-permute-start(bf16[27,16,256]{2,1,0:T(8,128)(2,1)S(1)} %collective-permute-done.10.refs_13_), channel_id=1, source_target_pairs={{0,8},{1,9},{2,10},{3,11},{4,12},{5,13},{6,14},{7,15},{8,16},{9,17... | collective-permute-start | bytes 663560 | tf_op jit(solution)/shard_map/ppermute | solution.py:37
  34.5 1.4 %collective-permute-start.8 = (bf16[27,16,256]{2,1,0:T(8,128)(2,1)S(1)}, bf16[27,16,256]{2,1,0:T(8,128)(2,1)}, u32[]{:S(2)}, u32[]{:S(2)}) collective-permute-start(bf16[27,16,256]{2,1,0:T(8,128)(2,1)S(1)} %collective-permute-done.7.refs_6_), channel_id=1, source_target_pairs={{0,56},{1,57},{2,58},{3,59},{4,60},{5,61},{6,62},{7,63},{8,0},{9,1... | collective-permute-start | bytes 663560 | tf_op jit(solution)/shard_map/ppermute | solution.py:37
  36.0 3.2 %collective-permute-done.13.refs_1_ = bf16[2,6,128,256]{3,2,1,0:T(8,128)(2,1)S(1)} collective-permute-done((bf16[2,6,128,256]{3,2,1,0:T(8,128)(2,1)S(1)}, bf16[2,6,128,256]{3,2,1,0:T(8,128)(2,1)S(1)}, u32[]{:S(2)}, u32[]{:S(2)}) %collective-permute-start.13) | collective-permute-done | bytes 786464 | tf_op jit(solution)/shard_map/ppermute | solution.py:37
  40.0 1.6 %collective-permute-start.15 = (bf16[1,6,128,256]{3,2,1,0:T(8,128)(2,1)}, bf16[1,6,128,256]{3,2,1,0:T(8,128)(2,1)}, u32[]{:S(2)}, u32[]{:S(2)}) collective-permute-start(bf16[1,6,128,256]{3,2,1,0:T(8,128)(2,1)} %slice.26), channel_id=1, source_target_pairs={{0,192},{1,193},{2,194},{3,195},{4,196},{5,197},{6,198},{7,199},{8... | collective-permute-start | bytes 1179656 | tf_op jit(solution)/shard_map/ppermute | solution.py:37
  43.1 2.7 %collective-permute-start.9 = (bf16[27,16,256]{2,1,0:T(8,128)(2,1)}, bf16[27,16,256]{2,1,0:T(8,128)(2,1)S(1)}, u32[]{:S(2)}, u32[]{:S(2)}) collective-permute-start(bf16[27,16,256]{2,1,0:T(8,128)(2,1)} %collective-permute-done.8.refs_7_), channel_id=1, source_target_pairs={{0,56},{1,57},{2,58},{3,59},{4,60},{5,61},{6,62},{7,63},{8,0},{9,1... | collective-permute-start | bytes 663560 | tf_op jit(solution)/shard_map/ppermute | solution.py:37
  46.0 3.0 %shard_map.58 = (bf16[2,6,128,256]{3,2,1,0:T(8,128)(2,1)S(1)}, bf16[2,6,128,256]{3,2,1,0:T(8,128)(2,1)S(1)}, bf16[2,6,128,256]{3,2,1,0:T(8,128)(2,1)S(1)}) custom-call(s32[5]{0:T(128)S(1)} %stack.31.info, f32[32,8,256]{2,1,0:T(8,128)S(1)} %all-to-all-done.stats, f32[1,256]{1,0:T(1,128)S(1)} %bitcast.15, f32[1,256]{1,0:T(1,128)S(1)} %bitcast.17, ...), custom_call_target="tpu_custom_call" | custom-call | flops 18874368 | bytes 4718592 | tf_op jit(solution)/shard_map/pallas_call | solution.py:183
  49.5 3.0 %collective-permute-start.17 = (bf16[27,16,128]{2,1,0:T(8,128)(2,1)S(1)}, bf16[27,16,128]{2,1,0:T(8,128)(2,1)S(1)}, u32[]{:S(2)}, u32[]{:S(2)}) collective-permute-start(bf16[27,16,128]{2,1,0:T(8,128)(2,1)S(1)} %slice.22), channel_id=1, source_target_pairs={{0,56},{1,57},{2,58},{3,59},{4,60},{5,61},{6,62},{7,63},{8,0},{9,1... | collective-permute-start | bytes 331784 | tf_op jit(solution)/shard_map/ppermute | solution.py:37
  52.6 2.0 %shard_map.59 = (bf16[1,6,128,256]{3,2,1,0:T(8,128)(2,1)S(1)}, bf16[1,6,128,256]{3,2,1,0:T(8,128)(2,1)S(1)}) custom-call(s32[5]{0:T(128)S(1)} %stack.31.info, f32[32,8,256]{2,1,0:T(8,128)S(1)} %all-to-all-done.stats, f32[1,256]{1,0:T(1,128)S(1)} %bitcast.16, f32[1,256]{1,0:T(1,128)S(1)} %bitcast.18, ...), custom_call_target="tpu_custom_call" | custom-call | flops 6291456 | bytes 1572864 | tf_op jit(solution)/shard_map/pallas_call | solution.py:183
  55.4 2.1 %collective-permute-done.18.refs_10_ = bf16[27,16,128]{2,1,0:T(8,128)(2,1)S(1)} collective-permute-done((bf16[27,16,128]{2,1,0:T(8,128)(2,1)S(1)}, bf16[27,16,128]{2,1,0:T(8,128)(2,1)S(1)}, u32[]{:S(2)}, u32[]{:S(2)}) %collective-permute-start.18) | collective-permute-done | bytes 110624 | tf_op jit(solution)/shard_map/ppermute | solution.py:37
  58.1 10.3 %shard_map.60 = (f32[3,2,2,128,128]{4,3,2,1,0:T(8,128)S(1)}, bf16[3,2,2,128,128]{4,3,2,1,0:T(8,128)(2,1)S(1)}) custom-call(s32[5]{0:T(128)S(1)} %stack.31.info, f32[1,512]{1,0:T(1,128)S(1)} %bitcast.19, bf16[2,6,128,256]{3,2,1,0:T(8,128)(2,1)S(1)} %get-tuple-element.46.refs_0_, bf16[2,6,128,256]{3,2,1,0:T(8,128)(2,1)S(1)} %get-tuple-element.47.refs_1_, ...), custom_call_target="tpu_custom_call" | custom-call | flops 5435817984 | bytes 5242880 | tf_op jit(solution)/shard_map/pallas_call | solution.py:261
  68.4 8.5 %collective-permute-start.19 = (bf16[3,2,2,128,128]{4,3,2,1,0:T(8,128)(2,1)S(1)}, bf16[3,2,2,128,128]{4,3,2,1,0:T(8,128)(2,1)S(1)}, u32[]{:S(2)}, u32[]{:S(2)}) collective-permute-start(bf16[3,2,2,128,128]{4,3,2,1,0:T(8,128)(2,1)S(1)} %get-tuple-element.54), channel_id=1, source_target_pairs={{0,1},{1,0},{2,3},{3,2},{4,5},{5,4},{6,7},{7,6},{8,9},{9,8},{10,11... | collective-permute-start | bytes 1179656 | tf_op jit(solution)/shard_map/ppermute | solution.py:37
  76.9 1.3 %collective-permute-done.19.taken = bf16[3,2,2,128,128]{4,3,2,1,0:T(8,128)(2,1)S(1)} collective-permute-done((bf16[3,2,2,128,128]{4,3,2,1,0:T(8,128)(2,1)S(1)}, bf16[3,2,2,128,128]{4,3,2,1,0:T(8,128)(2,1)S(1)}, u32[]{:S(2)}, u32[]{:S(2)}) %collective-permute-start.19) | collective-permute-done | bytes 393248 | tf_op jit(solution)/shard_map/ppermute | solution.py:37
  78.3 2.3 %collective-permute-start.22 = (bf16[2,2,128,128]{3,2,1,0:T(8,128)(2,1)S(1)}, bf16[2,2,128,128]{3,2,1,0:T(8,128)(2,1)S(1)}, u32[]{:S(2)}, u32[]{:S(2)}) collective-permute-start(bf16[2,2,128,128]{3,2,1,0:T(8,128)(2,1)S(1)} %get-tuple-element.62), channel_id=1, source_target_pairs={{0,192},{1,193},{2,194},{3,195},{4,196},{5,197},{6,198},{7,199},{8... | collective-permute-start | bytes 393224 | tf_op jit(solution)/shard_map/ppermute | solution.py:37
  81.3 4.1 %shard_map.62 = (f32[1,2,2,128,128]{4,3,2,1,0:T(8,128)S(1)}, bf16[2,128,128]{2,1,0:T(8,128)(2,1)S(1)}, bf16[2,128,128]{2,1,0:T(8,128)(2,1)S(1)}) custom-call(s32[5]{0:T(128)S(1)} %stack.31.info, f32[1,512]{1,0:T(1,128)S(1)} %bitcast.20, bf16[2,6,128,256]{3,2,1,0:T(8,128)(2,1)S(1)} %get-tuple-element.46.refs_0_, ...), custom_call_target="tpu_custom_call" | custom-call | flops 1811939328 | bytes 5242880 | tf_op jit(solution)/shard_map/pallas_call | solution.py:261
  87.7 2.1 %collective-permute-done.24.refs_2_ = bf16[2,2,128,128]{3,2,1,0:T(8,128)(2,1)S(1)} collective-permute-done((bf16[2,2,128,128]{3,2,1,0:T(8,128)(2,1)S(1)}, bf16[2,2,128,128]{3,2,1,0:T(8,128)(2,1)S(1)}, u32[]{:S(2)}, u32[]{:S(2)}) %collective-permute-start.24) | collective-permute-done | bytes 131104 | tf_op jit(solution)/shard_map/ppermute | solution.py:37
  89.7 1.4 %shard_map.63 = bf16[2,2,128,512]{3,2,1,0:T(8,128)(2,1)} custom-call(s32[5]{0:T(128)S(1)} %stack.31.info, f32[1,2,2,128,128]{4,3,2,1,0:T(8,128)S(1)} %get-tuple-element.59.keep, bf16[2,128,128]{2,1,0:T(8,128)(2,1)S(1)} %collective-permute-done.20.first, bf16[2,128,128]{2,1,0:T(8,128)(2,1)S(1)} %collective-permute-done.21.second, ...), custom_call_target="tpu_custom_call" | custom-call | tf_op jit(solution)/shard_map/pallas_call | solution.py:303
  (70 shorter events, 14.3 us)
Async XLA Ops:
  1.0 4.9 %collective-permute-start = (bf16[2,2,128,256]{3,2,1,0:T(8,128)(2,1)S(1)}, bf16[2,2,128,256]{3,2,1,0:T(8,128)(2,1)S(1)}, u32[]{:S(2)}, u32[]{:S(2)}) collective-permute-start(bf16[2,2,128,256]{3,2,1,0:T(8,128)(2,1)S(1)} %constant_dynamic-slice_fusion.2), channel_id=1, source_target_pairs={{0,1},{1,0},{2,3},{3,2},{4,5},{5,4},{6,7},{7,6},{8,9},{9,8},{10,11... | collective-permute-start | bytes 786440 | tf_op jit(solution)/shard_map/ppermute | solution.py:37
  7.5 7.5 %collective-permute-start.1 = (f32[2,256]{1,0:T(2,128)S(1)}, f32[2,256]{1,0:T(2,128)S(1)}, u32[]{:S(2)}, u32[]{:S(2)}) collective-permute-start(f32[2,256]{1,0:T(2,128)S(1)} %shard_map.56), channel_id=1, source_target_pairs={{0,64},{1,65},{2,66},{3,67},{4,68},{5,69},{6,70},{7,71},{8,72},{9,... | collective-permute-start | bytes 6152 | tf_op jit(solution)/shard_map/ppermute | solution.py:37
  7.6 11.9 %collective-permute-start.4 = (bf16[364,256]{1,0:T(8,128)(2,1)S(1)}, bf16[364,256]{1,0:T(8,128)(2,1)S(1)}, u32[]{:S(2)}, u32[]{:S(2)}) collective-permute-start(bf16[364,256]{1,0:T(8,128)(2,1)S(1)} %get-tuple-element.65), channel_id=1, source_target_pairs={{0,2},{1,3},{2,4},{3,5},{4,6},{5,7},{6,8},{7,9},{8,10},{9,11},{10,... | collective-permute-start | bytes 559112 | tf_op jit(solution)/shard_map/ppermute | solution.py:37
  8.4 11.1 %collective-permute-start.5 = (bf16[364,256]{1,0:T(8,128)(2,1)S(1)}, bf16[364,256]{1,0:T(8,128)(2,1)S(1)}, u32[]{:S(2)}, u32[]{:S(2)}) collective-permute-start(bf16[364,256]{1,0:T(8,128)(2,1)S(1)} %get-tuple-element.66), channel_id=1, source_target_pairs={{0,62},{1,63},{2,0},{3,1},{4,2},{5,3},{6,4},{7,5},{8,6},{9,7},{10,... | collective-permute-start | bytes 559112 | tf_op jit(solution)/shard_map/ppermute | solution.py:37
  15.1 4.4 %collective-permute-start.2 = (f32[4,256]{1,0:T(4,128)S(1)}, f32[4,256]{1,0:T(4,128)S(1)}, u32[]{:S(2)}, u32[]{:S(2)}) collective-permute-start(f32[4,256]{1,0:T(4,128)S(1)} %pad_maximum_fusion.4), channel_id=1, source_target_pairs={{0,128},{1,129},{2,130},{3,131},{4,132},{5,133},{6,134},{7,135},{8... | collective-permute-start | bytes 12296 | tf_op jit(solution)/shard_map/ppermute | solution.py:37
  17.8 4.5 %collective-permute-start.6 = (bf16[27,4,256]{2,1,0:T(4,128)(2,1)S(1)}, bf16[27,4,256]{2,1,0:T(4,128)(2,1)S(1)}, u32[]{:S(2)}, u32[]{:S(2)}) collective-permute-start(bf16[27,4,256]{2,1,0:T(4,128)(2,1)S(1)} %maximum_select_fusion), channel_id=1, source_target_pairs={{0,60},{1,61},{2,62},{3,63},{4,0},{5,1},{6,2},{7,3},{8,4},{9,5},{1... | collective-permute-start | bytes 165896 | tf_op jit(solution)/shard_map/ppermute | solution.py:37
  22.4 16.7 %collective-permute-start.13 = (bf16[2,6,128,256]{3,2,1,0:T(8,128)(2,1)S(1)}, bf16[2,6,128,256]{3,2,1,0:T(8,128)(2,1)S(1)}, u32[]{:S(2)}, u32[]{:S(2)}) collective-permute-start(bf16[2,6,128,256]{3,2,1,0:T(8,128)(2,1)S(1)} %shard_map.57.refs_0_), channel_id=1, source_target_pairs={{0,192},{1,193},{2,194},{3,195},{4,196},{5,197},{6,198},{7,199},{8... | collective-permute-start | bytes 2359304 | tf_op jit(solution)/shard_map/ppermute | solution.py:37
  22.7 18.9 %collective-permute-start.14 = (bf16[2,6,128,256]{3,2,1,0:T(8,128)(2,1)S(1)}, bf16[2,6,128,256]{3,2,1,0:T(8,128)(2,1)S(1)}, u32[]{:S(2)}, u32[]{:S(2)}) collective-permute-start(bf16[2,6,128,256]{3,2,1,0:T(8,128)(2,1)S(1)} %shard_map.57.refs_0_), channel_id=1, source_target_pairs={{0,64},{1,65},{2,66},{3,67},{4,68},{5,69},{6,70},{7,71},{8,72},{9,... | collective-permute-start | bytes 2359304 | tf_op jit(solution)/shard_map/ppermute | solution.py:37
  24.0 9.2 %collective-permute-start.10 = (bf16[27,16,256]{2,1,0:T(8,128)(2,1)S(1)}, bf16[27,16,256]{2,1,0:T(8,128)(2,1)S(1)}, u32[]{:S(2)}, u32[]{:S(2)}) collective-permute-start(bf16[27,16,256]{2,1,0:T(8,128)(2,1)S(1)} %pad_maximum_fusion.2.refs_5_), channel_id=1, source_target_pairs={{0,8},{1,9},{2,10},{3,11},{4,12},{5,13},{6,14},{7,15},{8,16},{9,17... | collective-permute-start | bytes 663560 | tf_op jit(solution)/shard_map/ppermute | solution.py:37
  24.0 10.6 %collective-permute-start.7 = (bf16[27,16,256]{2,1,0:T(8,128)(2,1)S(1)}, bf16[27,16,256]{2,1,0:T(8,128)(2,1)S(1)}, u32[]{:S(2)}, u32[]{:S(2)}) collective-permute-start(bf16[27,16,256]{2,1,0:T(8,128)(2,1)S(1)} %pad_maximum_fusion.2.refs_5_), channel_id=1, source_target_pairs={{0,56},{1,57},{2,58},{3,59},{4,60},{5,61},{6,62},{7,63},{8,0},{9,1... | collective-permute-start | bytes 663560 | tf_op jit(solution)/shard_map/ppermute | solution.py:37
  27.4 18.6 %all-to-all-start = ((f32[32,8,256]{2,1,0:T(8,128)}), f32[32,8,256]{2,1,0:T(8,128)S(1)}, u32[]{:S(2)}, u32[]{:S(2)}) async-start(f32[32,8,256]{2,1,0:T(8,128)} %broadcast_in_dim.5), calls=%async_computation | async-start | bytes 524288 | tf_op jit(solution)/shard_map/all_to_all | solution.py:344
  33.2 9.9 %collective-permute-start.11 = (bf16[27,16,256]{2,1,0:T(8,128)(2,1)S(1)}, bf16[27,16,256]{2,1,0:T(8,128)(2,1)}, u32[]{:S(2)}, u32[]{:S(2)}) collective-permute-start(bf16[27,16,256]{2,1,0:T(8,128)(2,1)S(1)} %collective-permute-done.10.refs_13_), channel_id=1, source_target_pairs={{0,8},{1,9},{2,10},{3,11},{4,12},{5,13},{6,14},{7,15},{8,16},{9,17... | collective-permute-start | bytes 663560 | tf_op jit(solution)/shard_map/ppermute | solution.py:37
  34.5 8.6 %collective-permute-start.8 = (bf16[27,16,256]{2,1,0:T(8,128)(2,1)S(1)}, bf16[27,16,256]{2,1,0:T(8,128)(2,1)}, u32[]{:S(2)}, u32[]{:S(2)}) collective-permute-start(bf16[27,16,256]{2,1,0:T(8,128)(2,1)S(1)} %collective-permute-done.7.refs_6_), channel_id=1, source_target_pairs={{0,56},{1,57},{2,58},{3,59},{4,60},{5,61},{6,62},{7,63},{8,0},{9,1... | collective-permute-start | bytes 663560 | tf_op jit(solution)/shard_map/ppermute | solution.py:37
  40.0 12.7 %collective-permute-start.15 = (bf16[1,6,128,256]{3,2,1,0:T(8,128)(2,1)}, bf16[1,6,128,256]{3,2,1,0:T(8,128)(2,1)}, u32[]{:S(2)}, u32[]{:S(2)}) collective-permute-start(bf16[1,6,128,256]{3,2,1,0:T(8,128)(2,1)} %slice.26), channel_id=1, source_target_pairs={{0,192},{1,193},{2,194},{3,195},{4,196},{5,197},{6,198},{7,199},{8... | collective-permute-start | bytes 1179656 | tf_op jit(solution)/shard_map/ppermute | solution.py:37
  42.4 10.3 %collective-permute-start.16 = (bf16[1,6,128,256]{3,2,1,0:T(8,128)(2,1)}, bf16[1,6,128,256]{3,2,1,0:T(8,128)(2,1)}, u32[]{:S(2)}, u32[]{:S(2)}) collective-permute-start(bf16[1,6,128,256]{3,2,1,0:T(8,128)(2,1)} %slice.27), channel_id=1, source_target_pairs={{0,64},{1,65},{2,66},{3,67},{4,68},{5,69},{6,70},{7,71},{8,72},{9,... | collective-permute-start | bytes 1179656 | tf_op jit(solution)/shard_map/ppermute | solution.py:37
  43.1 6.4 %collective-permute-start.12 = (bf16[27,16,256]{2,1,0:T(8,128)(2,1)}, bf16[27,16,256]{2,1,0:T(8,128)(2,1)S(1)}, u32[]{:S(2)}, u32[]{:S(2)}) collective-permute-start(bf16[27,16,256]{2,1,0:T(8,128)(2,1)} %collective-permute-done.11.refs_12_), channel_id=1, source_target_pairs={{0,8},{1,9},{2,10},{3,11},{4,12},{5,13},{6,14},{7,15},{8,16},{9,17... | collective-permute-start | bytes 663560 | tf_op jit(solution)/shard_map/ppermute | solution.py:37
  43.1 6.4 %collective-permute-start.9 = (bf16[27,16,256]{2,1,0:T(8,128)(2,1)}, bf16[27,16,256]{2,1,0:T(8,128)(2,1)S(1)}, u32[]{:S(2)}, u32[]{:S(2)}) collective-permute-start(bf16[27,16,256]{2,1,0:T(8,128)(2,1)} %collective-permute-done.8.refs_7_), channel_id=1, source_target_pairs={{0,56},{1,57},{2,58},{3,59},{4,60},{5,61},{6,62},{7,63},{8,0},{9,1... | collective-permute-start | bytes 663560 | tf_op jit(solution)/shard_map/ppermute | solution.py:37
  49.5 5.8 %collective-permute-start.17 = (bf16[27,16,128]{2,1,0:T(8,128)(2,1)S(1)}, bf16[27,16,128]{2,1,0:T(8,128)(2,1)S(1)}, u32[]{:S(2)}, u32[]{:S(2)}) collective-permute-start(bf16[27,16,128]{2,1,0:T(8,128)(2,1)S(1)} %slice.22), channel_id=1, source_target_pairs={{0,56},{1,57},{2,58},{3,59},{4,60},{5,61},{6,62},{7,63},{8,0},{9,1... | collective-permute-start | bytes 331784 | tf_op jit(solution)/shard_map/ppermute | solution.py:37
  52.5 4.9 %collective-permute-start.18 = (bf16[27,16,128]{2,1,0:T(8,128)(2,1)S(1)}, bf16[27,16,128]{2,1,0:T(8,128)(2,1)S(1)}, u32[]{:S(2)}, u32[]{:S(2)}) collective-permute-start(bf16[27,16,128]{2,1,0:T(8,128)(2,1)S(1)} %slice.23), channel_id=1, source_target_pairs={{0,8},{1,9},{2,10},{3,11},{4,12},{5,13},{6,14},{7,15},{8,16},{9,17... | collective-permute-start | bytes 331784 | tf_op jit(solution)/shard_map/ppermute | solution.py:37
  68.4 9.8 %collective-permute-start.19 = (bf16[3,2,2,128,128]{4,3,2,1,0:T(8,128)(2,1)S(1)}, bf16[3,2,2,128,128]{4,3,2,1,0:T(8,128)(2,1)S(1)}, u32[]{:S(2)}, u32[]{:S(2)}) collective-permute-start(bf16[3,2,2,128,128]{4,3,2,1,0:T(8,128)(2,1)S(1)} %get-tuple-element.54), channel_id=1, source_target_pairs={{0,1},{1,0},{2,3},{3,2},{4,5},{5,4},{6,7},{7,6},{8,9},{9,8},{10,11... | collective-permute-start | bytes 1179656 | tf_op jit(solution)/shard_map/ppermute | solution.py:37
  78.3 9.3 %collective-permute-start.22 = (bf16[2,2,128,128]{3,2,1,0:T(8,128)(2,1)S(1)}, bf16[2,2,128,128]{3,2,1,0:T(8,128)(2,1)S(1)}, u32[]{:S(2)}, u32[]{:S(2)}) collective-permute-start(bf16[2,2,128,128]{3,2,1,0:T(8,128)(2,1)S(1)} %get-tuple-element.62), channel_id=1, source_target_pairs={{0,192},{1,193},{2,194},{3,195},{4,196},{5,197},{6,198},{7,199},{8... | collective-permute-start | bytes 393224 | tf_op jit(solution)/shard_map/ppermute | solution.py:37
  80.6 7.0 %collective-permute-start.23 = (bf16[2,2,128,128]{3,2,1,0:T(8,128)(2,1)S(1)}, bf16[2,2,128,128]{3,2,1,0:T(8,128)(2,1)S(1)}, u32[]{:S(2)}, u32[]{:S(2)}) collective-permute-start(bf16[2,2,128,128]{3,2,1,0:T(8,128)(2,1)S(1)} %get-tuple-element.63), channel_id=1, source_target_pairs={{0,128},{1,129},{2,130},{3,131},{4,132},{5,133},{6,134},{7,135},{8... | collective-permute-start | bytes 393224 | tf_op jit(solution)/shard_map/ppermute | solution.py:37
  80.6 9.1 %collective-permute-start.24 = (bf16[2,2,128,128]{3,2,1,0:T(8,128)(2,1)S(1)}, bf16[2,2,128,128]{3,2,1,0:T(8,128)(2,1)S(1)}, u32[]{:S(2)}, u32[]{:S(2)}) collective-permute-start(bf16[2,2,128,128]{3,2,1,0:T(8,128)(2,1)S(1)} %get-tuple-element.64), channel_id=1, source_target_pairs={{0,64},{1,65},{2,66},{3,67},{4,68},{5,69},{6,70},{7,71},{8,72},{9,... | collective-permute-start | bytes 393224 | tf_op jit(solution)/shard_map/ppermute | solution.py:37
  85.4 1.9 %collective-permute-start.20 = (bf16[2,128,128]{2,1,0:T(8,128)(2,1)S(1)}, bf16[2,128,128]{2,1,0:T(8,128)(2,1)S(1)}, u32[]{:S(2)}, u32[]{:S(2)}) collective-permute-start(bf16[2,128,128]{2,1,0:T(8,128)(2,1)S(1)} %get-tuple-element.60), channel_id=1, source_target_pairs={{0,1},{1,0},{2,3},{3,2},{4,5},{5,4},{6,7},{7,6},{8,9},{9,8},{10,11... | collective-permute-start | bytes 196616 | tf_op jit(solution)/shard_map/ppermute | solution.py:37
  (8 other events, 29.1 us)
